TPU v7x, 32 devices: a whole 2x2x4 slice. The times are simulated.
32 devices in a mesh: groups: 2 (over x), shard: 16 (over z, y, core).
Axes of the slice: x: 2, y: 2, z: 4, core: 2. Of those that a mesh axis runs over, the one named last changes fastest.
Arguments:
- embeddings: bfloat16 [16384, 1024], P(('groups', 'shard')), parts along dimension 0, may hold values from -6 to 6
- scales: bfloat16 [16384], P(('groups', 'shard')), parts along dimension 0, may hold values from 0.039794922 to 0.119628906
- cluster: int32 [16384, 1], P(('groups', 'shard')), parts along dimension 0, may hold values from 0 to 15; in each aligned block of 512 rows (0 to 511, 512 to 1023, ...) at most 64 rows name the same one
- pair_listed: int32 [32, 5], P(('groups', 'shard')), parts along dimension 0, may hold values from 0 to 1, as said below
Outputs:
- best: float32 [16384], P(('groups', 'shard')), parts along dimension 0
There are 2 independent parts, one for each index of `groups`. A program takes and returns all parts, laid end to end along the dimension named above; each array names one. Nothing has to cross between parts.
Inputs may be any that keep to these rules, and one draw needn't show every extreme that they name: In each shard's 512 rows at most 64 rows name one sub-cluster, and every sub-cluster is named by some row of the group. `pair_listed`: column 0 is 1 for every a < 15; entries with a + k + 1 >= 16 are 0.
All inputs are finite; a program needn't handle non-finite values.
Results may differ from a plain program's by a relative error of at most 0.0003.
Values may be sent and summed in bfloat16 or wider, within the bound.
No kernel may reach another device: no remote copies, remote signals or barrier semaphores. Data moves between devices by JAX's collectives and lax.ppermute only.
A program may use at most 64 MiB of HBM per device.

v0:
```python
import jax
import jax.numpy as jnp
from jax import lax
from jax.sharding import PartitionSpec as P

PARTNERS = 5


lowest = -jnp.inf


def passed_along(value, axis, steps):
    count = lax.axis_size(axis)
    initial, last = (max(0, -steps), min(count, count - steps))
    return lax.ppermute(value, axis, [(source, source + steps) for source in range(initial, last)])


def scaled_tile(left, left_scale, right, right_scale):
    raw = lax.dot_general(left, right, (((1,), (1,)), ((), ())), preferred_element_type=jnp.float32)
    return raw * left_scale.astype(jnp.float32)[:, None] * right_scale.astype(jnp.float32)[None, :]


def partner_tile(left, left_scale, right, right_scale):
    scores = scaled_tile(left, left_scale, right, right_scale)
    live = (left_scale != 0)[:, None] & (right_scale != 0)[None, :]
    masked = jnp.where(live, scores, lowest)
    return (jnp.max(masked, axis=1), jnp.max(masked, axis=0))


def per_device(embeddings, scales, cluster, pair_listed):
    rows, width = embeddings.shape
    owners = lax.axis_size("shard")
    capacity = 2 * rows // owners
    slots = owners * capacity
    here = lax.axis_index("shard")
    target = cluster[:, 0]
    onehot = (target[:, None] == jnp.arange(owners, dtype=jnp.int32)[None, :]).astype(jnp.int32)
    before = jnp.cumsum(onehot, axis=0) - onehot
    position = target * capacity + jnp.sum(before * onehot, axis=1)
    placing = (jnp.arange(slots, dtype=jnp.int32)[:, None] == position[None, :]).astype(
        jnp.bfloat16
    )
    packed = jnp.dot(placing, embeddings, preferred_element_type=jnp.float32).astype(jnp.bfloat16)
    packed_scale = jnp.dot(placing, scales, preferred_element_type=jnp.float32).astype(jnp.bfloat16)
    block, block_scale = (
        lax.all_to_all(
            packed.reshape(owners, capacity, width),
            "shard",
            split_axis=0,
            concat_axis=0,
            tiled=True,
        ),
        lax.all_to_all(
            packed_scale.reshape(owners, capacity), "shard", split_axis=0, concat_axis=0, tiled=True
        ),
    )
    block = block.reshape(slots, width)
    block_scale = block_scale.reshape(slots)
    valid = block_scale != 0
    scores = scaled_tile(block, block_scale, block, block_scale)
    counter = jnp.arange(slots, dtype=jnp.int32)
    keep = valid[None, :] & (counter[:, None] != counter[None, :])
    row_best = jnp.max(jnp.where(keep, scores, lowest), axis=1)
    column_best = []
    carried = (block, block_scale)
    for step in range(PARTNERS):
        carried = passed_along((carried[0], carried[1]), "shard", -1)
        listed = pair_listed[0, step] == 1
        rows_part, cols_part = partner_tile(block, block_scale, carried[0], carried[1])
        rows_part = jnp.where(listed, rows_part, lowest)
        cols_part = jnp.where(listed, cols_part, lowest)
        row_best = jnp.maximum(row_best, rows_part)
        column_best.append(cols_part)
    returned = column_best[PARTNERS - 1]
    for step in range(PARTNERS - 1, -1, -1):
        returned = passed_along(returned, "shard", 1)
        returned = jnp.where(here == 0, lowest, returned)
        if step > 0:
            returned = jnp.maximum(returned, column_best[step - 1])
    slot_best = jnp.where(valid, jnp.maximum(row_best, returned), 0.0)
    homeward = lax.all_to_all(
        slot_best.reshape(owners, capacity), "shard", split_axis=0, concat_axis=0, tiled=True
    )
    return jnp.take(homeward.reshape(slots), position)


def solution(mesh):
    placed = (
        P(("groups", "shard"), None),
        P(("groups", "shard")),
        P(("groups", "shard"), None),
        P(("groups", "shard"), None),
    )
    return jax.shard_map(
        per_device, mesh=mesh, in_specs=placed, out_specs=P(("groups", "shard")), check_vma=False
    )
```

profile of v0, /device:TPU:0, one launch (start us, length us, event | category | flops | bytes accessed | tf_op | source)
XLA Modules:
  0.0 281.7 jit_solution(17017823350575949528)
XLA Ops:
  4.9 54.5 %all_to_all.24 = bf16[16,64,1024]{2,1,0:T(8,128)(2,1)S(1)} all-to-all(bf16[16,64,1024]{2,1,0:T(8,128)(2,1)S(1)} %bitcast.52), channel_id=1, replica_groups=mesh['groups'=2,'shard'=16] {'shard'}, dimensions={0} | all-to-all | bytes 4194304 | tf_op jit(solution)/shard_map/all_to_all | solution.py:46
  60.7 5.0 %collective-permute-done.1 = bf16[1024,1024]{1,0:T(8,128)(2,1)S(1)} collective-permute-done((bf16[1024,1024]{1,0:T(8,128)(2,1)S(1)}, bf16[1024,1024]{1,0:T(8,128)(2,1)S(1)}, u32[]{:S(2)}, u32[]{:S(2)}) %collective-permute-start.1) | collective-permute-done | bytes 2097184 | tf_op jit(solution)/shard_map/ppermute | solution.py:15
  67.0 26.1 %collective-permute-done.3 = bf16[1024,1024]{1,0:T(8,128)(2,1)S(1)} collective-permute-done((bf16[1024,1024]{1,0:T(8,128)(2,1)S(1)}, bf16[1024,1024]{1,0:T(8,128)(2,1)S(1)}, u32[]{:S(2)}, u32[]{:S(2)}) %collective-permute-start.3) | collective-permute-done | bytes 2097184 | tf_op jit(solution)/shard_map/ppermute | solution.py:15
  94.4 26.2 %collective-permute-done.5 = bf16[1024,1024]{1,0:T(8,128)(2,1)} collective-permute-done((bf16[1024,1024]{1,0:T(8,128)(2,1)S(1)}, bf16[1024,1024]{1,0:T(8,128)(2,1)}, u32[]{:S(2)}, u32[]{:S(2)}) %collective-permute-start.5) | collective-permute-done | bytes 2097184 | tf_op jit(solution)/shard_map/ppermute | solution.py:15
  123.0 29.7 %all-to-all-start = ((bf16[16,1,64]{2,1,0:T(2,128)(2,1)}), bf16[16,1,64]{2,1,0:T(2,128)(2,1)S(1)}, u32[]{:S(2)}, u32[]{:S(2)}) async-start(bf16[16,1,64]{2,1,0:T(2,128)(2,1)} %all_to_all.20), calls=%async_computation | async-start | bytes 16384 | tf_op jit(solution)/shard_map/all_to_all | solution.py:53
  154.1 20.4 %all-to-all-done = bf16[16,1,64]{2,1,0:T(2,128)(2,1)S(1)} async-done(((bf16[16,1,64]{2,1,0:T(2,128)(2,1)}), bf16[16,1,64]{2,1,0:T(2,128)(2,1)S(1)}, u32[]{:S(2)}, u32[]{:S(2)}) %all-to-all-start) | async-done | bytes 2080 | tf_op jit(solution)/shard_map/all_to_all | solution.py:53
  179.0 2.9 %collective-permute-done.2 = bf16[1024]{0:T(1024)(128)(2,1)S(1)} collective-permute-done((bf16[1024]{0:T(1024)(128)(2,1)S(1)}, bf16[1024]{0:T(1024)(128)(2,1)S(1)}, u32[]{:S(2)}, u32[]{:S(2)}) %collective-permute-start.2) | collective-permute-done | bytes 2080 | tf_op jit(solution)/shard_map/ppermute | solution.py:15
  183.2 3.6 %collective-permute-done.4 = bf16[1024]{0:T(1024)(128)(2,1)S(1)} collective-permute-done((bf16[1024]{0:T(1024)(128)(2,1)S(1)}, bf16[1024]{0:T(1024)(128)(2,1)S(1)}, u32[]{:S(2)}, u32[]{:S(2)}) %collective-permute-start.4) | collective-permute-done | bytes 2080 | tf_op jit(solution)/shard_map/ppermute | solution.py:15
  188.1 3.6 %collective-permute-done.6 = bf16[1024]{0:T(1024)(128)(2,1)S(1)} collective-permute-done((bf16[1024]{0:T(1024)(128)(2,1)S(1)}, bf16[1024]{0:T(1024)(128)(2,1)S(1)}, u32[]{:S(2)}, u32[]{:S(2)}) %collective-permute-start.6) | collective-permute-done | bytes 2080 | tf_op jit(solution)/shard_map/ppermute | solution.py:15
  193.0 3.6 %collective-permute-done.8 = bf16[1024]{0:T(1024)(128)(2,1)S(1)} collective-permute-done((bf16[1024]{0:T(1024)(128)(2,1)S(1)}, bf16[1024]{0:T(1024)(128)(2,1)S(1)}, u32[]{:S(2)}, u32[]{:S(2)}) %collective-permute-start.8) | collective-permute-done | bytes 2080 | tf_op jit(solution)/shard_map/ppermute | solution.py:15
  198.2 4.0 %fusion.21 = f32[1024,1024]{0,1:T(8,128)S(1)} fusion(bf16[1024,1024]{1,0:T(8,128)(2,1)S(1)} %bitcast.46, bf16[1024,1024]{1,0:T(8,128)(2,1)} %copy-done.4), kind=kOutput, calls=%fused_computation.52 | convolution fusion | flops 2147483648 | bytes 8388608 | tf_op jit(solution)/shard_map/dot_general | solution.py:19
  202.2 2.4 fusion.22
  204.6 4.0 %fusion.23 = f32[1024,1024]{0,1:T(8,128)S(1)} fusion(bf16[1024,1024]{1,0:T(8,128)(2,1)S(1)} %bitcast.48, bf16[1024,1024]{1,0:T(8,128)(2,1)} %collective-permute-done.5), kind=kOutput, calls=%fused_computation.54 | convolution fusion | flops 2147483648 | bytes 8388608 | tf_op jit(solution)/shard_map/dot_general | solution.py:19
  208.6 4.0 %fusion.24 = f32[1024,1024]{0,1:T(8,128)S(1)} fusion(bf16[1024,1024]{1,0:T(8,128)(2,1)S(1)} %bitcast.49, bf16[1024,1024]{1,0:T(8,128)(2,1)} %collective-permute-done.7), kind=kOutput, calls=%fused_computation.55 | convolution fusion | flops 2147483648 | bytes 8388608 | tf_op jit(solution)/shard_map/dot_general | solution.py:19
  212.6 8.0 %fusion.2 = (f32[1024]{0:T(1024)S(1)}, f32[1024]{0:T(1024)S(1)}, f32[1024]{0:T(1024)S(1)}, f32[1024]{0:T(1024)S(1)}, f32[1024]{0:T(1024)S(1)}, /*index=5*/f32[10...) fusion(f32[1024,1024]{0,1:T(8,128)S(1)} %fusion.21, ...), kind=kOutput, calls=%fused_computation.10 | convolution fusion | flops 2178930688 | bytes 21043200 | tf_op jit(solution)/shard_map/dot_general | solution.py:19
  220.6 17.0 %collective-permute-start.10 = (f32[1024]{0:T(1024)S(1)}, f32[1024]{0:T(1024)S(1)}, u32[]{:S(2)}, u32[]{:S(2)}) collective-permute-start(f32[1024]{0:T(1024)S(1)} %broadcast_select_fusion), channel_id=1, source_target_pairs={{0,1},{1,2},{2,3},{3,4},{4,5},{5,6},{6,7},{7,8},{8,9},{9,10},{10,1... | collective-permute-start | bytes 12296 | tf_op jit(solution)/shard_map/ppermute | solution.py:15
  238.5 2.2 collective-permute-start.11
  241.5 7.4 %collective-permute-start.12 = (f32[1024]{0:T(1024)S(1)}, f32[1024]{0:T(1024)S(1)}, u32[]{:S(2)}, u32[]{:S(2)}) collective-permute-start(f32[1024]{0:T(1024)S(1)} %select_maximum_fusion.2), channel_id=1, source_target_pairs={{0,1},{1,2},{2,3},{3,4},{4,5},{5,6},{6,7},{7,8},{8,9},{9,10},{10,1... | collective-permute-start | bytes 12296 | tf_op jit(solution)/shard_map/ppermute | solution.py:15
  249.7 4.1 %collective-permute-start.13 = (f32[1024]{0:T(1024)S(1)}, f32[1024]{0:T(1024)S(1)}, u32[]{:S(2)}, u32[]{:S(2)}) collective-permute-start(f32[1024]{0:T(1024)S(1)} %select_maximum_fusion.1), channel_id=1, source_target_pairs={{0,1},{1,2},{2,3},{3,4},{4,5},{5,6},{6,7},{7,8},{8,9},{9,10},{10,1... | collective-permute-start | bytes 12296 | tf_op jit(solution)/shard_map/ppermute | solution.py:15
  254.6 4.1 %collective-permute-start.14 = (f32[1024]{0:T(1024)S(1)}, f32[1024]{0:T(1024)S(1)}, u32[]{:S(2)}, u32[]{:S(2)}) collective-permute-start(f32[1024]{0:T(1024)S(1)} %select_maximum_fusion), channel_id=1, source_target_pairs={{0,1},{1,2},{2,3},{3,4},{4,5},{5,6},{6,7},{7,8},{8,9},{9,10},{10,1... | collective-permute-start | bytes 12296 | tf_op jit(solution)/shard_map/ppermute | solution.py:15
  258.7 2.5 select_reduce_fusion
  261.9 9.3 %all-to-all-start.2 = ((f32[16,1,64]{2,1,0:T(1,128)}), f32[16,1,64]{2,1,0:T(1,128)S(1)}, u32[]{:S(2)}, u32[]{:S(2)}) async-start(f32[16,1,64]{2,1,0:T(1,128)} %all_to_all.18), calls=%async_computation.2 | async-start | bytes 16384 | tf_op jit(solution)/shard_map/all_to_all | solution.py:81
  271.2 6.4 %all-to-all-done.2 = f32[16,1,64]{2,1,0:T(1,128)S(1)} async-done(((f32[16,1,64]{2,1,0:T(1,128)}), f32[16,1,64]{2,1,0:T(1,128)S(1)}, u32[]{:S(2)}, u32[]{:S(2)}) %all-to-all-start.2) | async-done | bytes 4128 | tf_op jit(solution)/shard_map/all_to_all | solution.py:81
  278.9 2.3 gather_fusion
  (72 shorter events, 25.1 us)
Async XLA Ops:
  0.0 3.6 %copy-start = (bf16[512,1024]{1,0:T(8,128)(2,1)S(1)}, bf16[512,1024]{1,0:T(8,128)(2,1)}, u32[]{:S(2)}) copy-start(bf16[512,1024]{1,0:T(8,128)(2,1)} %param.4) | copy-start | bytes 3145732
  4.9 117.0 %copy-start.3 = (bf16[512]{0:T(512)(128)(2,1)S(1)}, bf16[512]{0:T(512)(128)(2,1)}, u32[]{:S(2)}) copy-start(bf16[512]{0:T(512)(128)(2,1)} %param.5) | copy-start | bytes 3076
  4.9 147.8 %copy-start.2 = (s32[1,5]{1,0:T(1,128)S(1)}, s32[1,5]{1,0:T(1,128)}, u32[]{:S(2)}) copy-start(s32[1,5]{1,0:T(1,128)} %param.7) | copy-start | bytes 64
  59.4 6.3 %collective-permute-start.1 = (bf16[1024,1024]{1,0:T(8,128)(2,1)S(1)}, bf16[1024,1024]{1,0:T(8,128)(2,1)S(1)}, u32[]{:S(2)}, u32[]{:S(2)}) collective-permute-start(bf16[1024,1024]{1,0:T(8,128)(2,1)S(1)} %bitcast.45), channel_id=1, source_target_pairs={{1,0},{2,1},{3,2},{4,3},{5,4},{6,5},{7,6},{8,7},{9,8},{10,9},{11,1... | collective-permute-start | bytes 6291464 | tf_op jit(solution)/shard_map/ppermute | solution.py:15
  65.7 54.8 %copy-start.4 = (bf16[1024,1024]{1,0:T(8,128)(2,1)}, bf16[1024,1024]{1,0:T(8,128)(2,1)S(1)}, u32[]{:S(2)}) copy-start(bf16[1024,1024]{1,0:T(8,128)(2,1)S(1)} %collective-permute-done.1) | copy-start | bytes 6291460
  65.7 27.3 %collective-permute-start.3 = (bf16[1024,1024]{1,0:T(8,128)(2,1)S(1)}, bf16[1024,1024]{1,0:T(8,128)(2,1)S(1)}, u32[]{:S(2)}, u32[]{:S(2)}) collective-permute-start(bf16[1024,1024]{1,0:T(8,128)(2,1)S(1)} %collective-permute-done.1), channel_id=1, source_target_pairs={{1,0},{2,1},{3,2},{4,3},{5,4},{6,5},{7,6},{8,7},{9,8},{10,9},{11,1... | collective-permute-start | bytes 6291464 | tf_op jit(solution)/shard_map/ppermute | solution.py:15
  93.1 27.5 %copy-start.5 = (bf16[1024,1024]{1,0:T(8,128)(2,1)}, bf16[1024,1024]{1,0:T(8,128)(2,1)S(1)}, u32[]{:S(2)}) copy-start(bf16[1024,1024]{1,0:T(8,128)(2,1)S(1)} %collective-permute-done.3) | copy-start | bytes 6291460
  93.1 27.5 %collective-permute-start.5 = (bf16[1024,1024]{1,0:T(8,128)(2,1)S(1)}, bf16[1024,1024]{1,0:T(8,128)(2,1)}, u32[]{:S(2)}, u32[]{:S(2)}) collective-permute-start(bf16[1024,1024]{1,0:T(8,128)(2,1)S(1)} %collective-permute-done.3), channel_id=1, source_target_pairs={{1,0},{2,1},{3,2},{4,3},{5,4},{6,5},{7,6},{8,7},{9,8},{10,9},{11,1... | collective-permute-start | bytes 6291464 | tf_op jit(solution)/shard_map/ppermute | solution.py:15
  120.6 76.1 %collective-permute-start.7 = (bf16[1024,1024]{1,0:T(8,128)(2,1)}, bf16[1024,1024]{1,0:T(8,128)(2,1)}, u32[]{:S(2)}, u32[]{:S(2)}) collective-permute-start(bf16[1024,1024]{1,0:T(8,128)(2,1)} %collective-permute-done.5), channel_id=1, source_target_pairs={{1,0},{2,1},{3,2},{4,3},{5,4},{6,5},{7,6},{8,7},{9,8},{10,9},{11,1... | collective-permute-start | bytes 6291464 | tf_op jit(solution)/shard_map/ppermute | solution.py:15
  123.0 51.5 %all-to-all-start = ((bf16[16,1,64]{2,1,0:T(2,128)(2,1)}), bf16[16,1,64]{2,1,0:T(2,128)(2,1)S(1)}, u32[]{:S(2)}, u32[]{:S(2)}) async-start(bf16[16,1,64]{2,1,0:T(2,128)(2,1)} %all_to_all.20), calls=%async_computation | async-start | bytes 16384 | tf_op jit(solution)/shard_map/all_to_all | solution.py:53
  174.6 3.0 %collective-permute-start = (bf16[1024]{0:T(1024)(128)(2,1)S(1)}, bf16[1024]{0:T(1024)(128)(2,1)S(1)}, u32[]{:S(2)}, u32[]{:S(2)}) collective-permute-start(bf16[1024]{0:T(1024)(128)(2,1)S(1)} %reshape.97), channel_id=1, source_target_pairs={{1,0},{2,1},{3,2},{4,3},{5,4},{6,5},{7,6},{8,7},{9,8},{10,9},{11,1... | collective-permute-start | bytes 6152 | tf_op jit(solution)/shard_map/ppermute | solution.py:15
  177.7 4.2 %collective-permute-start.2 = (bf16[1024]{0:T(1024)(128)(2,1)S(1)}, bf16[1024]{0:T(1024)(128)(2,1)S(1)}, u32[]{:S(2)}, u32[]{:S(2)}) collective-permute-start(bf16[1024]{0:T(1024)(128)(2,1)S(1)} %collective-permute-done), channel_id=1, source_target_pairs={{1,0},{2,1},{3,2},{4,3},{5,4},{6,5},{7,6},{8,7},{9,8},{10,9},{11,1... | collective-permute-start | bytes 6152 | tf_op jit(solution)/shard_map/ppermute | solution.py:15
  181.9 4.9 %collective-permute-start.4 = (bf16[1024]{0:T(1024)(128)(2,1)S(1)}, bf16[1024]{0:T(1024)(128)(2,1)S(1)}, u32[]{:S(2)}, u32[]{:S(2)}) collective-permute-start(bf16[1024]{0:T(1024)(128)(2,1)S(1)} %collective-permute-done.2), channel_id=1, source_target_pairs={{1,0},{2,1},{3,2},{4,3},{5,4},{6,5},{7,6},{8,7},{9,8},{10,9},{11,1... | collective-permute-start | bytes 6152 | tf_op jit(solution)/shard_map/ppermute | solution.py:15
  186.8 4.9 %collective-permute-start.6 = (bf16[1024]{0:T(1024)(128)(2,1)S(1)}, bf16[1024]{0:T(1024)(128)(2,1)S(1)}, u32[]{:S(2)}, u32[]{:S(2)}) collective-permute-start(bf16[1024]{0:T(1024)(128)(2,1)S(1)} %collective-permute-done.4), channel_id=1, source_target_pairs={{1,0},{2,1},{3,2},{4,3},{5,4},{6,5},{7,6},{8,7},{9,8},{10,9},{11,1... | collective-permute-start | bytes 6152 | tf_op jit(solution)/shard_map/ppermute | solution.py:15
  191.7 4.9 %collective-permute-start.8 = (bf16[1024]{0:T(1024)(128)(2,1)S(1)}, bf16[1024]{0:T(1024)(128)(2,1)S(1)}, u32[]{:S(2)}, u32[]{:S(2)}) collective-permute-start(bf16[1024]{0:T(1024)(128)(2,1)S(1)} %collective-permute-done.6), channel_id=1, source_target_pairs={{1,0},{2,1},{3,2},{4,3},{5,4},{6,5},{7,6},{8,7},{9,8},{10,9},{11,1... | collective-permute-start | bytes 6152 | tf_op jit(solution)/shard_map/ppermute | solution.py:15
  196.6 5.6 %copy-start.6 = (bf16[1024,1024]{1,0:T(8,128)(2,1)S(1)}, bf16[1024,1024]{1,0:T(8,128)(2,1)}, u32[]{:S(2)}) copy-start(bf16[1024,1024]{1,0:T(8,128)(2,1)} %copy-done.5) | copy-start | bytes 6291460
  196.6 16.0 %collective-permute-start.9 = (bf16[1024,1024]{1,0:T(8,128)(2,1)}, bf16[1024,1024]{1,0:T(8,128)(2,1)S(1)}, u32[]{:S(2)}, u32[]{:S(2)}) collective-permute-start(bf16[1024,1024]{1,0:T(8,128)(2,1)} %collective-permute-done.7), channel_id=1, source_target_pairs={{1,0},{2,1},{3,2},{4,3},{5,4},{6,5},{7,6},{8,7},{9,8},{10,9},{11,1... | collective-permute-start | bytes 6291464 | tf_op jit(solution)/shard_map/ppermute | solution.py:15
  212.6 41.2 %copy-start.1 = (s32[512,1]{0,1:T(1,128)S(1)}, s32[512,1]{0,1:T(1,128)}, u32[]{:S(2)}) copy-start(s32[512,1]{0,1:T(1,128)} %param.6) | copy-start | bytes 6148
  220.6 17.8 %collective-permute-start.10 = (f32[1024]{0:T(1024)S(1)}, f32[1024]{0:T(1024)S(1)}, u32[]{:S(2)}, u32[]{:S(2)}) collective-permute-start(f32[1024]{0:T(1024)S(1)} %broadcast_select_fusion), channel_id=1, source_target_pairs={{0,1},{1,2},{2,3},{3,4},{4,5},{5,6},{6,7},{7,8},{8,9},{9,10},{10,1... | collective-permute-start | bytes 12296 | tf_op jit(solution)/shard_map/ppermute | solution.py:15
  238.5 3.0 %collective-permute-start.11 = (f32[1024]{0:T(1024)S(1)}, f32[1024]{0:T(1024)S(1)}, u32[]{:S(2)}, u32[]{:S(2)}) collective-permute-start(f32[1024]{0:T(1024)S(1)} %select_maximum_fusion.3), channel_id=1, source_target_pairs={{0,1},{1,2},{2,3},{3,4},{4,5},{5,6},{6,7},{7,8},{8,9},{9,10},{10,1... | collective-permute-start | bytes 12296 | tf_op jit(solution)/shard_map/ppermute | solution.py:15
  241.5 8.2 %collective-permute-start.12 = (f32[1024]{0:T(1024)S(1)}, f32[1024]{0:T(1024)S(1)}, u32[]{:S(2)}, u32[]{:S(2)}) collective-permute-start(f32[1024]{0:T(1024)S(1)} %select_maximum_fusion.2), channel_id=1, source_target_pairs={{0,1},{1,2},{2,3},{3,4},{4,5},{5,6},{6,7},{7,8},{8,9},{9,10},{10,1... | collective-permute-start | bytes 12296 | tf_op jit(solution)/shard_map/ppermute | solution.py:15
  249.7 4.9 %collective-permute-start.13 = (f32[1024]{0:T(1024)S(1)}, f32[1024]{0:T(1024)S(1)}, u32[]{:S(2)}, u32[]{:S(2)}) collective-permute-start(f32[1024]{0:T(1024)S(1)} %select_maximum_fusion.1), channel_id=1, source_target_pairs={{0,1},{1,2},{2,3},{3,4},{4,5},{5,6},{6,7},{7,8},{8,9},{9,10},{10,1... | collective-permute-start | bytes 12296 | tf_op jit(solution)/shard_map/ppermute | solution.py:15
  254.6 6.6 %collective-permute-start.14 = (f32[1024]{0:T(1024)S(1)}, f32[1024]{0:T(1024)S(1)}, u32[]{:S(2)}, u32[]{:S(2)}) collective-permute-start(f32[1024]{0:T(1024)S(1)} %select_maximum_fusion), channel_id=1, source_target_pairs={{0,1},{1,2},{2,3},{3,4},{4,5},{5,6},{6,7},{7,8},{8,9},{9,10},{10,1... | collective-permute-start | bytes 12296 | tf_op jit(solution)/shard_map/ppermute | solution.py:15
  261.9 15.7 %all-to-all-start.2 = ((f32[16,1,64]{2,1,0:T(1,128)}), f32[16,1,64]{2,1,0:T(1,128)S(1)}, u32[]{:S(2)}, u32[]{:S(2)}) async-start(f32[16,1,64]{2,1,0:T(1,128)} %all_to_all.18), calls=%async_computation.2 | async-start | bytes 16384 | tf_op jit(solution)/shard_map/all_to_all | solution.py:81
where the time goes:
time: 283 us; the launch traced here: 282 us
  waiting for transfers between devices  100 us (35%)
  starting transfers between devices  87 us (31%)
  blocking collectives  54.5 us (19%)
  matrix products  26.5 us (9%)
  local copies, waits for them, and re-layouts  5.21 us (2%)
  other arithmetic  4.84 us (2%)
  between operations  3.48 us (1%)
    ppermute x15, waiting for transfers between devices, passed_along(): lax.ppermute(value, axis, [(source, source + steps) for source in range(i...  73.5 us
    all_to_all x1, blocking collectives, per_device(): lax.all_to_all(packed.reshape(owners, capacity, width), 'shard', split_ax...  54.5 us
    ppermute x15, starting transfers between devices, passed_along(): lax.ppermute(value, axis, [(source, source + steps) for source in range(i...  48 us
    all_to_all x1, starting transfers between devices, per_device(): lax.all_to_all(packed_scale.reshape(owners, capacity), 'shard', split_axi...  29.7 us
    dot_general x6, matrix products, scaled_tile(): lax.dot_general(left, right, (((1,), (1,)), ((), ())), preferred_element_...  24.8 us
    all_to_all x1, waiting for transfers between devices, per_device(): lax.all_to_all(packed_scale.reshape(owners, capacity), 'shard', split_axi...  20.4 us
    all_to_all x1, starting transfers between devices, per_device(): lax.all_to_all(slot_best.reshape(owners, capacity), 'shard', split_axis=0...  9.27 us
    all_to_all x1, waiting for transfers between devices, per_device(): lax.all_to_all(slot_best.reshape(owners, capacity), 'shard', split_axis=0...  6.39 us
  transfers between devices with their start and end apart: 17, of which 14 were waited for; matrix products, arithmetic and copies ran while one was open for 6% of the time, Pallas kernels for 0%

commit v1 on v0

v1 whole, which is shorter than its diff:
```python
import functools

import jax
import jax.numpy as jnp
from jax import lax
from jax.experimental import pallas as pl
from jax.experimental.pallas import tpu as pltpu
from jax.sharding import PartitionSpec as P

LOWEST = float("-inf")
WORD = 31
LANES = 128


def meet_kernel(words, sides, diagonal, chunk, count, known, *refs):
    index, moving = refs[0], refs[1]
    blocks = refs[2 : 2 + count]
    scale, ones, bits = refs[2 + count : 5 + count]
    before = dict(zip(known, refs[5 + count :]))
    outs = list(refs[5 + count + len(known) :])
    column = outs.pop() if "column" in sides else None
    rows = moving.shape[0]
    who = index[0]

    def along_sublanes(value):
        return jnp.transpose(jnp.broadcast_to(value, (LANES, rows)))

    own_scale = along_sublanes(scale[pl.ds(who, 1), :])
    own_bits = [along_sublanes(bits[pl.ds(who * words + w, 1), :]) for w in range(words)]
    best = None
    for j, block in enumerate(blocks):
        other = index[1 + j]
        other_scale = scale[pl.ds(other, 1), :]
        other_ones = [ones[pl.ds(other * words + w, 1), :] for w in range(words)]
        for first in range(0, block.shape[0], chunk):
            raw = lax.dot_general(
                moving[...],
                block[first : first + chunk, :],
                (((1,), (1,)), ((), ())),
                preferred_element_type=jnp.float32,
            )
            for at in range(0, chunk, LANES):
                here = slice(first + at, first + at + LANES)
                scores = raw[:, at : at + LANES] * own_scale * other_scale[:, here]
                shared = own_bits[0] & other_ones[0][:, here]
                for w in range(1, words):
                    shared = shared | (own_bits[w] & other_ones[w][:, here])
                keep = shared != 0
                if diagonal and j == 0:
                    row = lax.broadcasted_iota(jnp.int32, scores.shape, 0)
                    lane = lax.broadcasted_iota(jnp.int32, scores.shape, 1) + (first + at)
                    keep = keep & (row != lane)
                scores = jnp.where(keep, scores, LOWEST)
                if "row" in sides:
                    found = jnp.max(scores, axis=0, keepdims=True)
                    if j in before:
                        found = jnp.maximum(found, before[j][:, here])
                    outs[j][:, here] = found
                if column is not None:
                    best = scores if best is None else jnp.maximum(best, scores)
    if column is not None:
        column[...] = jnp.max(jnp.transpose(best), axis=0, keepdims=True)


def meet(index, moving, blocks, scale, ones, bits, words, sides, before={}, diagonal=False):
    rows, width = moving.shape
    count = len(blocks)
    chunk = min(256, rows)
    outs = []
    if "row" in sides:
        outs += [jax.ShapeDtypeStruct((1, rows), jnp.float32)] * count
    if "column" in sides:
        outs += [jax.ShapeDtypeStruct((1, rows), jnp.float32)]
    vmem = pl.BlockSpec(memory_space=pltpu.VMEM)
    return pl.pallas_call(
        functools.partial(meet_kernel, words, sides, diagonal, chunk, count, tuple(before)),
        out_shape=outs,
        in_specs=[pl.BlockSpec(memory_space=pltpu.SMEM)] + [vmem] * (count + 4 + len(before)),
        out_specs=[vmem] * len(outs),
        compiler_params=pltpu.CompilerParams(vmem_limit_bytes=20 * 2**20),
        cost_estimate=pl.CostEstimate(
            flops=2 * rows * rows * count * width,
            bytes_accessed=2 * rows * width * (count + 1),
            transcendentals=0,
        ),
    )(index, moving, *blocks, scale, ones, bits, *before.values())


def pair_words(listed, subclusters, words):
    source = jnp.arange(subclusters, dtype=jnp.int32)
    met = source[:, None] == source[None, :]
    ahead = source[None, :] - source[:, None]
    for k in range(listed.shape[1]):
        forward = (ahead == k + 1) & (listed[:, k] == 1)[:, None]
        backward = (ahead == -k - 1) & (listed[:, k] == 1)[None, :]
        met = met | forward | backward
    table = []
    for w in range(words):
        weight = jnp.where(source // WORD == w, jnp.int32(1) << (source % WORD), 0)
        table.append(jnp.sum(jnp.where(met, weight[None, :], 0), axis=1))
    return table


def per_device(embeddings, scales, cluster, pair_listed):
    rows, width = embeddings.shape
    shards = lax.axis_size("shard")
    here = lax.axis_index("shard")
    plane = 1
    while plane * plane * 4 <= shards:
        plane *= 2
    planes = shards // plane
    half = planes // 2
    owned, partners = pair_listed.shape
    subclusters = shards * owned
    words = -(-subclusters // WORD)

    order = [place // 2 + (place % 2) * half for place in range(planes)]
    place_of = [order.index(z) for z in range(planes)]

    def permuted(value, target):
        return lax.ppermute(value, "shard", [(s, target(s)) for s in range(shards)])

    def across(bit):
        return lambda s: s ^ bit

    def along(distance):
        def target(s):
            z = order[(place_of[s // plane] + distance) % planes]
            return z * plane + s % plane

        return target

    def sender_of(distance):
        table = [0] * shards
        for s in range(shards):
            table[along(distance)(s)] = s
        return jnp.asarray(table, jnp.int32)[here]

    arrived = {}
    for distance in range(half, 0, -1):
        arrived[distance] = permuted(embeddings, along(distance))
    held = {0: embeddings}
    bit = plane // 2
    while bit:
        for j in sorted(held):
            held[j | bit] = permuted(held[j], across(bit))
        bit //= 2
    blocks = [held[j] for j in range(plane)]

    pairs = jnp.pad(pair_listed.reshape(-1), (0, -(owned * partners) % LANES))
    info = jnp.concatenate(
        [scales.astype(jnp.float32), cluster[:, 0].astype(jnp.float32), pairs.astype(jnp.float32)]
    )
    everyone = lax.all_to_all(
        jnp.broadcast_to(info[None, :], (shards, info.shape[0])),
        "shard",
        split_axis=0,
        concat_axis=0,
        tiled=True,
    )
    scale = everyone[:, :rows]
    named = everyone[:, rows : 2 * rows].astype(jnp.int32)
    listed = everyone[:, 2 * rows : 2 * rows + owned * partners].astype(jnp.int32)
    table = pair_words(listed.reshape(subclusters, partners), subclusters, words)
    source = jnp.arange(subclusters, dtype=jnp.int32)
    same = named[:, None, :] == source[None, :, None]
    ones = jnp.stack(
        [jnp.where(named // WORD == w, jnp.int32(1) << (named % WORD), 0) for w in range(words)], axis=1
    ).reshape(shards * words, rows)
    bits = jnp.stack(
        [jnp.sum(jnp.where(same, table[w][None, :, None], 0), axis=1) for w in range(words)], axis=1
    ).reshape(shards * words, rows)

    mates = here ^ jnp.arange(plane, dtype=jnp.int32)

    def index_of(mover):
        return jnp.concatenate([mover[None], mates])

    [own] = meet(index_of(here), embeddings, blocks, scale, ones, bits, words, ("column",), diagonal=True)
    gathered = {0: own}
    returned = []
    for distance in range(half, 0, -1):
        two_sided = 2 * distance != planes
        found = meet(
            index_of(sender_of(distance)),
            arrived[distance],
            blocks,
            scale,
            ones,
            bits,
            words,
            ("row", "column") if two_sided else ("row",),
            gathered,
        )
        if two_sided:
            returned.append(permuted(found[plane], along(-distance)))
        gathered = dict(enumerate(found[:plane]))
    returned += [permuted(gathered[j], across(j)) for j in range(plane - 1, 0, -1)]
    result = functools.reduce(jnp.maximum, returned, gathered[0])
    return result.reshape(rows)


def solution(mesh):
    placed = (
        P(("groups", "shard"), None),
        P(("groups", "shard")),
        P(("groups", "shard"), None),
        P(("groups", "shard"), None),
    )
    return jax.shard_map(
        per_device, mesh=mesh, in_specs=placed, out_specs=P(("groups", "shard")), check_vma=False
    )
```

time: 283 us -> 77.4 us (0.27)
  starting transfers between devices: 87 us -> 15.4 us
  waiting for transfers between devices: 100 us -> 41.6 us
  blocking collectives: 54.5 us -> 0 us
  matrix products: 26.5 us -> 0 us
  Pallas kernels: 0 us -> 12.3 us
  between operations: 3.48 us -> 0.12 us
    ppermute x15 -> x9, waiting for transfers between devices: 73.5 us -> 13.3 us  [permuted(): return lax.ppermute(value, 'shard', [(s, target(s)) for s in range(shards)])]
    all_to_all x1 -> x0, blocking collectives: 54.5 us -> none  [per_device(): lax.all_to_all(packed.reshape(owners, capacity, width), 'shard', split_ax...]
    ppermute x15 -> x9, starting transfers between devices: 48 us -> 11.9 us  [permuted(): return lax.ppermute(value, 'shard', [(s, target(s)) for s in range(shards)])]
    all_to_all x2 -> x1, starting transfers between devices: 39 us -> 3.5 us  [per_device(): lax.all_to_all(jnp.broadcast_to(info[None, :], (shards, info.shape[0])),...]
    dot_general x8 -> x0, matrix products: 26.5 us -> none  [the longest x6 24.8 us: scaled_tile(): lax.dot_general(left, right, (((1,), (1,)), ((), ())), preferred_element_...]
    pallas_call x0 -> x3, Pallas kernels: none -> 12.3 us  [meet(): pl.pallas_call(functools.partial(meet_kernel, words, sides, diagonal, chu...]
    all_to_all x2 -> x1, waiting for transfers between devices: 26.8 us -> 28.3 us  [per_device(): lax.all_to_all(jnp.broadcast_to(info[None, :], (shards, info.shape[0])),...]
  transfers between devices with their start and end apart: 17 -> 10, of which waited for: 14 -> 4; matrix products, arithmetic and copies ran while one was open for 6% -> 6% of each run, Pallas kernels for 0% -> 11%
where the time goes in v1:
time: 77.4 us; the launch traced here: 77.1 us
  waiting for transfers between devices  41.6 us (54%)
  starting transfers between devices  15.4 us (20%)
  Pallas kernels  12.3 us (16%)
  local copies, waits for them, and re-layouts  4.44 us (6%)
  other arithmetic  3.21 us (4%)
    all_to_all x1, waiting for transfers between devices, per_device(): lax.all_to_all(jnp.broadcast_to(info[None, :], (shards, info.shape[0])),...  28.3 us
    ppermute x9, waiting for transfers between devices, permuted(): return lax.ppermute(value, 'shard', [(s, target(s)) for s in range(shards)])  13.3 us
    pallas_call x3, Pallas kernels, meet(): pl.pallas_call(functools.partial(meet_kernel, words, sides, diagonal, chu...  12.3 us
    ppermute x9, starting transfers between devices, permuted(): return lax.ppermute(value, 'shard', [(s, target(s)) for s in range(shards)])  11.9 us
    all_to_all x1, starting transfers between devices, per_device(): lax.all_to_all(jnp.broadcast_to(info[None, :], (shards, info.shape[0])),...  3.5 us
    unnamed x11, local copies, waits for them, and re-layouts  2.58 us
  transfers between devices with their start and end apart: 10, of which 4 were waited for; matrix products, arithmetic and copies ran while one was open for 6% of the time, Pallas kernels for 11%

profile of v1, /device:TPU:0, one launch (start us, length us, event | category | flops | bytes accessed | tf_op | source)
XLA Modules:
  0.0 77.1 jit_solution(17832687544226461374)
XLA Ops:
  0.0 3.0 %collective-permute-start.2 = (bf16[512,1024]{1,0:T(8,128)(2,1)}, bf16[512,1024]{1,0:T(8,128)(2,1)S(1)}, u32[]{:S(2)}, u32[]{:S(2)}) collective-permute-start(bf16[512,1024]{1,0:T(8,128)(2,1)} %refs_2_.5), channel_id=1, source_target_pairs={{0,2},{1,3},{2,0},{3,1},{4,6},{5,7},{6,4},{7,5},{8,10},{9,11},{10,... | collective-permute-start | bytes 3145736 | tf_op jit(solution)/shard_map/ppermute | solution.py:121
  3.0 1.6 %collective-permute-start.4 = (bf16[512,1024]{1,0:T(8,128)(2,1)}, bf16[512,1024]{1,0:T(8,128)(2,1)}, u32[]{:S(2)}, u32[]{:S(2)}) collective-permute-start(bf16[512,1024]{1,0:T(8,128)(2,1)} %refs_2_.5), channel_id=1, source_target_pairs={{0,4},{1,5},{2,6},{3,7},{4,0},{5,1},{6,2},{7,3},{8,12},{9,13},{10,... | collective-permute-start | bytes 3145736 | tf_op jit(solution)/shard_map/ppermute | solution.py:121
  4.5 2.6 %collective-permute-start = (bf16[512,1024]{1,0:T(8,128)(2,1)}, bf16[512,1024]{1,0:T(8,128)(2,1)S(1)}, u32[]{:S(2)}, u32[]{:S(2)}) collective-permute-start(bf16[512,1024]{1,0:T(8,128)(2,1)} %refs_2_.5), channel_id=1, source_target_pairs={{0,8},{1,9},{2,10},{3,11},{4,12},{5,13},{6,14},{7,15},{8,4},{9,5},... | collective-permute-start | bytes 3145736 | tf_op jit(solution)/shard_map/ppermute | solution.py:121
  7.1 0.7 convert_element_type.18
  7.8 0.6 copy-done.2
  8.5 0.7 broadcast_in_dim.23
  9.2 3.5 %all-to-all-start = ((f32[16,1,1152]{2,1,0:T(1,128)}), f32[16,1,1152]{2,1,0:T(1,128)S(1)}, u32[]{:S(2)}, u32[]{:S(2)}) async-start(f32[16,1,1152]{2,1,0:T(1,128)} %broadcast_in_dim.23), calls=%async_computation | async-start | bytes 147456 | tf_op jit(solution)/shard_map/all_to_all | solution.py:154
  12.7 0.6 copy-done.4
  13.3 0.6 dynamic_slice.6
  14.0 0.6 dynamic_slice.7
  14.6 1.3 %pad_add_fusion.2 = (s32[5]{0:T(128)S(1)}, s32[5]{0:T(128)S(1)}, s32[5]{0:T(128)S(1)}) fusion(s32[1]{0:T(128)} %bitcast.2, s32[4]{0:T(128)S(1)} %iota_xor_fusion, s32[1]{0:T(128)} %dynamic_slice.7, s32[1]{0:T(128)} %dynamic_slice.6), kind=kLoop, calls=%fused_computation.65 | loop fusion | flops 15 | bytes 88 | tf_op jit(solution)/shard_map/concatenate | solution.py:177
  15.9 10.6 %collective-permute-done.2.refs_4_ = bf16[512,1024]{1,0:T(8,128)(2,1)S(1)} collective-permute-done((bf16[512,1024]{1,0:T(8,128)(2,1)}, bf16[512,1024]{1,0:T(8,128)(2,1)S(1)}, u32[]{:S(2)}, u32[]{:S(2)}) %collective-permute-start.2) | collective-permute-done | bytes 1048608 | tf_op jit(solution)/shard_map/ppermute | solution.py:121
  26.4 28.3 %all-to-all-done = f32[16,1,1152]{2,1,0:T(1,128)S(1)} async-done(((f32[16,1,1152]{2,1,0:T(1,128)}), f32[16,1,1152]{2,1,0:T(1,128)S(1)}, u32[]{:S(2)}, u32[]{:S(2)}) %all-to-all-start) | async-done | bytes 73760 | tf_op jit(solution)/shard_map/all_to_all | solution.py:154
  55.5 1.2 %copy-done = bf16[512,1024]{1,0:T(8,128)(2,1)S(1)} copy-done((bf16[512,1024]{1,0:T(8,128)(2,1)S(1)}, bf16[512,1024]{1,0:T(8,128)(2,1)}, u32[]{:S(2)}) %copy-start) | copy-done | bytes 1048600
  56.7 4.0 %shard_map.64.refs_9_ = f32[1,512]{1,0:T(1,128)S(1)} custom-call(s32[5]{0:T(128)S(1)} %get-tuple-element.30.refs_0_, bf16[512,1024]{1,0:T(8,128)(2,1)S(1)} %copy-done, bf16[512,1024]{1,0:T(8,128)(2,1)S(1)} %copy-done, bf16[512,1024]{1,0:T(8,128)(2,1)S(1)} %collective-permute-done.1.refs_3_, bf16[512,1024]{1,0:T(8,128)(2,1)S(1)} %collective-permute-done.2.refs_4_, ...), custom_call_target="tpu_custom_call" | custom-call | flops 2147483648 | bytes 5242880 | tf_op jit(solution)/shard_map/pallas_call | solution.py:75
  60.7 4.3 %shard_map.65 = (f32[1,512]{1,0:T(1,128)S(1)}, f32[1,512]{1,0:T(1,128)S(1)}, f32[1,512]{1,0:T(1,128)S(1)}, f32[1,512]{1,0:T(1,128)S(1)}) custom-call(s32[5]{0:T(128)S(1)} %get-tuple-element.31.refs_0_, bf16[512,1024]{1,0:T(8,128)(2,1)} %collective-permute-done.4.refs_1_, bf16[512,1024]{1,0:T(8,128)(2,1)S(1)} %copy-done, ...), custom_call_target="tpu_custom_call" | custom-call | flops 2147483648 | bytes 5242880 | tf_op jit(solution)/shard_map/pallas_call | solution.py:75
  65.0 4.1 %shard_map.66 = (f32[1,512]{1,0:T(1,128)S(1)}, f32[1,512]{1,0:T(1,128)S(1)}, f32[1,512]{1,0:T(1,128)S(1)}, f32[1,512]{1,0:T(1,128)S(1)}, f32[1,512]{1,0:T(1,128)S(1)}) custom-call(s32[5]{0:T(128)S(1)} %get-tuple-element.32.refs_0_, bf16[512,1024]{1,0:T(8,128)(2,1)S(1)} %collective-permute-done.refs_1_, bf16[512,1024]{1,0:T(8,128)(2,1)S(1)} %copy-done, ...), custom_call_target="tpu_custom_call" | custom-call | flops 2147483648 | bytes 5242880 | tf_op jit(solution)/shard_map/pallas_call | solution.py:75
  69.1 2.9 %collective-permute-start.5 = (f32[1,512]{1,0:T(1,128)S(1)}, f32[1,512]{1,0:T(1,128)S(1)}, u32[]{:S(2)}, u32[]{:S(2)}) collective-permute-start(f32[1,512]{1,0:T(1,128)S(1)} %get-tuple-element.19), channel_id=1, source_target_pairs={{0,12},{1,13},{2,14},{3,15},{4,8},{5,9},{6,10},{7,11},{8,0},{9,1},... | collective-permute-start | bytes 6152 | tf_op jit(solution)/shard_map/ppermute | solution.py:121
  71.9 0.9 %collective-permute-start.6 = (f32[1,512]{1,0:T(1,128)S(1)}, f32[1,512]{1,0:T(1,128)S(1)}, u32[]{:S(2)}, u32[]{:S(2)}) collective-permute-start(f32[1,512]{1,0:T(1,128)S(1)} %get-tuple-element.20), channel_id=1, source_target_pairs={{0,3},{1,2},{2,1},{3,0},{4,7},{5,6},{6,5},{7,4},{8,11},{9,10},{10,... | collective-permute-start | bytes 6152 | tf_op jit(solution)/shard_map/ppermute | solution.py:121
  72.9 0.6 collective-permute-start.7
  73.5 0.3 collective-permute-start.8
  73.8 1.1 %collective-permute-done.6 = f32[1,512]{1,0:T(1,128)S(1)} collective-permute-done((f32[1,512]{1,0:T(1,128)S(1)}, f32[1,512]{1,0:T(1,128)S(1)}, u32[]{:S(2)}, u32[]{:S(2)}) %collective-permute-start.6) | collective-permute-done | bytes 2080 | tf_op jit(solution)/shard_map/ppermute | solution.py:121
  74.9 1.5 %collective-permute-done.7 = f32[1,512]{1,0:T(1,128)S(1)} collective-permute-done((f32[1,512]{1,0:T(1,128)S(1)}, f32[1,512]{1,0:T(1,128)S(1)}, u32[]{:S(2)}, u32[]{:S(2)}) %collective-permute-start.7) | collective-permute-done | bytes 2080 | tf_op jit(solution)/shard_map/ppermute | solution.py:121
  76.5 0.6 maximum_maximum_fusion
  (27 shorter events, 0.8 us)
Async XLA Ops:
  0.0 7.8 %copy-start.1 = (s32[512,1]{0,1:T(1,128)S(1)}, s32[512,1]{0,1:T(1,128)}, u32[]{:S(2)}) copy-start(s32[512,1]{0,1:T(1,128)} %param.8) | copy-start | bytes 6148
  0.0 26.4 %collective-permute-start.2 = (bf16[512,1024]{1,0:T(8,128)(2,1)}, bf16[512,1024]{1,0:T(8,128)(2,1)S(1)}, u32[]{:S(2)}, u32[]{:S(2)}) collective-permute-start(bf16[512,1024]{1,0:T(8,128)(2,1)} %refs_2_.5), channel_id=1, source_target_pairs={{0,2},{1,3},{2,0},{3,1},{4,6},{5,7},{6,4},{7,5},{8,10},{9,11},{10,... | collective-permute-start | bytes 3145736 | tf_op jit(solution)/shard_map/ppermute | solution.py:121
  3.0 57.7 %collective-permute-start.4 = (bf16[512,1024]{1,0:T(8,128)(2,1)}, bf16[512,1024]{1,0:T(8,128)(2,1)}, u32[]{:S(2)}, u32[]{:S(2)}) collective-permute-start(bf16[512,1024]{1,0:T(8,128)(2,1)} %refs_2_.5), channel_id=1, source_target_pairs={{0,4},{1,5},{2,6},{3,7},{4,0},{5,1},{6,2},{7,3},{8,12},{9,13},{10,... | collective-permute-start | bytes 3145736 | tf_op jit(solution)/shard_map/ppermute | solution.py:121
  4.5 50.9 %collective-permute-start.1 = (bf16[512,1024]{1,0:T(8,128)(2,1)}, bf16[512,1024]{1,0:T(8,128)(2,1)S(1)}, u32[]{:S(2)}, u32[]{:S(2)}) collective-permute-start(bf16[512,1024]{1,0:T(8,128)(2,1)} %refs_2_.5), channel_id=1, source_target_pairs={{0,1},{1,0},{2,3},{3,2},{4,5},{5,4},{6,7},{7,6},{8,9},{9,8},{10,11... | collective-permute-start | bytes 3145736 | tf_op jit(solution)/shard_map/ppermute | solution.py:121
  4.5 60.4 %collective-permute-start = (bf16[512,1024]{1,0:T(8,128)(2,1)}, bf16[512,1024]{1,0:T(8,128)(2,1)S(1)}, u32[]{:S(2)}, u32[]{:S(2)}) collective-permute-start(bf16[512,1024]{1,0:T(8,128)(2,1)} %refs_2_.5), channel_id=1, source_target_pairs={{0,8},{1,9},{2,10},{3,11},{4,12},{5,13},{6,14},{7,15},{8,4},{9,5},... | collective-permute-start | bytes 3145736 | tf_op jit(solution)/shard_map/ppermute | solution.py:121
  7.8 0.7 copy-start.2
  9.2 45.6 %all-to-all-start = ((f32[16,1,1152]{2,1,0:T(1,128)}), f32[16,1,1152]{2,1,0:T(1,128)S(1)}, u32[]{:S(2)}, u32[]{:S(2)}) async-start(f32[16,1,1152]{2,1,0:T(1,128)} %broadcast_in_dim.23), calls=%async_computation | async-start | bytes 147456 | tf_op jit(solution)/shard_map/all_to_all | solution.py:154
  12.7 0.7 copy-start.4
  13.3 0.7 copy-start.3
  26.4 29.0 %collective-permute-start.3 = (bf16[512,1024]{1,0:T(8,128)(2,1)S(1)}, bf16[512,1024]{1,0:T(8,128)(2,1)}, u32[]{:S(2)}, u32[]{:S(2)}) collective-permute-start(bf16[512,1024]{1,0:T(8,128)(2,1)S(1)} %collective-permute-done.2.refs_4_), channel_id=1, source_target_pairs={{0,1},{1,0},{2,3},{3,2},{4,5},{5,4},{6,7},{7,6},{8,9},{9,8},{10,11... | collective-permute-start | bytes 3145736 | tf_op jit(solution)/shard_map/ppermute | solution.py:121
  55.4 1.2 %copy-start = (bf16[512,1024]{1,0:T(8,128)(2,1)S(1)}, bf16[512,1024]{1,0:T(8,128)(2,1)}, u32[]{:S(2)}) copy-start(bf16[512,1024]{1,0:T(8,128)(2,1)} %refs_2_.5) | copy-start | bytes 3145732
  69.1 4.7 %collective-permute-start.5 = (f32[1,512]{1,0:T(1,128)S(1)}, f32[1,512]{1,0:T(1,128)S(1)}, u32[]{:S(2)}, u32[]{:S(2)}) collective-permute-start(f32[1,512]{1,0:T(1,128)S(1)} %get-tuple-element.19), channel_id=1, source_target_pairs={{0,12},{1,13},{2,14},{3,15},{4,8},{5,9},{6,10},{7,11},{8,0},{9,1},... | collective-permute-start | bytes 6152 | tf_op jit(solution)/shard_map/ppermute | solution.py:121
  71.9 3.0 %collective-permute-start.6 = (f32[1,512]{1,0:T(1,128)S(1)}, f32[1,512]{1,0:T(1,128)S(1)}, u32[]{:S(2)}, u32[]{:S(2)}) collective-permute-start(f32[1,512]{1,0:T(1,128)S(1)} %get-tuple-element.20), channel_id=1, source_target_pairs={{0,3},{1,2},{2,1},{3,0},{4,7},{5,6},{6,5},{7,4},{8,11},{9,10},{10,... | collective-permute-start | bytes 6152 | tf_op jit(solution)/shard_map/ppermute | solution.py:121
  72.9 3.6 %collective-permute-start.7 = (f32[1,512]{1,0:T(1,128)S(1)}, f32[1,512]{1,0:T(1,128)S(1)}, u32[]{:S(2)}, u32[]{:S(2)}) collective-permute-start(f32[1,512]{1,0:T(1,128)S(1)} %get-tuple-element.21), channel_id=1, source_target_pairs={{0,2},{1,3},{2,0},{3,1},{4,6},{5,7},{6,4},{7,5},{8,10},{9,11},{10,... | collective-permute-start | bytes 6152 | tf_op jit(solution)/shard_map/ppermute | solution.py:121
  73.5 3.0 %collective-permute-start.8 = (f32[1,512]{1,0:T(1,128)S(1)}, f32[1,512]{1,0:T(1,128)S(1)}, u32[]{:S(2)}, u32[]{:S(2)}) collective-permute-start(f32[1,512]{1,0:T(1,128)S(1)} %get-tuple-element.22), channel_id=1, source_target_pairs={{0,1},{1,0},{2,3},{3,2},{4,5},{5,4},{6,7},{7,6},{8,9},{9,8},{10,11... | collective-permute-start | bytes 6152 | tf_op jit(solution)/shard_map/ppermute | solution.py:121

commit v2 on v0

v2 whole, which is shorter than its diff:
```python
import functools

import jax
import jax.numpy as jnp
from jax import lax
from jax.experimental import pallas as pl
from jax.experimental.pallas import tpu as pltpu
from jax.sharding import PartitionSpec as P

LOWEST = float("-inf")
WORD = 16
LANES = 128
SUBLANES = 8
STRIP = 64
VMEM_RAW = 24 * 2**20
VMEM_CALL = 40 * 2**20


def product_kernel(moving, *refs):
    blocks, out = refs[:-1], refs[-1]
    rows = moving.shape[0]
    chunk = min(256, rows)
    for j, block in enumerate(blocks):
        for first in range(0, rows, chunk):
            out[:, j * rows + first : j * rows + first + chunk] = lax.dot_general(
                moving[...],
                block[first : first + chunk, :],
                (((1,), (1,)), ((), ())),
                preferred_element_type=jnp.float32,
            )


def products(moving, blocks):
    rows, width = moving.shape
    vmem = pl.BlockSpec(memory_space=pltpu.VMEM)
    return pl.pallas_call(
        product_kernel,
        out_shape=jax.ShapeDtypeStruct((rows, len(blocks) * rows), jnp.float32),
        in_specs=[vmem] * (1 + len(blocks)),
        out_specs=vmem,
        compiler_params=pltpu.CompilerParams(vmem_limit_bytes=VMEM_CALL),
        cost_estimate=pl.CostEstimate(
            flops=2 * rows * rows * len(blocks) * width,
            bytes_accessed=2 * rows * width * (len(blocks) + 1),
            transcendentals=0,
        ),
    )(moving, *blocks)


def maxima_kernel(partners, count, kinds, carried, index, device, everyone, *refs):
    raws = refs[: len(kinds)]
    before = refs[len(kinds) : len(kinds) + carried]
    row_outs = refs[len(kinds) + carried : len(kinds) + carried + count]
    column_outs = list(refs[len(kinds) + carried + count : -1])
    strip_best = refs[-1]
    rows = raws[0].shape[0]
    strip = min(STRIP, rows)
    per_block = rows // LANES
    groups = count * per_block

    shards = everyone.shape[0]
    words = -(-shards // WORD)
    source = device[...]
    table = pair_words(everyone[:, 2 * rows :], source, partners, words)

    def scale_of(at):
        return everyone[at : at + 1, 0:rows]

    def cluster_of(at):
        return everyone[at : at + 1, rows : 2 * rows].astype(jnp.int32)

    def bits_of(at):
        named = cluster_of(at) == source
        return [jnp.sum(jnp.where(named, t, 0.0), axis=0, keepdims=True).astype(jnp.int32) for t in table]

    def ones_of(at):
        named = cluster_of(at)
        return [jnp.where(named // WORD == w, jnp.int32(1) << (named % WORD), 0) for w in range(words)]

    def along_sublanes(value):
        return jnp.transpose(jnp.broadcast_to(value, (LANES, rows)))

    lane_scale = [scale_of(index[j]) for j in range(count)]
    lane_ones = [ones_of(index[j]) for j in range(count)]

    def lanes_of(per, g):
        first = g % per_block * LANES
        return per[g // per_block][:, first : first + LANES]

    row_part = [None] * groups
    own_best = None
    for r, (same, wants_row, wants_column) in enumerate(kinds):
        who = index[count + r]
        mine = scale_of(who)
        mine_down = along_sublanes(mine)
        bits_down = [along_sublanes(b) for b in bits_of(who)]
        for first in range(0, rows, strip):
            here = slice(first, first + strip)
            best = None
            for g in range(groups):
                value = raws[r][here, g * LANES : (g + 1) * LANES]
                met = bits_down[0][here] & lanes_of([o[0] for o in lane_ones], g)
                for w in range(1, words):
                    met = met | (bits_down[w][here] & lanes_of([o[w] for o in lane_ones], g))
                keep = met != 0
                if same and g < per_block and g * LANES < first + strip and first < (g + 1) * LANES:
                    down = lax.broadcasted_iota(jnp.int32, value.shape, 0) + first
                    across = lax.broadcasted_iota(jnp.int32, value.shape, 1) + g * LANES
                    keep = keep & (down != across)
                if wants_row:
                    value = jnp.where(keep, value * mine_down[here], LOWEST)
                    part = jnp.max(value.reshape(strip // SUBLANES, SUBLANES, LANES), axis=0)
                    row_part[g] = part if row_part[g] is None else jnp.maximum(row_part[g], part)
                    if wants_column:
                        value = value * lanes_of(lane_scale, g)
                else:
                    value = jnp.where(keep, value * lanes_of(lane_scale, g), LOWEST)
                if wants_column:
                    best = value if best is None else jnp.maximum(best, value)
            if wants_column:
                strip_best[here, :] = best
        if wants_column:
            found = jnp.max(jnp.transpose(strip_best[...]), axis=0, keepdims=True)
            if not wants_row:
                found = found * mine
            if same:
                own_best = found
            else:
                column_outs.pop(0)[...] = found
    for j in range(count):
        for at in range(per_block):
            here = slice(at * LANES, (at + 1) * LANES)
            part = row_part[j * per_block + at]
            found = None
            if part is not None:
                found = jnp.max(part, axis=0, keepdims=True) * lane_scale[j][:, here]
            for other in ([own_best] if j == 0 and own_best is not None else []) + ([before[j]] if carried else []):
                found = other[:, here] if found is None else jnp.maximum(found, other[:, here])
            row_outs[j][:, here] = found


def maxima(index, device, everyone, partners, raws, kinds, count, before):
    rows = raws[0].shape[0]
    vmem = pl.BlockSpec(memory_space=pltpu.VMEM)
    columns = sum(column and not same for same, _, column in kinds)
    return pl.pallas_call(
        functools.partial(maxima_kernel, partners, count, tuple(kinds), len(before), index),
        out_shape=[jax.ShapeDtypeStruct((1, rows), jnp.float32)] * (count + columns),
        in_specs=[vmem] * (2 + len(raws) + len(before)),
        out_specs=[vmem] * (count + columns),
        scratch_shapes=[pltpu.VMEM((rows, LANES), jnp.float32)],
        compiler_params=pltpu.CompilerParams(vmem_limit_bytes=VMEM_CALL),
        cost_estimate=pl.CostEstimate(
            flops=8 * rows * rows * count * len(raws),
            bytes_accessed=4 * rows * rows * count * len(raws),
            transcendentals=0,
        ),
    )(device, everyone, *raws, *before)


def pair_words(listed, source, partners, words):
    shards = listed.shape[0]
    lane = lax.broadcasted_iota(jnp.int32, listed.shape, 1)
    target = source + lane + 1
    used = (lane < partners) & (target < shards) & (listed == 1.0)

    def weight(which, w):
        return jnp.where(which // WORD == w, jnp.int32(1) << (which % WORD), 0).astype(jnp.float32)

    table = []
    for w in range(words):
        met = jnp.where(used, weight(target, w), 0.0) + jnp.where(lane == 0, weight(source, w), 0.0)
        met = jnp.sum(met, axis=1, keepdims=True)
        behind = jnp.where(used, weight(source, w), 0.0)
        for i in range(shards):
            hit = jnp.where(target == source[i : i + 1, :], behind, 0.0)
            here = jnp.sum(jnp.sum(hit, axis=0, keepdims=True), axis=1, keepdims=True)
            met = met + jnp.where(lax.broadcasted_iota(jnp.int32, met.shape, 0) == i, here, 0.0)
        table.append(met)
    return table


def joined_kernel(*refs):
    pieces, out = refs[:-2], refs[-1]
    at = 0
    for piece in pieces:
        out[at : at + piece.shape[0], :] = piece[...]
        at += piece.shape[0]


def joined(pieces, after):
    vmem = pl.BlockSpec(memory_space=pltpu.VMEM)
    return pl.pallas_call(
        joined_kernel,
        out_shape=jax.ShapeDtypeStruct((sum(p.shape[0] for p in pieces), pieces[0].shape[1]), jnp.float32),
        in_specs=[vmem] * len(pieces) + [pl.BlockSpec(memory_space=pl.ANY)],
        out_specs=vmem,
        compiler_params=pltpu.CompilerParams(vmem_limit_bytes=2**20),
    )(*pieces, after)


def device_table(shards, plane, planes, order, place_of, here):
    rel = jnp.arange(shards, dtype=jnp.int32)
    place = jnp.sum(jnp.where(jnp.arange(planes) == here // plane, jnp.asarray(place_of, jnp.int32), 0))
    place = (place - rel // plane) % planes
    z = jnp.sum(jnp.where(place[:, None] == jnp.arange(planes)[None, :], jnp.asarray(order, jnp.int32)[None, :], 0), axis=1)
    return (z * plane + (here % plane ^ rel % plane)).reshape(shards, 1)


def per_device(embeddings, scales, cluster, pair_listed):
    rows, width = embeddings.shape
    shards = lax.axis_size("shard")
    here = lax.axis_index("shard")
    plane = 1
    while plane * plane * 4 <= shards:
        plane *= 2
    planes = shards // plane
    half = planes // 2
    owned, partners = pair_listed.shape

    order = [place // 2 + (place % 2) * half for place in range(planes)]
    place_of = [order.index(z) for z in range(planes)]

    def permuted(value, target):
        return lax.ppermute(value, "shard", [(s, target(s)) for s in range(shards)])

    def across(bit):
        return lambda s: s ^ bit

    def along(distance):
        def target(s):
            z = order[(place_of[s // plane] + distance) % planes]
            return z * plane + s % plane

        return target

    arrived = {}
    for distance in range(1, half + 1):
        arrived[distance] = permuted(embeddings, along(distance))
    held = {0: embeddings}
    bit = plane // 2
    while bit:
        for j in sorted(held):
            held[j | bit] = permuted(held[j], across(bit))
        bit //= 2
    blocks = [held[j] for j in range(plane)]

    pairs = jnp.pad(pair_listed.reshape(-1).astype(jnp.float32), (0, -(owned * partners) % LANES))
    told = jnp.concatenate([scales.astype(jnp.float32), cluster[:, 0].astype(jnp.float32), pairs])[None, :]
    pieces, bit = [told], 1
    while bit < plane:
        mine = pieces[0] if len(pieces) == 1 else jnp.concatenate(pieces, axis=0)
        pieces.append(permuted(mine, across(bit)))
        bit *= 2
    raw = products(embeddings, blocks)
    tiles = [(0, raw, (True, False, True))]
    told = joined(pieces, raw)
    everyone = jnp.concatenate([told] + [permuted(told, along(t)) for t in range(1, planes)], axis=0)
    for distance in range(half, 0, -1):
        moving, raw = lax.optimization_barrier((arrived[distance], raw))
        tiles[-1] = (tiles[-1][0], raw, tiles[-1][2])
        raw = products(moving, blocks)
        tiles.append((distance * plane, raw, (False, True, 2 * distance != planes)))
    device = device_table(shards, plane, planes, order, place_of, here)
    at_once = max(1, VMEM_RAW // (4 * rows * rows * plane))
    gathered, columns = [], []
    for first in range(0, len(tiles), at_once):
        part = tiles[first : first + at_once]
        rows_of = tuple(range(plane)) + tuple(tile[0] for tile in part)
        found = maxima(rows_of, device, everyone, partners, [t[1] for t in part], [t[2] for t in part], plane, gathered)
        gathered = found[:plane]
        columns += found[plane:]

    result = gathered[0]
    returned = []
    for distance in range(half - (2 * half == planes), 0, -1):
        returned.append(permuted(columns.pop(0), along(-distance)))
    returned += [permuted(gathered[j], across(j)) for j in range(plane - 1, 0, -1)]
    return functools.reduce(jnp.maximum, returned, result).reshape(rows)


def solution(mesh):
    placed = (
        P(("groups", "shard"), None),
        P(("groups", "shard")),
        P(("groups", "shard"), None),
        P(("groups", "shard"), None),
    )
    return jax.shard_map(
        per_device, mesh=mesh, in_specs=placed, out_specs=P(("groups", "shard")), check_vma=False
    )
```

time: 283 us -> 68.8 us (0.24)
  starting transfers between devices: 87 us -> 16 us
  waiting for transfers between devices: 100 us -> 33.1 us
  blocking collectives: 54.5 us -> 0 us
  matrix products: 26.5 us -> 0 us
  Pallas kernels: 0 us -> 12.6 us
  local copies, waits for them, and re-layouts: 5.21 us -> 1.32 us
  between operations: 3.48 us -> 0.13 us
    all_to_all x1 -> x0, blocking collectives: 54.5 us -> none  [per_device(): lax.all_to_all(packed.reshape(owners, capacity, width), 'shard', split_ax...]
    ppermute x15 -> x14, waiting for transfers between devices: 73.5 us -> 33.1 us  [permuted(): return lax.ppermute(value, 'shard', [(s, target(s)) for s in range(shards)])]
    all_to_all x2 -> x0, starting transfers between devices: 39 us -> none  [the longest x1 29.7 us: per_device(): lax.all_to_all(packed_scale.reshape(owners, capacity), 'shard', split_axi...]
    ppermute x15 -> x14, starting transfers between devices: 48 us -> 16 us  [permuted(): return lax.ppermute(value, 'shard', [(s, target(s)) for s in range(shards)])]
    all_to_all x2 -> x0, waiting for transfers between devices: 26.8 us -> none  [the longest x1 20.4 us: per_device(): lax.all_to_all(packed_scale.reshape(owners, capacity), 'shard', split_axi...]
    dot_general x8 -> x0, matrix products: 26.5 us -> none  [the longest x6 24.8 us: scaled_tile(): lax.dot_general(left, right, (((1,), (1,)), ((), ())), preferred_element_...]
    pallas_call x0 -> x5, Pallas kernels: none -> 12.6 us  [the longest x3 9.56 us: products(): pl.pallas_call(product_kernel, out_shape=jax.ShapeDtypeStruct((rows, len(...]
  transfers between devices with their start and end apart: 17 -> 14, of which waited for: 14 -> 3; matrix products, arithmetic and copies ran while one was open for 6% -> 7% of each run, Pallas kernels for 0% -> 14%
where the time goes in v2:
time: 68.8 us; the launch traced here: 68.5 us
  waiting for transfers between devices  33.1 us (48%)
  starting transfers between devices  16 us (23%)
  Pallas kernels  12.6 us (18%)
  other arithmetic  5.36 us (8%)
  local copies, waits for them, and re-layouts  1.32 us (2%)
    ppermute x14, waiting for transfers between devices, permuted(): return lax.ppermute(value, 'shard', [(s, target(s)) for s in range(shards)])  33.1 us
    ppermute x14, starting transfers between devices, permuted(): return lax.ppermute(value, 'shard', [(s, target(s)) for s in range(shards)])  16 us
    pallas_call x3, Pallas kernels, products(): pl.pallas_call(product_kernel, out_shape=jax.ShapeDtypeStruct((rows, len(...  9.56 us
    pallas_call x1, Pallas kernels, maxima(): pl.pallas_call(functools.partial(maxima_kernel, partners, count, tuple(ki...  3.01 us
  transfers between devices with their start and end apart: 14, of which 3 were waited for; matrix products, arithmetic and copies ran while one was open for 7% of the time, Pallas kernels for 14%

profile of v2, /device:TPU:0, one launch (start us, length us, event | category | flops | bytes accessed | tf_op | source)
XLA Modules:
  0.0 68.5 jit_solution(16701652377530524708)
XLA Ops:
  0.0 3.0 %collective-permute-start.3 = (bf16[512,1024]{1,0:T(8,128)(2,1)}, bf16[512,1024]{1,0:T(8,128)(2,1)S(1)}, u32[]{:S(2)}, u32[]{:S(2)}) collective-permute-start(bf16[512,1024]{1,0:T(8,128)(2,1)} %refs_0_.5), channel_id=1, source_target_pairs={{0,2},{1,3},{2,0},{3,1},{4,6},{5,7},{6,4},{7,5},{8,10},{9,11},{10,... | collective-permute-start | bytes 3145736 | tf_op jit(solution)/shard_map/ppermute | solution.py:225
  3.0 2.6 %collective-permute-start.9 = (bf16[512,1024]{1,0:T(8,128)(2,1)}, bf16[512,1024]{1,0:T(8,128)(2,1)}, u32[]{:S(2)}, u32[]{:S(2)}) collective-permute-start(bf16[512,1024]{1,0:T(8,128)(2,1)} %refs_0_.5), channel_id=1, source_target_pairs={{0,8},{1,9},{2,10},{3,11},{4,12},{5,13},{6,14},{7,15},{8,4},{9,5},... | collective-permute-start | bytes 3145736 | tf_op jit(solution)/shard_map/ppermute | solution.py:225
  5.6 1.6 %collective-permute-start.8 = (bf16[512,1024]{1,0:T(8,128)(2,1)}, bf16[512,1024]{1,0:T(8,128)(2,1)}, u32[]{:S(2)}, u32[]{:S(2)}) collective-permute-start(bf16[512,1024]{1,0:T(8,128)(2,1)} %refs_0_.5), channel_id=1, source_target_pairs={{0,4},{1,5},{2,6},{3,7},{4,0},{5,1},{6,2},{7,3},{8,12},{9,13},{10,... | collective-permute-start | bytes 3145736 | tf_op jit(solution)/shard_map/ppermute | solution.py:225
  7.1 0.7 convert_element_type.17
  7.8 0.7 convert_element_type.18
  8.5 0.7 convert_bitcast_fusion
  9.2 17.2 %collective-permute-done.3.refs_2_ = bf16[512,1024]{1,0:T(8,128)(2,1)S(1)} collective-permute-done((bf16[512,1024]{1,0:T(8,128)(2,1)}, bf16[512,1024]{1,0:T(8,128)(2,1)S(1)}, u32[]{:S(2)}, u32[]{:S(2)}) %collective-permute-start.3) | collective-permute-done | bytes 1048608 | tf_op jit(solution)/shard_map/ppermute | solution.py:225
  26.4 0.6 collective-permute-start
  26.9 1.3 %fusion.6 = s32[]{:T(128)} fusion(s32[4]{0:T(128)} %constant.61.clone, s32[]{:T(128)S(6)} %select_n.49), kind=kLoop, calls=%fused_computation.23 | loop fusion | flops 11 | bytes 24 | tf_op jit(solution)/shard_map/reduce_sum | solution.py:204
  28.2 0.7 and_select_fusion
  28.9 0.7 %select_reduce_fusion = s32[16]{0:T(128)S(1)} fusion(s32[4]{0:T(128)} %constant.61.clone, s32[16]{0:T(128)S(1)} %and_select_fusion), kind=kLoop, calls=%fused_computation.14 | loop fusion | flops 176 | bytes 144 | tf_op jit(solution)/shard_map/reduce_sum | solution.py:206
  29.7 1.8 %collective-permute-start.1 = (f32[2,1152]{1,0:T(2,128)S(1)}, f32[2,1152]{1,0:T(2,128)S(1)}, u32[]{:S(2)}, u32[]{:S(2)}) collective-permute-start(f32[2,1152]{1,0:T(2,128)S(1)} %pad_maximum_fusion.1), channel_id=1, source_target_pairs={{0,2},{1,3},{2,0},{3,1},{4,6},{5,7},{6,4},{7,5},{8,10},{9,11},{10,... | collective-permute-start | bytes 27656 | tf_op jit(solution)/shard_map/ppermute | solution.py:225
  31.6 1.2 %copy-done = bf16[512,1024]{1,0:T(8,128)(2,1)S(1)} copy-done((bf16[512,1024]{1,0:T(8,128)(2,1)S(1)}, bf16[512,1024]{1,0:T(8,128)(2,1)}, u32[]{:S(2)}) %copy-start) | copy-done | bytes 1048600
  32.8 2.4 %shard_map.64.refs_3_.refs_0_ = f32[512,2048]{1,0:T(8,128)S(1)} custom-call(bf16[512,1024]{1,0:T(8,128)(2,1)S(1)} %copy-done, bf16[512,1024]{1,0:T(8,128)(2,1)S(1)} %copy-done, bf16[512,1024]{1,0:T(8,128)(2,1)S(1)} %collective-permute-done.2.refs_1_, bf16[512,1024]{1,0:T(8,128)(2,1)S(1)} %collective-permute-done.3.refs_2_, ...), custom_call_target="tpu_custom_call" | custom-call | flops 2147483648 | bytes 5242880 | tf_op jit(solution)/shard_map/pallas_call | solution.py:36
  35.2 3.6 %collective-permute-start.7 = (f32[4,1152]{1,0:T(4,128)S(1)}, f32[4,1152]{1,0:T(4,128)S(1)}, u32[]{:S(2)}, u32[]{:S(2)}) collective-permute-start(f32[4,1152]{1,0:T(4,128)S(1)} %shard_map.65), channel_id=1, source_target_pairs={{0,12},{1,13},{2,14},{3,15},{4,8},{5,9},{6,10},{7,11},{8,0},{9,1},... | collective-permute-start | bytes 55304 | tf_op jit(solution)/shard_map/ppermute | solution.py:225
  38.8 0.9 %collective-permute-start.5 = (f32[4,1152]{1,0:T(4,128)S(1)}, f32[4,1152]{1,0:T(4,128)S(1)}, u32[]{:S(2)}, u32[]{:S(2)}) collective-permute-start(f32[4,1152]{1,0:T(4,128)S(1)} %shard_map.65), channel_id=1, source_target_pairs={{0,8},{1,9},{2,10},{3,11},{4,12},{5,13},{6,14},{7,15},{8,4},{9,5},... | collective-permute-start | bytes 55304 | tf_op jit(solution)/shard_map/ppermute | solution.py:225
  39.7 13.3 %collective-permute-done.8.moving = bf16[512,1024]{1,0:T(8,128)(2,1)} collective-permute-done((bf16[512,1024]{1,0:T(8,128)(2,1)}, bf16[512,1024]{1,0:T(8,128)(2,1)}, u32[]{:S(2)}, u32[]{:S(2)}) %collective-permute-start.8) | collective-permute-done | bytes 1048608 | tf_op jit(solution)/shard_map/ppermute | solution.py:225
  53.1 3.6 %shard_map.66.refs_1_ = f32[512,2048]{1,0:T(8,128)S(1)} custom-call(bf16[512,1024]{1,0:T(8,128)(2,1)} %collective-permute-done.8.moving, bf16[512,1024]{1,0:T(8,128)(2,1)S(1)} %copy-done, bf16[512,1024]{1,0:T(8,128)(2,1)S(1)} %collective-permute-done.2.refs_1_, bf16[512,1024]{1,0:T(8,128)(2,1)S(1)} %collective-permute-done.3.refs_2_, ...), custom_call_target="tpu_custom_call" | custom-call | flops 2147483648 | bytes 5242880 | tf_op jit(solution)/shard_map/pallas_call | solution.py:36
  56.7 3.6 %shard_map.67.refs_2_ = f32[512,2048]{1,0:T(8,128)S(1)} custom-call(bf16[512,1024]{1,0:T(8,128)(2,1)} %collective-permute-done.9.moving, bf16[512,1024]{1,0:T(8,128)(2,1)S(1)} %copy-done, bf16[512,1024]{1,0:T(8,128)(2,1)S(1)} %collective-permute-done.2.refs_1_, bf16[512,1024]{1,0:T(8,128)(2,1)S(1)} %collective-permute-done.3.refs_2_, ...), custom_call_target="tpu_custom_call" | custom-call | flops 2147483648 | bytes 5242880 | tf_op jit(solution)/shard_map/pallas_call | solution.py:36
  60.3 3.0 %shard_map.68 = (f32[1,512]{1,0:T(1,128)S(1)}, f32[1,512]{1,0:T(1,128)S(1)}, f32[1,512]{1,0:T(1,128)S(1)}, f32[1,512]{1,0:T(1,128)S(1)}, f32[1,512]{1,0:T(1,128)S(1)}) custom-call(s32[16,1]{1,0:T(8,128)S(1)} %fusion.1.device, f32[16,1152]{1,0:T(8,128)S(1)} %pad_maximum_fusion.everyone, f32[512,2048]{1,0:T(8,128)S(1)} %shard_map.64.refs_3_.refs_0_, ...), custom_call_target="tpu_custom_call" | custom-call | flops 25165824 | bytes 12582912 | tf_op jit(solution)/shard_map/pallas_call | solution.py:146
  63.5 1.5 %collective-permute-start.12 = (f32[1,512]{1,0:T(1,128)S(1)}, f32[1,512]{1,0:T(1,128)S(1)}, u32[]{:S(2)}, u32[]{:S(2)}) collective-permute-start(f32[1,512]{1,0:T(1,128)S(1)} %get-tuple-element.21), channel_id=1, source_target_pairs={{0,2},{1,3},{2,0},{3,1},{4,6},{5,7},{6,4},{7,5},{8,10},{9,11},{10,... | collective-permute-start | bytes 6152 | tf_op jit(solution)/shard_map/ppermute | solution.py:225
  65.0 0.3 collective-permute-start.13
  65.3 2.5 %collective-permute-done.10 = f32[1,512]{1,0:T(1,128)S(1)} collective-permute-done((f32[1,512]{1,0:T(1,128)S(1)}, f32[1,512]{1,0:T(1,128)S(1)}, u32[]{:S(2)}, u32[]{:S(2)}) %collective-permute-start.10) | collective-permute-done | bytes 2080 | tf_op jit(solution)/shard_map/ppermute | solution.py:225
  67.9 0.6 maximum_maximum_fusion
  (25 shorter events, 0.4 us)
Async XLA Ops:
  0.0 26.3 %collective-permute-start.3 = (bf16[512,1024]{1,0:T(8,128)(2,1)}, bf16[512,1024]{1,0:T(8,128)(2,1)S(1)}, u32[]{:S(2)}, u32[]{:S(2)}) collective-permute-start(bf16[512,1024]{1,0:T(8,128)(2,1)} %refs_0_.5), channel_id=1, source_target_pairs={{0,2},{1,3},{2,0},{3,1},{4,6},{5,7},{6,4},{7,5},{8,10},{9,11},{10,... | collective-permute-start | bytes 3145736 | tf_op jit(solution)/shard_map/ppermute | solution.py:225
  3.0 53.7 %collective-permute-start.9 = (bf16[512,1024]{1,0:T(8,128)(2,1)}, bf16[512,1024]{1,0:T(8,128)(2,1)}, u32[]{:S(2)}, u32[]{:S(2)}) collective-permute-start(bf16[512,1024]{1,0:T(8,128)(2,1)} %refs_0_.5), channel_id=1, source_target_pairs={{0,8},{1,9},{2,10},{3,11},{4,12},{5,13},{6,14},{7,15},{8,4},{9,5},... | collective-permute-start | bytes 3145736 | tf_op jit(solution)/shard_map/ppermute | solution.py:225
  5.6 47.5 %collective-permute-start.8 = (bf16[512,1024]{1,0:T(8,128)(2,1)}, bf16[512,1024]{1,0:T(8,128)(2,1)}, u32[]{:S(2)}, u32[]{:S(2)}) collective-permute-start(bf16[512,1024]{1,0:T(8,128)(2,1)} %refs_0_.5), channel_id=1, source_target_pairs={{0,4},{1,5},{2,6},{3,7},{4,0},{5,1},{6,2},{7,3},{8,12},{9,13},{10,... | collective-permute-start | bytes 3145736 | tf_op jit(solution)/shard_map/ppermute | solution.py:225
  7.1 24.4 %collective-permute-start.2 = (bf16[512,1024]{1,0:T(8,128)(2,1)}, bf16[512,1024]{1,0:T(8,128)(2,1)S(1)}, u32[]{:S(2)}, u32[]{:S(2)}) collective-permute-start(bf16[512,1024]{1,0:T(8,128)(2,1)} %refs_0_.5), channel_id=1, source_target_pairs={{0,1},{1,0},{2,3},{3,2},{4,5},{5,4},{6,7},{7,6},{8,9},{9,8},{10,11... | collective-permute-start | bytes 3145736 | tf_op jit(solution)/shard_map/ppermute | solution.py:225
  26.3 5.2 %collective-permute-start.4 = (bf16[512,1024]{1,0:T(8,128)(2,1)S(1)}, bf16[512,1024]{1,0:T(8,128)(2,1)S(1)}, u32[]{:S(2)}, u32[]{:S(2)}) collective-permute-start(bf16[512,1024]{1,0:T(8,128)(2,1)S(1)} %collective-permute-done.3.refs_2_), channel_id=1, source_target_pairs={{0,1},{1,0},{2,3},{3,2},{4,5},{5,4},{6,7},{7,6},{8,9},{9,8},{10,11... | collective-permute-start | bytes 3145736 | tf_op jit(solution)/shard_map/ppermute | solution.py:225
  26.4 3.4 %collective-permute-start = (f32[1,1152]{1,0:T(1,128)S(1)}, f32[1,1152]{1,0:T(1,128)S(1)}, u32[]{:S(2)}, u32[]{:S(2)}) collective-permute-start(f32[1,1152]{1,0:T(1,128)S(1)} %broadcast_in_dim.25.refs_0_), channel_id=1, source_target_pairs={{0,1},{1,0},{2,3},{3,2},{4,5},{5,4},{6,7},{7,6},{8,9},{9,8},{10,11... | collective-permute-start | bytes 13832 | tf_op jit(solution)/shard_map/ppermute | solution.py:225
  29.7 5.4 %collective-permute-start.1 = (f32[2,1152]{1,0:T(2,128)S(1)}, f32[2,1152]{1,0:T(2,128)S(1)}, u32[]{:S(2)}, u32[]{:S(2)}) collective-permute-start(f32[2,1152]{1,0:T(2,128)S(1)} %pad_maximum_fusion.1), channel_id=1, source_target_pairs={{0,2},{1,3},{2,0},{3,1},{4,6},{5,7},{6,4},{7,5},{8,10},{9,11},{10,... | collective-permute-start | bytes 27656 | tf_op jit(solution)/shard_map/ppermute | solution.py:225
  31.6 1.2 %copy-start = (bf16[512,1024]{1,0:T(8,128)(2,1)S(1)}, bf16[512,1024]{1,0:T(8,128)(2,1)}, u32[]{:S(2)}) copy-start(bf16[512,1024]{1,0:T(8,128)(2,1)} %refs_0_.5) | copy-start | bytes 3145732
  35.2 25.1 %collective-permute-start.7 = (f32[4,1152]{1,0:T(4,128)S(1)}, f32[4,1152]{1,0:T(4,128)S(1)}, u32[]{:S(2)}, u32[]{:S(2)}) collective-permute-start(f32[4,1152]{1,0:T(4,128)S(1)} %shard_map.65), channel_id=1, source_target_pairs={{0,12},{1,13},{2,14},{3,15},{4,8},{5,9},{6,10},{7,11},{8,0},{9,1},... | collective-permute-start | bytes 55304 | tf_op jit(solution)/shard_map/ppermute | solution.py:225
  38.8 21.4 %collective-permute-start.6 = (f32[4,1152]{1,0:T(4,128)S(1)}, f32[4,1152]{1,0:T(4,128)S(1)}, u32[]{:S(2)}, u32[]{:S(2)}) collective-permute-start(f32[4,1152]{1,0:T(4,128)S(1)} %shard_map.65), channel_id=1, source_target_pairs={{0,4},{1,5},{2,6},{3,7},{4,0},{5,1},{6,2},{7,3},{8,12},{9,13},{10,... | collective-permute-start | bytes 55304 | tf_op jit(solution)/shard_map/ppermute | solution.py:225
  38.8 21.5 %collective-permute-start.5 = (f32[4,1152]{1,0:T(4,128)S(1)}, f32[4,1152]{1,0:T(4,128)S(1)}, u32[]{:S(2)}, u32[]{:S(2)}) collective-permute-start(f32[4,1152]{1,0:T(4,128)S(1)} %shard_map.65), channel_id=1, source_target_pairs={{0,8},{1,9},{2,10},{3,11},{4,12},{5,13},{6,14},{7,15},{8,4},{9,5},... | collective-permute-start | bytes 55304 | tf_op jit(solution)/shard_map/ppermute | solution.py:225
  63.3 4.5 %collective-permute-start.10 = (f32[1,512]{1,0:T(1,128)S(1)}, f32[1,512]{1,0:T(1,128)S(1)}, u32[]{:S(2)}, u32[]{:S(2)}) collective-permute-start(f32[1,512]{1,0:T(1,128)S(1)} %get-tuple-element.19), channel_id=1, source_target_pairs={{0,12},{1,13},{2,14},{3,15},{4,8},{5,9},{6,10},{7,11},{8,0},{9,1},... | collective-permute-start | bytes 6152 | tf_op jit(solution)/shard_map/ppermute | solution.py:225
  63.4 4.5 %collective-permute-start.11 = (f32[1,512]{1,0:T(1,128)S(1)}, f32[1,512]{1,0:T(1,128)S(1)}, u32[]{:S(2)}, u32[]{:S(2)}) collective-permute-start(f32[1,512]{1,0:T(1,128)S(1)} %get-tuple-element.20), channel_id=1, source_target_pairs={{0,3},{1,2},{2,1},{3,0},{4,7},{5,6},{6,5},{7,4},{8,11},{9,10},{10,... | collective-permute-start | bytes 6152 | tf_op jit(solution)/shard_map/ppermute | solution.py:225
  63.5 4.4 %collective-permute-start.12 = (f32[1,512]{1,0:T(1,128)S(1)}, f32[1,512]{1,0:T(1,128)S(1)}, u32[]{:S(2)}, u32[]{:S(2)}) collective-permute-start(f32[1,512]{1,0:T(1,128)S(1)} %get-tuple-element.21), channel_id=1, source_target_pairs={{0,2},{1,3},{2,0},{3,1},{4,6},{5,7},{6,4},{7,5},{8,10},{9,11},{10,... | collective-permute-start | bytes 6152 | tf_op jit(solution)/shard_map/ppermute | solution.py:225
  65.0 2.9 %collective-permute-start.13 = (f32[1,512]{1,0:T(1,128)S(1)}, f32[1,512]{1,0:T(1,128)S(1)}, u32[]{:S(2)}, u32[]{:S(2)}) collective-permute-start(f32[1,512]{1,0:T(1,128)S(1)} %get-tuple-element.22), channel_id=1, source_target_pairs={{0,1},{1,0},{2,3},{3,2},{4,5},{5,4},{6,7},{7,6},{8,9},{9,8},{10,11... | collective-permute-start | bytes 6152 | tf_op jit(solution)/shard_map/ppermute | solution.py:225

commit v3 on v2

v3 whole, which is shorter than its diff:
```python
import functools

import jax
import jax.numpy as jnp
from jax import lax
from jax.experimental import pallas as pl
from jax.experimental.pallas import tpu as pltpu
from jax.sharding import PartitionSpec as P

LOWEST = float("-inf")
WORD = 16
LANES = 128
SUBLANES = 8
STRIP = 64
VMEM_SPARE = 4 * 2**20


def gather_kernel(count, *refs):
    blocks, out, plane, arrived = refs[:count], refs[count], refs[count + 1], refs[count + 2]
    rows = blocks[0].shape[0]
    copies = [
        pltpu.make_async_copy(block, plane.at[j * rows : (j + 1) * rows, :], arrived.at[j])
        for j, block in enumerate(blocks)
    ]
    for copy in copies:
        copy.start()
    for copy in copies:
        copy.wait()
    times_plane(plane.at[:rows, :], plane, out)


def times_plane(moving, plane, out):
    chunk = min(256, moving.shape[0])
    for first in range(0, plane.shape[0], chunk):
        out[:, first : first + chunk] = lax.dot_general(
            moving[...],
            plane[first : first + chunk, :],
            (((1,), (1,)), ((), ())),
            preferred_element_type=jnp.float32,
        )


def cost_of(rows, width, others):
    return pl.CostEstimate(
        flops=2 * rows * others * width, bytes_accessed=2 * (rows + others) * width, transcendentals=0
    )


def gathered_plane(blocks):
    rows, width = blocks[0].shape
    others = rows * len(blocks)
    vmem = pl.BlockSpec(memory_space=pltpu.VMEM)
    return pl.pallas_call(
        functools.partial(gather_kernel, len(blocks)),
        out_shape=[
            jax.ShapeDtypeStruct((rows, others), jnp.float32),
            jax.ShapeDtypeStruct((others, width), blocks[0].dtype),
        ],
        in_specs=[pl.BlockSpec(memory_space=pl.ANY)] * len(blocks),
        out_specs=[vmem, vmem],
        scratch_shapes=[pltpu.SemaphoreType.DMA((len(blocks),))],
        compiler_params=pltpu.CompilerParams(vmem_limit_bytes=4 * rows * others + 2 * others * width + VMEM_SPARE),
        cost_estimate=cost_of(rows, width, others),
    )(*blocks)


def products(moving, plane):
    rows, width = moving.shape
    others = plane.shape[0]
    vmem = pl.BlockSpec(memory_space=pltpu.VMEM)
    return pl.pallas_call(
        times_plane,
        out_shape=jax.ShapeDtypeStruct((rows, others), jnp.float32),
        in_specs=[vmem, vmem],
        out_specs=vmem,
        compiler_params=pltpu.CompilerParams(
            vmem_limit_bytes=4 * rows * others + 2 * (rows + others) * width + VMEM_SPARE
        ),
        cost_estimate=cost_of(rows, width, others),
    )(moving, plane)


def maxima_kernel(partners, count, two_sided, device, everyone, moving, plane, *refs):
    tiles = 1 + len(two_sided)
    given = dict(zip([0, *range(2, tiles)], refs))
    row_outs = refs[len(given) : len(given) + count]
    column_outs = list(refs[len(given) + count : -2])
    fresh, column_best = refs[-2:]
    rows = moving.shape[0]
    strip = min(STRIP, rows)
    per_block = rows // LANES
    chunk = fresh.shape[2]
    per_chunk = chunk // LANES
    chunks = plane.shape[0] // chunk
    shards = everyone.shape[0]
    words = -(-shards // WORD)
    source = device[...]
    table = pair_words(everyone[:, 2 * rows :], source, partners, words)

    def scale_of(at):
        return everyone[at : at + 1, 0:rows]

    def cluster_of(at):
        return everyone[at : at + 1, rows : 2 * rows].astype(jnp.int32)

    def bits_of(at):
        named = cluster_of(at) == source
        return [jnp.sum(jnp.where(named, t, 0.0), axis=0, keepdims=True).astype(jnp.int32) for t in table]

    def ones_of(at):
        named = cluster_of(at)
        return [jnp.where(named // WORD == w, jnp.int32(1) << (named % WORD), 0) for w in range(words)]

    def along_sublanes(value):
        return jnp.transpose(jnp.broadcast_to(value, (LANES, rows)))

    lane_scale = [scale_of(j) for j in range(count)]
    lane_ones = [ones_of(j) for j in range(count)]
    scale_down = [along_sublanes(scale_of(r * count)) for r in range(tiles)]
    bits_down = [[along_sublanes(b) for b in bits_of(r * count)] for r in range(tiles)]

    def lanes_of(per, g):
        first = g % per_block * LANES
        return per[g // per_block][:, first : first + LANES]

    row_part = {}

    def passed(r, c):
        wants_row = r > 0
        wants_column = r == 0 or two_sided[r - 1]
        for first in range(0, rows, strip):
            here = slice(first, first + strip)
            best = None
            for at in range(per_chunk):
                g = c * per_chunk + at
                if r in given:
                    value = given[r][here, g * LANES : (g + 1) * LANES]
                else:
                    value = fresh[c % 2, here, at * LANES : (at + 1) * LANES]
                met = bits_down[r][0][here] & lanes_of([o[0] for o in lane_ones], g)
                for w in range(1, words):
                    met = met | (bits_down[r][w][here] & lanes_of([o[w] for o in lane_ones], g))
                keep = met != 0
                if r == 0 and g < per_block and g * LANES < first + strip and first < (g + 1) * LANES:
                    down = lax.broadcasted_iota(jnp.int32, value.shape, 0) + first
                    across = lax.broadcasted_iota(jnp.int32, value.shape, 1) + g * LANES
                    keep = keep & (down != across)
                if wants_row:
                    value = jnp.where(keep, value * scale_down[r][here], LOWEST)
                    part = jnp.max(value.reshape(strip // SUBLANES, SUBLANES, LANES), axis=0)
                    row_part[g] = jnp.maximum(row_part[g], part) if g in row_part else part
                    if wants_column:
                        value = value * lanes_of(lane_scale, g)
                else:
                    value = jnp.where(keep, value * lanes_of(lane_scale, g), LOWEST)
                if wants_column:
                    best = value if best is None else jnp.maximum(best, value)
            if wants_column:
                column_best[r, here, :] = best if c == 0 else jnp.maximum(column_best[r, here, :], best)

    for c in range(chunks + 1):
        if c < chunks:
            fresh[c % 2] = lax.dot_general(
                moving[...],
                plane[c * chunk : (c + 1) * chunk, :],
                (((1,), (1,)), ((), ())),
                preferred_element_type=jnp.float32,
            )
            for r in given:
                passed(r, c)
        if c > 0:
            passed(1, c - 1)

    def column_of(r):
        return jnp.max(jnp.transpose(column_best[r]), axis=0, keepdims=True)

    for r in range(1, tiles):
        if two_sided[r - 1]:
            column_outs.pop(0)[...] = column_of(r)
    own_best = column_of(0) * scale_of(0)
    for j in range(count):
        for at in range(per_block):
            here = slice(at * LANES, (at + 1) * LANES)
            found = jnp.max(row_part[j * per_block + at], axis=0, keepdims=True) * lane_scale[j][:, here]
            if j == 0:
                found = jnp.maximum(found, own_best[:, here])
            row_outs[j][:, here] = found


def maxima(device, everyone, partners, moving, plane, given, two_sided):
    rows, width = moving.shape
    count = plane.shape[0] // rows
    chunk = min(256, rows)
    vmem = pl.BlockSpec(memory_space=pltpu.VMEM)
    outs = count + sum(two_sided)
    return pl.pallas_call(
        functools.partial(maxima_kernel, partners, count, tuple(two_sided)),
        out_shape=[jax.ShapeDtypeStruct((1, rows), jnp.float32)] * outs,
        in_specs=[vmem] * (4 + len(given)),
        out_specs=[vmem] * outs,
        scratch_shapes=[
            pltpu.VMEM((2, rows, chunk), jnp.float32),
            pltpu.VMEM((1 + len(two_sided), rows, LANES), jnp.float32),
        ],
        compiler_params=pltpu.CompilerParams(
            vmem_limit_bytes=4 * rows * plane.shape[0] * len(given)
            + 2 * width * (plane.shape[0] + rows)
            + 2 * VMEM_SPARE
        ),
        cost_estimate=cost_of(rows, width, plane.shape[0]),
    )(device, everyone, moving, plane, *given)


def pair_words(listed, source, partners, words):
    shards = listed.shape[0]
    lane = lax.broadcasted_iota(jnp.int32, listed.shape, 1)
    target = source + lane + 1
    used = (lane < partners) & (target < shards) & (listed == 1.0)

    def weight(which, w):
        return jnp.where(which // WORD == w, jnp.int32(1) << (which % WORD), 0).astype(jnp.float32)

    table = []
    for w in range(words):
        met = jnp.where(used, weight(target, w), 0.0) + jnp.where(lane == 0, weight(source, w), 0.0)
        met = jnp.sum(met, axis=1, keepdims=True)
        behind = jnp.where(used, weight(source, w), 0.0)
        for i in range(shards):
            hit = jnp.where(target == source[i : i + 1, :], behind, 0.0)
            here = jnp.sum(jnp.sum(hit, axis=0, keepdims=True), axis=1, keepdims=True)
            met = met + jnp.where(lax.broadcasted_iota(jnp.int32, met.shape, 0) == i, here, 0.0)
        table.append(met)
    return table


def joined_kernel(*refs):
    pieces, out = refs[:-2], refs[-1]
    at = 0
    for piece in pieces:
        out[at : at + piece.shape[0], :] = piece[...]
        at += piece.shape[0]


def joined(pieces, after):
    vmem = pl.BlockSpec(memory_space=pltpu.VMEM)
    return pl.pallas_call(
        joined_kernel,
        out_shape=jax.ShapeDtypeStruct((sum(p.shape[0] for p in pieces), pieces[0].shape[1]), jnp.float32),
        in_specs=[vmem] * len(pieces) + [pl.BlockSpec(memory_space=pl.ANY)],
        out_specs=vmem,
        compiler_params=pltpu.CompilerParams(vmem_limit_bytes=2**20),
    )(*pieces, after)


def device_table(shards, plane, planes, order, place_of, here):
    rel = jnp.arange(shards, dtype=jnp.int32)
    place = jnp.sum(jnp.where(jnp.arange(planes) == here // plane, jnp.asarray(place_of, jnp.int32), 0))
    place = (place - rel // plane) % planes
    z = jnp.sum(jnp.where(place[:, None] == jnp.arange(planes)[None, :], jnp.asarray(order, jnp.int32)[None, :], 0), axis=1)
    return (z * plane + (here % plane ^ rel % plane)).reshape(shards, 1)


def per_device(embeddings, scales, cluster, pair_listed):
    rows, width = embeddings.shape
    shards = lax.axis_size("shard")
    here = lax.axis_index("shard")
    plane = 1
    while plane * plane * 4 <= shards:
        plane *= 2
    planes = shards // plane
    half = planes // 2
    owned, partners = pair_listed.shape

    order = [place // 2 + (place % 2) * half for place in range(planes)]
    place_of = [order.index(z) for z in range(planes)]

    def permuted(value, target):
        return lax.ppermute(value, "shard", [(s, target(s)) for s in range(shards)])

    def across(bit):
        return lambda s: s ^ bit

    def along(distance):
        def target(s):
            z = order[(place_of[s // plane] + distance) % planes]
            return z * plane + s % plane

        return target

    arrived = {}
    for distance in range(1, half + 1):
        arrived[distance] = permuted(embeddings, along(distance))
    held = {0: embeddings}
    bit = plane // 2
    while bit:
        for j in sorted(held):
            held[j | bit] = permuted(held[j], across(bit))
        bit //= 2
    blocks = [held[j] for j in range(plane)]

    pairs = jnp.pad(pair_listed.reshape(-1).astype(jnp.float32), (0, -(owned * partners) % LANES))
    told = jnp.concatenate([scales.astype(jnp.float32), cluster[:, 0].astype(jnp.float32), pairs])[None, :]
    pieces, bit = [told], 1
    while bit < plane:
        mine = pieces[0] if len(pieces) == 1 else jnp.concatenate(pieces, axis=0)
        pieces.append(permuted(mine, across(bit)))
        bit *= 2
    raw, whole = gathered_plane(blocks)
    told = joined(pieces, raw)
    everyone = jnp.concatenate([told] + [permuted(told, along(t)) for t in range(1, planes)], axis=0)
    device = device_table(shards, plane, planes, order, place_of, here)
    distances = range(1, half + 1)
    two_sided = [2 * distance != planes for distance in distances]
    given = [raw] + [products(arrived[distance], whole) for distance in distances[1:]]
    found = maxima(device, everyone, partners, arrived[1], whole, given, two_sided)
    gathered, columns = found[:plane], list(found[plane:])

    result = gathered[0]
    returned = []
    for distance in distances:
        if two_sided[distance - 1]:
            returned.append(permuted(columns.pop(0), along(-distance)))
    returned += [permuted(gathered[j], across(j)) for j in range(plane - 1, 0, -1)]
    return functools.reduce(jnp.maximum, returned, result).reshape(rows)


def solution(mesh):
    placed = (
        P(("groups", "shard"), None),
        P(("groups", "shard")),
        P(("groups", "shard"), None),
        P(("groups", "shard"), None),
    )
    return jax.shard_map(
        per_device, mesh=mesh, in_specs=placed, out_specs=P(("groups", "shard")), check_vma=False
    )
```

time: 68.8 us -> 66.2 us (0.962)
  waiting for transfers between devices: 33.1 us -> 30.1 us
  starting transfers between devices: 16 us -> 18.3 us
  Pallas kernels: 12.6 us -> 10.7 us
    ppermute x14, waiting for transfers between devices: 33.1 us -> 30.1 us  [permuted(): return lax.ppermute(value, 'shard', [(s, target(s)) for s in range(shards)])]
    ppermute x14, starting transfers between devices: 16 us -> 18.3 us  [permuted(): return lax.ppermute(value, 'shard', [(s, target(s)) for s in range(shards)])]
    pallas_call x4 -> x3, Pallas kernels: 12.6 us -> 10.7 us  [the longest x1 4.27 us: maxima(): pl.pallas_call(functools.partial(maxima_kernel, partners, count, tuple(tw...]
  transfers between devices with their start and end apart: 14 -> 14, of which waited for: 3 -> 6; matrix products, arithmetic and copies ran while one was open for 7% -> 7% of each run, Pallas kernels for 14% -> 10%
where the time goes in v3:
time: 66.2 us; the launch traced here: 65.9 us
  waiting for transfers between devices  30.1 us (45%)
  starting transfers between devices  18.3 us (28%)
  Pallas kernels  10.7 us (16%)
  other arithmetic  5.36 us (8%)
  local copies, waits for them, and re-layouts  1.32 us (2%)
    ppermute x14, waiting for transfers between devices, permuted(): return lax.ppermute(value, 'shard', [(s, target(s)) for s in range(shards)])  30.1 us
    ppermute x14, starting transfers between devices, permuted(): return lax.ppermute(value, 'shard', [(s, target(s)) for s in range(shards)])  18.3 us
    pallas_call x1, Pallas kernels, maxima(): pl.pallas_call(functools.partial(maxima_kernel, partners, count, tuple(tw...  4.27 us
    pallas_call x1, Pallas kernels, gathered_plane(): pl.pallas_call(functools.partial(gather_kernel, len(blocks)), out_shape=[...  4.03 us
    pallas_call x1, Pallas kernels, products(): pl.pallas_call(times_plane, out_shape=jax.ShapeDtypeStruct((rows, others)...  2.37 us
  transfers between devices with their start and end apart: 14, of which 6 were waited for; matrix products, arithmetic and copies ran while one was open for 7% of the time, Pallas kernels for 10%

profile of v3, /device:TPU:0, one launch (start us, length us, event | category | flops | bytes accessed | tf_op | source)
XLA Modules:
  0.0 65.9 jit_solution(1802617195105564421)
XLA Ops:
  0.0 3.0 %collective-permute-start.3 = (bf16[512,1024]{1,0:T(8,128)(2,1)}, bf16[512,1024]{1,0:T(8,128)(2,1)S(1)}, u32[]{:S(2)}, u32[]{:S(2)}) collective-permute-start(bf16[512,1024]{1,0:T(8,128)(2,1)} %refs_0_.1), channel_id=1, source_target_pairs={{0,2},{1,3},{2,0},{3,1},{4,6},{5,7},{6,4},{7,5},{8,10},{9,11},{10,... | collective-permute-start | bytes 3145736 | tf_op jit(solution)/shard_map/ppermute | solution.py:278
  3.0 1.6 %collective-permute-start.9 = (bf16[512,1024]{1,0:T(8,128)(2,1)}, bf16[512,1024]{1,0:T(8,128)(2,1)S(1)}, u32[]{:S(2)}, u32[]{:S(2)}) collective-permute-start(bf16[512,1024]{1,0:T(8,128)(2,1)} %refs_0_.1), channel_id=1, source_target_pairs={{0,4},{1,5},{2,6},{3,7},{4,0},{5,1},{6,2},{7,3},{8,12},{9,13},{10,... | collective-permute-start | bytes 3145736 | tf_op jit(solution)/shard_map/ppermute | solution.py:278
  4.5 2.6 %collective-permute-start.8 = (bf16[512,1024]{1,0:T(8,128)(2,1)}, bf16[512,1024]{1,0:T(8,128)(2,1)S(1)}, u32[]{:S(2)}, u32[]{:S(2)}) collective-permute-start(bf16[512,1024]{1,0:T(8,128)(2,1)} %refs_0_.1), channel_id=1, source_target_pairs={{0,8},{1,9},{2,10},{3,11},{4,12},{5,13},{6,14},{7,15},{8,4},{9,5},... | collective-permute-start | bytes 3145736 | tf_op jit(solution)/shard_map/ppermute | solution.py:278
  7.1 0.7 %convert_element_type.18 = f32[512,1]{0,1:T(1,128)S(1)} convert(s32[512,1]{0,1:T(1,128)} %param.8) | non-fusion elementwise | flops 512 | bytes 4096 | tf_op jit(solution)/shard_map/convert_element_type | solution.py:302
  7.8 0.7 %convert_element_type.17 = f32[512]{0:T(512)S(1)} convert(bf16[512]{0:T(512)(128)(2,1)} %param.7) | non-fusion elementwise | flops 512 | bytes 3072 | tf_op jit(solution)/shard_map/convert_element_type | solution.py:302
  8.5 0.7 convert_bitcast_fusion
  9.2 17.2 %collective-permute-done.3.refs_2_ = bf16[512,1024]{1,0:T(8,128)(2,1)S(1)} collective-permute-done((bf16[512,1024]{1,0:T(8,128)(2,1)}, bf16[512,1024]{1,0:T(8,128)(2,1)S(1)}, u32[]{:S(2)}, u32[]{:S(2)}) %collective-permute-start.3) | collective-permute-done | bytes 1048608 | tf_op jit(solution)/shard_map/ppermute | solution.py:278
  26.9 1.3 %fusion.6 = s32[]{:T(128)} fusion(s32[4]{0:T(128)} %constant.61.clone, s32[]{:T(128)S(6)} %select_n.49), kind=kLoop, calls=%fused_computation.23 | loop fusion | flops 11 | bytes 24 | tf_op jit(solution)/shard_map/reduce_sum | solution.py:257
  28.2 0.7 and_select_fusion
  28.9 0.7 %select_reduce_fusion = s32[16]{0:T(128)S(1)} fusion(s32[4]{0:T(128)} %constant.61.clone, s32[16]{0:T(128)S(1)} %and_select_fusion), kind=kLoop, calls=%fused_computation.14 | loop fusion | flops 176 | bytes 144 | tf_op jit(solution)/shard_map/reduce_sum | solution.py:259
  29.7 1.8 %collective-permute-start.1 = (f32[2,1152]{1,0:T(2,128)S(1)}, f32[2,1152]{1,0:T(2,128)S(1)}, u32[]{:S(2)}, u32[]{:S(2)}) collective-permute-start(f32[2,1152]{1,0:T(2,128)S(1)} %pad_maximum_fusion.1), channel_id=1, source_target_pairs={{0,2},{1,3},{2,0},{3,1},{4,6},{5,7},{6,4},{7,5},{8,10},{9,11},{10,... | collective-permute-start | bytes 27656 | tf_op jit(solution)/shard_map/ppermute | solution.py:278
  31.6 1.2 %copy-done = bf16[512,1024]{1,0:T(8,128)(2,1)S(1)} copy-done((bf16[512,1024]{1,0:T(8,128)(2,1)S(1)}, bf16[512,1024]{1,0:T(8,128)(2,1)}, u32[]{:S(2)}) %copy-start) | copy-done | bytes 1048600
  32.8 4.0 %shard_map.64 = (f32[512,2048]{1,0:T(8,128)S(1)}, bf16[2048,1024]{1,0:T(8,128)(2,1)S(1)}) custom-call(bf16[512,1024]{1,0:T(8,128)(2,1)S(1)} %copy-done, bf16[512,1024]{1,0:T(8,128)(2,1)} %collective-permute-done.2.refs_1_, bf16[512,1024]{1,0:T(8,128)(2,1)S(1)} %collective-permute-done.3.refs_2_, bf16[512,1024]{1,0:T(8,128)(2,1)} %collective-permute-done.4.refs_3_), custom_call_target="tpu_custom_call" | custom-call | flops 2147483648 | bytes 5242880 | tf_op jit(solution)/shard_map/pallas_call | solution.py:53
  36.9 2.6 %collective-permute-start.5 = (f32[4,1152]{1,0:T(4,128)S(1)}, f32[4,1152]{1,0:T(4,128)S(1)}, u32[]{:S(2)}, u32[]{:S(2)}) collective-permute-start(f32[4,1152]{1,0:T(4,128)S(1)} %shard_map.65), channel_id=1, source_target_pairs={{0,8},{1,9},{2,10},{3,11},{4,12},{5,13},{6,14},{7,15},{8,4},{9,5},... | collective-permute-start | bytes 55304 | tf_op jit(solution)/shard_map/ppermute | solution.py:278
  39.5 1.6 %collective-permute-start.6 = (f32[4,1152]{1,0:T(4,128)S(1)}, f32[4,1152]{1,0:T(4,128)S(1)}, u32[]{:S(2)}, u32[]{:S(2)}) collective-permute-start(f32[4,1152]{1,0:T(4,128)S(1)} %shard_map.65), channel_id=1, source_target_pairs={{0,4},{1,5},{2,6},{3,7},{4,0},{5,1},{6,2},{7,3},{8,12},{9,13},{10,... | collective-permute-start | bytes 55304 | tf_op jit(solution)/shard_map/ppermute | solution.py:278
  41.4 2.4 %shard_map.66.refs_1_ = f32[512,2048]{1,0:T(8,128)S(1)} custom-call(bf16[512,1024]{1,0:T(8,128)(2,1)S(1)} %collective-permute-done.9.moving, bf16[2048,1024]{1,0:T(8,128)(2,1)S(1)} %get-tuple-element.13.plane), custom_call_target="tpu_custom_call" | custom-call | flops 2147483648 | bytes 5242880 | tf_op jit(solution)/shard_map/pallas_call | solution.py:71
  43.8 10.4 %collective-permute-done.5 = f32[4,1152]{1,0:T(4,128)S(1)} collective-permute-done((f32[4,1152]{1,0:T(4,128)S(1)}, f32[4,1152]{1,0:T(4,128)S(1)}, u32[]{:S(2)}, u32[]{:S(2)}) %collective-permute-start.5) | collective-permute-done | bytes 18464 | tf_op jit(solution)/shard_map/ppermute | solution.py:278
  54.2 0.8 %collective-permute-done.7 = f32[4,1152]{1,0:T(4,128)S(1)} collective-permute-done((f32[4,1152]{1,0:T(4,128)S(1)}, f32[4,1152]{1,0:T(4,128)S(1)}, u32[]{:S(2)}, u32[]{:S(2)}) %collective-permute-start.7) | collective-permute-done | bytes 18464 | tf_op jit(solution)/shard_map/ppermute | solution.py:278
  55.0 4.3 %shard_map.67 = (f32[1,512]{1,0:T(1,128)S(1)}, f32[1,512]{1,0:T(1,128)S(1)}, f32[1,512]{1,0:T(1,128)S(1)}, f32[1,512]{1,0:T(1,128)S(1)}, f32[1,512]{1,0:T(1,128)S(1)}) custom-call(s32[16,1]{1,0:T(8,128)S(1)} %fusion.1.device, f32[16,1152]{1,0:T(8,128)S(1)} %pad_maximum_fusion.everyone, bf16[512,1024]{1,0:T(8,128)(2,1)S(1)} %collective-permute-done.8.moving, ...), custom_call_target="tpu_custom_call" | custom-call | flops 2147483648 | bytes 5242880 | tf_op jit(solution)/shard_map/pallas_call | solution.py:196
  59.3 2.4 %collective-permute-start.10 = (f32[1,512]{1,0:T(1,128)S(1)}, f32[1,512]{1,0:T(1,128)S(1)}, u32[]{:S(2)}, u32[]{:S(2)}) collective-permute-start(f32[1,512]{1,0:T(1,128)S(1)} %get-tuple-element.15), channel_id=1, source_target_pairs={{0,12},{1,13},{2,14},{3,15},{4,8},{5,9},{6,10},{7,11},{8,0},{9,1},... | collective-permute-start | bytes 6152 | tf_op jit(solution)/shard_map/ppermute | solution.py:278
  62.3 1.3 %collective-permute-start.13 = (f32[1,512]{1,0:T(1,128)S(1)}, f32[1,512]{1,0:T(1,128)S(1)}, u32[]{:S(2)}, u32[]{:S(2)}) collective-permute-start(f32[1,512]{1,0:T(1,128)S(1)} %get-tuple-element.18), channel_id=1, source_target_pairs={{0,1},{1,0},{2,3},{3,2},{4,5},{5,4},{6,7},{7,6},{8,9},{9,8},{10,11... | collective-permute-start | bytes 6152 | tf_op jit(solution)/shard_map/ppermute | solution.py:278
  63.8 0.9 %collective-permute-done.11 = f32[1,512]{1,0:T(1,128)S(1)} collective-permute-done((f32[1,512]{1,0:T(1,128)S(1)}, f32[1,512]{1,0:T(1,128)S(1)}, u32[]{:S(2)}, u32[]{:S(2)}) %collective-permute-start.11) | collective-permute-done | bytes 2080 | tf_op jit(solution)/shard_map/ppermute | solution.py:278
  64.7 0.6 collective-permute-done.12
  65.3 0.6 maximum_maximum_fusion
  (24 shorter events, 1.9 us)
Async XLA Ops:
  0.0 26.3 %collective-permute-start.3 = (bf16[512,1024]{1,0:T(8,128)(2,1)}, bf16[512,1024]{1,0:T(8,128)(2,1)S(1)}, u32[]{:S(2)}, u32[]{:S(2)}) collective-permute-start(bf16[512,1024]{1,0:T(8,128)(2,1)} %refs_0_.1), channel_id=1, source_target_pairs={{0,2},{1,3},{2,0},{3,1},{4,6},{5,7},{6,4},{7,5},{8,10},{9,11},{10,... | collective-permute-start | bytes 3145736 | tf_op jit(solution)/shard_map/ppermute | solution.py:278
  3.0 28.6 %collective-permute-start.2 = (bf16[512,1024]{1,0:T(8,128)(2,1)}, bf16[512,1024]{1,0:T(8,128)(2,1)}, u32[]{:S(2)}, u32[]{:S(2)}) collective-permute-start(bf16[512,1024]{1,0:T(8,128)(2,1)} %refs_0_.1), channel_id=1, source_target_pairs={{0,1},{1,0},{2,3},{3,2},{4,5},{5,4},{6,7},{7,6},{8,9},{9,8},{10,11... | collective-permute-start | bytes 3145736 | tf_op jit(solution)/shard_map/ppermute | solution.py:278
  3.0 38.4 %collective-permute-start.9 = (bf16[512,1024]{1,0:T(8,128)(2,1)}, bf16[512,1024]{1,0:T(8,128)(2,1)S(1)}, u32[]{:S(2)}, u32[]{:S(2)}) collective-permute-start(bf16[512,1024]{1,0:T(8,128)(2,1)} %refs_0_.1), channel_id=1, source_target_pairs={{0,4},{1,5},{2,6},{3,7},{4,0},{5,1},{6,2},{7,3},{8,12},{9,13},{10,... | collective-permute-start | bytes 3145736 | tf_op jit(solution)/shard_map/ppermute | solution.py:278
  4.5 50.4 %collective-permute-start.8 = (bf16[512,1024]{1,0:T(8,128)(2,1)}, bf16[512,1024]{1,0:T(8,128)(2,1)S(1)}, u32[]{:S(2)}, u32[]{:S(2)}) collective-permute-start(bf16[512,1024]{1,0:T(8,128)(2,1)} %refs_0_.1), channel_id=1, source_target_pairs={{0,8},{1,9},{2,10},{3,11},{4,12},{5,13},{6,14},{7,15},{8,4},{9,5},... | collective-permute-start | bytes 3145736 | tf_op jit(solution)/shard_map/ppermute | solution.py:278
  26.3 5.2 %collective-permute-start.4 = (bf16[512,1024]{1,0:T(8,128)(2,1)S(1)}, bf16[512,1024]{1,0:T(8,128)(2,1)}, u32[]{:S(2)}, u32[]{:S(2)}) collective-permute-start(bf16[512,1024]{1,0:T(8,128)(2,1)S(1)} %collective-permute-done.3.refs_2_), channel_id=1, source_target_pairs={{0,1},{1,0},{2,3},{3,2},{4,5},{5,4},{6,7},{7,6},{8,9},{9,8},{10,11... | collective-permute-start | bytes 3145736 | tf_op jit(solution)/shard_map/ppermute | solution.py:278
  26.4 3.4 %collective-permute-start = (f32[1,1152]{1,0:T(1,128)S(1)}, f32[1,1152]{1,0:T(1,128)S(1)}, u32[]{:S(2)}, u32[]{:S(2)}) collective-permute-start(f32[1,1152]{1,0:T(1,128)S(1)} %broadcast_in_dim.25.refs_0_), channel_id=1, source_target_pairs={{0,1},{1,0},{2,3},{3,2},{4,5},{5,4},{6,7},{7,6},{8,9},{9,8},{10,11... | collective-permute-start | bytes 13832 | tf_op jit(solution)/shard_map/ppermute | solution.py:278
  29.7 7.1 %collective-permute-start.1 = (f32[2,1152]{1,0:T(2,128)S(1)}, f32[2,1152]{1,0:T(2,128)S(1)}, u32[]{:S(2)}, u32[]{:S(2)}) collective-permute-start(f32[2,1152]{1,0:T(2,128)S(1)} %pad_maximum_fusion.1), channel_id=1, source_target_pairs={{0,2},{1,3},{2,0},{3,1},{4,6},{5,7},{6,4},{7,5},{8,10},{9,11},{10,... | collective-permute-start | bytes 27656 | tf_op jit(solution)/shard_map/ppermute | solution.py:278
  31.6 1.2 %copy-start = (bf16[512,1024]{1,0:T(8,128)(2,1)S(1)}, bf16[512,1024]{1,0:T(8,128)(2,1)}, u32[]{:S(2)}) copy-start(bf16[512,1024]{1,0:T(8,128)(2,1)} %refs_0_.1) | copy-start | bytes 3145732
  36.9 17.3 %collective-permute-start.5 = (f32[4,1152]{1,0:T(4,128)S(1)}, f32[4,1152]{1,0:T(4,128)S(1)}, u32[]{:S(2)}, u32[]{:S(2)}) collective-permute-start(f32[4,1152]{1,0:T(4,128)S(1)} %shard_map.65), channel_id=1, source_target_pairs={{0,8},{1,9},{2,10},{3,11},{4,12},{5,13},{6,14},{7,15},{8,4},{9,5},... | collective-permute-start | bytes 55304 | tf_op jit(solution)/shard_map/ppermute | solution.py:278
  39.5 14.7 %collective-permute-start.6 = (f32[4,1152]{1,0:T(4,128)S(1)}, f32[4,1152]{1,0:T(4,128)S(1)}, u32[]{:S(2)}, u32[]{:S(2)}) collective-permute-start(f32[4,1152]{1,0:T(4,128)S(1)} %shard_map.65), channel_id=1, source_target_pairs={{0,4},{1,5},{2,6},{3,7},{4,0},{5,1},{6,2},{7,3},{8,12},{9,13},{10,... | collective-permute-start | bytes 55304 | tf_op jit(solution)/shard_map/ppermute | solution.py:278
  41.1 13.9 %collective-permute-start.7 = (f32[4,1152]{1,0:T(4,128)S(1)}, f32[4,1152]{1,0:T(4,128)S(1)}, u32[]{:S(2)}, u32[]{:S(2)}) collective-permute-start(f32[4,1152]{1,0:T(4,128)S(1)} %shard_map.65), channel_id=1, source_target_pairs={{0,12},{1,13},{2,14},{3,15},{4,8},{5,9},{6,10},{7,11},{8,0},{9,1},... | collective-permute-start | bytes 55304 | tf_op jit(solution)/shard_map/ppermute | solution.py:278
  59.3 4.5 %collective-permute-start.10 = (f32[1,512]{1,0:T(1,128)S(1)}, f32[1,512]{1,0:T(1,128)S(1)}, u32[]{:S(2)}, u32[]{:S(2)}) collective-permute-start(f32[1,512]{1,0:T(1,128)S(1)} %get-tuple-element.15), channel_id=1, source_target_pairs={{0,12},{1,13},{2,14},{3,15},{4,8},{5,9},{6,10},{7,11},{8,0},{9,1},... | collective-permute-start | bytes 6152 | tf_op jit(solution)/shard_map/ppermute | solution.py:278
  61.7 3.0 %collective-permute-start.11 = (f32[1,512]{1,0:T(1,128)S(1)}, f32[1,512]{1,0:T(1,128)S(1)}, u32[]{:S(2)}, u32[]{:S(2)}) collective-permute-start(f32[1,512]{1,0:T(1,128)S(1)} %get-tuple-element.16), channel_id=1, source_target_pairs={{0,3},{1,2},{2,1},{3,0},{4,7},{5,6},{6,5},{7,4},{8,11},{9,10},{10,... | collective-permute-start | bytes 6152 | tf_op jit(solution)/shard_map/ppermute | solution.py:278
  61.7 3.6 %collective-permute-start.12 = (f32[1,512]{1,0:T(1,128)S(1)}, f32[1,512]{1,0:T(1,128)S(1)}, u32[]{:S(2)}, u32[]{:S(2)}) collective-permute-start(f32[1,512]{1,0:T(1,128)S(1)} %get-tuple-element.17), channel_id=1, source_target_pairs={{0,2},{1,3},{2,0},{3,1},{4,6},{5,7},{6,4},{7,5},{8,10},{9,11},{10,... | collective-permute-start | bytes 6152 | tf_op jit(solution)/shard_map/ppermute | solution.py:278
  62.3 3.1 %collective-permute-start.13 = (f32[1,512]{1,0:T(1,128)S(1)}, f32[1,512]{1,0:T(1,128)S(1)}, u32[]{:S(2)}, u32[]{:S(2)}) collective-permute-start(f32[1,512]{1,0:T(1,128)S(1)} %get-tuple-element.18), channel_id=1, source_target_pairs={{0,1},{1,0},{2,3},{3,2},{4,5},{5,4},{6,7},{7,6},{8,9},{9,8},{10,11... | collective-permute-start | bytes 6152 | tf_op jit(solution)/shard_map/ppermute | solution.py:278

commit v4 on v3

--- a/solution.py
+++ b/solution.py
@@ -26,10 +26,17 @@
         copy.start()
     for copy in copies:
         copy.wait()
-    times_plane(plane.at[:rows, :], plane, out)
-
-
-def times_plane(moving, plane, out):
+    chunk = min(256, rows)
+    for first in range(0, plane.shape[0], chunk):
+        out[first : first + chunk, :] = lax.dot_general(
+            plane[first : first + chunk, :],
+            plane[:rows, :],
+            (((1,), (1,)), ((), ())),
+            preferred_element_type=jnp.float32,
+        )
+
+
+def product_kernel(moving, plane, after, out):
     chunk = min(256, moving.shape[0])
     for first in range(0, plane.shape[0], chunk):
         out[:, first : first + chunk] = lax.dot_general(
@@ -53,7 +60,7 @@
     return pl.pallas_call(
         functools.partial(gather_kernel, len(blocks)),
         out_shape=[
-            jax.ShapeDtypeStruct((rows, others), jnp.float32),
+            jax.ShapeDtypeStruct((others, rows), jnp.float32),
             jax.ShapeDtypeStruct((others, width), blocks[0].dtype),
         ],
         in_specs=[pl.BlockSpec(memory_space=pl.ANY)] * len(blocks),
@@ -64,25 +71,73 @@
     )(*blocks)
 
 
-def products(moving, plane):
+def products(moving, plane, after):
     rows, width = moving.shape
     others = plane.shape[0]
     vmem = pl.BlockSpec(memory_space=pltpu.VMEM)
     return pl.pallas_call(
-        times_plane,
+        product_kernel,
         out_shape=jax.ShapeDtypeStruct((rows, others), jnp.float32),
-        in_specs=[vmem, vmem],
+        in_specs=[vmem, vmem, pl.BlockSpec(memory_space=pl.ANY)],
         out_specs=vmem,
         compiler_params=pltpu.CompilerParams(
             vmem_limit_bytes=4 * rows * others + 2 * (rows + others) * width + VMEM_SPARE
         ),
         cost_estimate=cost_of(rows, width, others),
-    )(moving, plane)
-
-
-def maxima_kernel(partners, count, two_sided, device, everyone, moving, plane, *refs):
+    )(moving, plane, after)
+
+
+def along_sublanes(value):
+    return jnp.transpose(jnp.broadcast_to(value, (LANES, value.shape[1])))
+
+
+def classes_kernel(told, raw, out, scale_down, cluster_down):
+    count, rows = told.shape[0], raw.shape[1]
+    strip = min(STRIP, rows)
+    for j in range(count):
+        here = slice(j * rows, (j + 1) * rows)
+        scale_down[here, :] = along_sublanes(told[j : j + 1, 0:rows])
+        cluster_down[here, :] = along_sublanes(told[j : j + 1, rows : 2 * rows])
+    subclusters = out.shape[0]
+    for first in range(0, rows, LANES):
+
+        def step(i, best):
+            here = pl.ds(pl.multiple_of(i * strip, strip), strip)
+            down = lax.broadcasted_iota(jnp.int32, (strip, LANES), 0) + i * strip
+            across = lax.broadcasted_iota(jnp.int32, (strip, LANES), 1) + first
+            value = raw[here, first : first + LANES] * scale_down[here, :]
+            value = jnp.where(down == across, LOWEST, value)
+            cluster = cluster_down[here, :]
+            found = []
+            for a in range(subclusters):
+                one = jnp.where(cluster == float(a), value, LOWEST)
+                one = jnp.max(one.reshape(strip // SUBLANES, SUBLANES, LANES), axis=0)
+                found.append(jnp.maximum(best[a], one))
+            return tuple(found)
+
+        start = tuple(jnp.full((SUBLANES, LANES), LOWEST, jnp.float32) for _ in range(subclusters))
+        best = lax.fori_loop(0, raw.shape[0] // strip, step, start)
+        for a in range(subclusters):
+            out[a : a + 1, first : first + LANES] = jnp.max(best[a], axis=0, keepdims=True)
+
+
+def classes(told, raw, subclusters):
+    others, rows = raw.shape
+    vmem = pl.BlockSpec(memory_space=pltpu.VMEM)
+    return pl.pallas_call(
+        classes_kernel,
+        out_shape=jax.ShapeDtypeStruct((subclusters, rows), jnp.float32),
+        in_specs=[vmem, vmem],
+        out_specs=vmem,
+        scratch_shapes=[pltpu.VMEM((others, LANES), jnp.float32)] * 2,
+        compiler_params=pltpu.CompilerParams(vmem_limit_bytes=4 * others * (rows + 2 * LANES) + VMEM_SPARE),
+    )(told, raw)
+
+
+def maxima_kernel(partners, count, others, two_sided, device, told, own_classes, moving, plane, *refs):
     tiles = 1 + len(two_sided)
-    given = dict(zip([0, *range(2, tiles)], refs))
+    distant, refs = refs[:others], refs[others:]
+    given = dict(zip(range(2, tiles), refs))
     row_outs = refs[len(given) : len(given) + count]
     column_outs = list(refs[len(given) + count : -2])
     fresh, column_best = refs[-2:]
@@ -92,32 +147,31 @@
     chunk = fresh.shape[2]
     per_chunk = chunk // LANES
     chunks = plane.shape[0] // chunk
-    shards = everyone.shape[0]
+    shards = device.shape[0]
     words = -(-shards // WORD)
     source = device[...]
-    table = pair_words(everyone[:, 2 * rows :], source, partners, words)
-
-    def scale_of(at):
-        return everyone[at : at + 1, 0:rows]
-
-    def cluster_of(at):
-        return everyone[at : at + 1, rows : 2 * rows].astype(jnp.int32)
-
-    def bits_of(at):
-        named = cluster_of(at) == source
+    pairs = [told[:, 2 * rows :]] + [d[0:count, 2 * LANES :] for d in distant]
+    table = pair_words(jnp.concatenate(pairs, axis=0), source, partners, words)
+
+    def facts_of(r):
+        if r == 0:
+            return told[0:1, 0:rows], told[0:1, rows : 2 * rows]
+        parts = [distant[r - 1][p : p + 1, 0 : 2 * LANES] for p in range(rows // LANES)]
+        return [jnp.concatenate([p[:, at : at + LANES] for p in parts], axis=1) for at in (0, LANES)]
+
+    def bits_of(clusters):
+        named = clusters.astype(jnp.int32) == source
         return [jnp.sum(jnp.where(named, t, 0.0), axis=0, keepdims=True).astype(jnp.int32) for t in table]
 
     def ones_of(at):
-        named = cluster_of(at)
+        named = told[at : at + 1, rows : 2 * rows].astype(jnp.int32)
         return [jnp.where(named // WORD == w, jnp.int32(1) << (named % WORD), 0) for w in range(words)]
 
-    def along_sublanes(value):
-        return jnp.transpose(jnp.broadcast_to(value, (LANES, rows)))
-
-    lane_scale = [scale_of(j) for j in range(count)]
+    lane_scale = [told[j : j + 1, 0:rows] for j in range(count)]
     lane_ones = [ones_of(j) for j in range(count)]
-    scale_down = [along_sublanes(scale_of(r * count)) for r in range(tiles)]
-    bits_down = [[along_sublanes(b) for b in bits_of(r * count)] for r in range(tiles)]
+    facts = [facts_of(r) for r in range(tiles)]
+    scale_down = {r: along_sublanes(facts[r][0]) for r in range(1, tiles)}
+    bits_down = {r: [along_sublanes(b) for b in bits_of(facts[r][1])] for r in range(1, tiles)}
 
     def lanes_of(per, g):
         first = g % per_block * LANES
@@ -126,8 +180,7 @@
     row_part = {}
 
     def passed(r, c):
-        wants_row = r > 0
-        wants_column = r == 0 or two_sided[r - 1]
+        wants_column = two_sided[r - 1]
         for first in range(0, rows, strip):
             here = slice(first, first + strip)
             best = None
@@ -141,18 +194,11 @@
                 for w in range(1, words):
                     met = met | (bits_down[r][w][here] & lanes_of([o[w] for o in lane_ones], g))
                 keep = met != 0
-                if r == 0 and g < per_block and g * LANES < first + strip and first < (g + 1) * LANES:
-                    down = lax.broadcasted_iota(jnp.int32, value.shape, 0) + first
-                    across = lax.broadcasted_iota(jnp.int32, value.shape, 1) + g * LANES
-                    keep = keep & (down != across)
-                if wants_row:
-                    value = jnp.where(keep, value * scale_down[r][here], LOWEST)
-                    part = jnp.max(value.reshape(strip // SUBLANES, SUBLANES, LANES), axis=0)
-                    row_part[g] = jnp.maximum(row_part[g], part) if g in row_part else part
-                    if wants_column:
-                        value = value * lanes_of(lane_scale, g)
-                else:
-                    value = jnp.where(keep, value * lanes_of(lane_scale, g), LOWEST)
+                value = jnp.where(keep, value * scale_down[r][here], LOWEST)
+                part = jnp.max(value.reshape(strip // SUBLANES, SUBLANES, LANES), axis=0)
+                row_part[g] = jnp.maximum(row_part[g], part) if g in row_part else part
+                if wants_column:
+                    value = value * lanes_of(lane_scale, g)
                 if wants_column:
                     best = value if best is None else jnp.maximum(best, value)
             if wants_column:
@@ -177,7 +223,15 @@
     for r in range(1, tiles):
         if two_sided[r - 1]:
             column_outs.pop(0)[...] = column_of(r)
-    own_best = column_of(0) * scale_of(0)
+    own_bits = bits_of(facts[0][1])
+    own_best = jnp.full((1, rows), LOWEST, jnp.float32)
+    for w in range(words):
+        first = w * WORD
+        part = own_classes[first : min(first + WORD, shards), :]
+        bit = jnp.int32(1) << lax.broadcasted_iota(jnp.int32, part.shape, 0)
+        part = jnp.where((own_bits[w] & bit) != 0, part, LOWEST)
+        own_best = jnp.maximum(own_best, jnp.max(part, axis=0, keepdims=True))
+    own_best = own_best * lane_scale[0]
     for j in range(count):
         for at in range(per_block):
             here = slice(at * LANES, (at + 1) * LANES)
@@ -187,16 +241,16 @@
             row_outs[j][:, here] = found
 
 
-def maxima(device, everyone, partners, moving, plane, given, two_sided):
+def maxima(device, told, own_classes, distant, partners, moving, plane, given, two_sided):
     rows, width = moving.shape
     count = plane.shape[0] // rows
     chunk = min(256, rows)
     vmem = pl.BlockSpec(memory_space=pltpu.VMEM)
     outs = count + sum(two_sided)
     return pl.pallas_call(
-        functools.partial(maxima_kernel, partners, count, tuple(two_sided)),
+        functools.partial(maxima_kernel, partners, count, len(distant), tuple(two_sided)),
         out_shape=[jax.ShapeDtypeStruct((1, rows), jnp.float32)] * outs,
-        in_specs=[vmem] * (4 + len(given)),
+        in_specs=[vmem] * (5 + len(distant) + len(given)),
         out_specs=[vmem] * outs,
         scratch_shapes=[
             pltpu.VMEM((2, rows, chunk), jnp.float32),
@@ -208,7 +262,7 @@
             + 2 * VMEM_SPARE
         ),
         cost_estimate=cost_of(rows, width, plane.shape[0]),
-    )(device, everyone, moving, plane, *given)
+    )(device, told, own_classes, moving, plane, *distant, *given)
 
 
 def pair_words(listed, source, partners, words):
@@ -233,21 +287,34 @@
     return table
 
 
-def joined_kernel(*refs):
-    pieces, out = refs[:-2], refs[-1]
+def joined_kernel(plane, *refs):
+    pieces, told, packed = refs[:-3], refs[-2], refs[-1]
     at = 0
     for piece in pieces:
-        out[at : at + piece.shape[0], :] = piece[...]
+        told[at : at + piece.shape[0], :] = piece[...]
         at += piece.shape[0]
-
-
-def joined(pieces, after):
+    rows = packed.shape[1] - 2 * LANES
+    facts = (pieces[0].shape[1] - rows) // 2
+    packed[...] = jnp.zeros(packed.shape, packed.dtype)
+    for part in range(facts // LANES):
+        here = slice(part * LANES, (part + 1) * LANES)
+        packed[part : part + 1, 0:LANES] = pieces[0][0:1, here]
+        packed[part : part + 1, LANES : 2 * LANES] = pieces[0][0:1, facts + part * LANES : facts + (part + 1) * LANES]
+    packed[0:plane, 2 * LANES :] = told[0:plane, 2 * facts :]
+
+
+def joined(pieces, facts, after):
     vmem = pl.BlockSpec(memory_space=pltpu.VMEM)
+    length = pieces[0].shape[1]
+    plane = sum(p.shape[0] for p in pieces)
     return pl.pallas_call(
-        joined_kernel,
-        out_shape=jax.ShapeDtypeStruct((sum(p.shape[0] for p in pieces), pieces[0].shape[1]), jnp.float32),
+        functools.partial(joined_kernel, plane),
+        out_shape=[
+            jax.ShapeDtypeStruct((plane, length), jnp.float32),
+            jax.ShapeDtypeStruct((max(plane, facts // LANES), length - 2 * facts + 2 * LANES), jnp.float32),
+        ],
         in_specs=[vmem] * len(pieces) + [pl.BlockSpec(memory_space=pl.ANY)],
-        out_specs=vmem,
+        out_specs=[vmem, vmem],
         compiler_params=pltpu.CompilerParams(vmem_limit_bytes=2**20),
     )(*pieces, after)
 
@@ -306,13 +373,14 @@
         pieces.append(permuted(mine, across(bit)))
         bit *= 2
     raw, whole = gathered_plane(blocks)
-    told = joined(pieces, raw)
-    everyone = jnp.concatenate([told] + [permuted(told, along(t)) for t in range(1, planes)], axis=0)
+    told, packed = joined(pieces, rows, raw)
+    distant = [permuted(packed, along(t)) for t in range(1, planes)]
     device = device_table(shards, plane, planes, order, place_of, here)
     distances = range(1, half + 1)
     two_sided = [2 * distance != planes for distance in distances]
-    given = [raw] + [products(arrived[distance], whole) for distance in distances[1:]]
-    found = maxima(device, everyone, partners, arrived[1], whole, given, two_sided)
+    own_classes = classes(told, raw, shards)
+    given = [products(arrived[distance], whole, own_classes) for distance in distances[1:]]
+    found = maxima(device, told, own_classes, distant, partners, arrived[1], whole, given, two_sided)
     gathered, columns = found[:plane], list(found[plane:])
 
     result = gathered[0]

time: 66.2 us -> 64.6 us (0.976)
  waiting for transfers between devices: 30.1 us -> 20.3 us
  Pallas kernels: 10.7 us -> 18.8 us
    ppermute x14, waiting for transfers between devices: 30.1 us -> 20.3 us  [permuted(): return lax.ppermute(value, 'shard', [(s, target(s)) for s in range(shards)])]
    pallas_call x3 -> x4, Pallas kernels: 6.65 us -> 14.8 us  [the longest x1 8.71 us: classes(): pl.pallas_call(classes_kernel, out_shape=jax.ShapeDtypeStruct((subcluster...]
  transfers between devices with their start and end apart: 14 -> 14, of which waited for: 6 -> 7; matrix products, arithmetic and copies ran while one was open for 7% -> 8% of each run, Pallas kernels for 10% -> 23%
where the time goes in v4:
time: 64.6 us; the launch traced here: 64.4 us
  waiting for transfers between devices  20.3 us (31%)
  Pallas kernels  18.8 us (29%)
  starting transfers between devices  18.5 us (29%)
  other arithmetic  5.33 us (8%)
  local copies, waits for them, and re-layouts  1.32 us (2%)
    ppermute x14, waiting for transfers between devices, permuted(): return lax.ppermute(value, 'shard', [(s, target(s)) for s in range(shards)])  20.3 us
    ppermute x14, starting transfers between devices, permuted(): return lax.ppermute(value, 'shard', [(s, target(s)) for s in range(shards)])  18.5 us
    pallas_call x1, Pallas kernels, classes(): pl.pallas_call(classes_kernel, out_shape=jax.ShapeDtypeStruct((subcluster...  8.71 us
    pallas_call x1, Pallas kernels, gathered_plane(): pl.pallas_call(functools.partial(gather_kernel, len(blocks)), out_shape=[...  4.03 us
    pallas_call x1, Pallas kernels, maxima(): pl.pallas_call(functools.partial(maxima_kernel, partners, count, len(dist...  3.68 us
    pallas_call x1, Pallas kernels, products(): pl.pallas_call(product_kernel, out_shape=jax.ShapeDtypeStruct((rows, othe...  2.38 us
    reduce_sum x1, other arithmetic, device_table(): jnp.sum(jnp.where(jnp.arange(planes) == here // plane, jnp.asarray(place_...  1.29 us
  transfers between devices with their start and end apart: 14, of which 7 were waited for; matrix products, arithmetic and copies ran while one was open for 8% of the time, Pallas kernels for 23%

profile of v4, /device:TPU:0, one launch (start us, length us, event | category | flops | bytes accessed | tf_op | source)
XLA Modules:
  0.0 64.4 jit_solution(8619332037893585933)
XLA Ops:
  0.0 3.0 %collective-permute-start.3 = (bf16[512,1024]{1,0:T(8,128)(2,1)}, bf16[512,1024]{1,0:T(8,128)(2,1)S(1)}, u32[]{:S(2)}, u32[]{:S(2)}) collective-permute-start(bf16[512,1024]{1,0:T(8,128)(2,1)} %refs_0_.1), channel_id=1, source_target_pairs={{0,2},{1,3},{2,0},{3,1},{4,6},{5,7},{6,4},{7,5},{8,10},{9,11},{10,... | collective-permute-start | bytes 3145736 | tf_op jit(solution)/shard_map/ppermute | solution.py:345
  3.0 1.6 %collective-permute-start.9 = (bf16[512,1024]{1,0:T(8,128)(2,1)}, bf16[512,1024]{1,0:T(8,128)(2,1)S(1)}, u32[]{:S(2)}, u32[]{:S(2)}) collective-permute-start(bf16[512,1024]{1,0:T(8,128)(2,1)} %refs_0_.1), channel_id=1, source_target_pairs={{0,4},{1,5},{2,6},{3,7},{4,0},{5,1},{6,2},{7,3},{8,12},{9,13},{10,... | collective-permute-start | bytes 3145736 | tf_op jit(solution)/shard_map/ppermute | solution.py:345
  4.5 2.6 %collective-permute-start.5 = (bf16[512,1024]{1,0:T(8,128)(2,1)}, bf16[512,1024]{1,0:T(8,128)(2,1)S(1)}, u32[]{:S(2)}, u32[]{:S(2)}) collective-permute-start(bf16[512,1024]{1,0:T(8,128)(2,1)} %refs_0_.1), channel_id=1, source_target_pairs={{0,8},{1,9},{2,10},{3,11},{4,12},{5,13},{6,14},{7,15},{8,4},{9,5},... | collective-permute-start | bytes 3145736 | tf_op jit(solution)/shard_map/ppermute | solution.py:345
  7.1 0.7 %convert_element_type.18 = f32[512,1]{0,1:T(1,128)S(1)} convert(s32[512,1]{0,1:T(1,128)} %param.8) | non-fusion elementwise | flops 512 | bytes 4096 | tf_op jit(solution)/shard_map/convert_element_type | solution.py:369
  7.8 0.7 %convert_element_type.17 = f32[512]{0:T(512)S(1)} convert(bf16[512]{0:T(512)(128)(2,1)} %param.7) | non-fusion elementwise | flops 512 | bytes 3072 | tf_op jit(solution)/shard_map/convert_element_type | solution.py:369
  8.5 0.7 %convert_bitcast_fusion = f32[5]{0:T(128)S(1)} fusion(s32[1,5]{1,0:T(1,128)} %param.9), kind=kLoop, calls=%fused_computation.24 | loop fusion | flops 5 | bytes 40 | tf_op jit(solution)/shard_map/convert_element_type | solution.py:368
  9.2 17.2 %collective-permute-done.3.refs_2_ = bf16[512,1024]{1,0:T(8,128)(2,1)S(1)} collective-permute-done((bf16[512,1024]{1,0:T(8,128)(2,1)}, bf16[512,1024]{1,0:T(8,128)(2,1)S(1)}, u32[]{:S(2)}, u32[]{:S(2)}) %collective-permute-start.3) | collective-permute-done | bytes 1048608 | tf_op jit(solution)/shard_map/ppermute | solution.py:345
  26.9 1.3 %fusion.6 = s32[]{:T(128)} fusion(s32[4]{0:T(128)} %constant.61.clone, s32[]{:T(128)S(6)} %select_n.49), kind=kLoop, calls=%fused_computation.22 | loop fusion | flops 11 | bytes 24 | tf_op jit(solution)/shard_map/reduce_sum | solution.py:324
  28.2 0.7 %and_select_fusion = s32[16]{0:T(128)S(1)} fusion(s32[]{:T(128)} %fusion.6), kind=kLoop, calls=%fused_computation.15 | loop fusion | flops 320 | bytes 68 | tf_op jit(solution)/shard_map/jit(remainder)/select_n | solution.py:325
  28.9 0.7 %select_reduce_fusion = s32[16]{0:T(128)S(1)} fusion(s32[4]{0:T(128)} %constant.61.clone, s32[16]{0:T(128)S(1)} %and_select_fusion), kind=kLoop, calls=%fused_computation.13 | loop fusion | flops 176 | bytes 144 | tf_op jit(solution)/shard_map/reduce_sum | solution.py:326
  29.7 1.8 %collective-permute-start.1 = (f32[2,1152]{1,0:T(2,128)S(1)}, f32[2,1152]{1,0:T(2,128)S(1)}, u32[]{:S(2)}, u32[]{:S(2)}) collective-permute-start(f32[2,1152]{1,0:T(2,128)S(1)} %pad_maximum_fusion), channel_id=1, source_target_pairs={{0,2},{1,3},{2,0},{3,1},{4,6},{5,7},{6,4},{7,5},{8,10},{9,11},{10,... | collective-permute-start | bytes 27656 | tf_op jit(solution)/shard_map/ppermute | solution.py:345
  31.6 1.2 %copy-done = bf16[512,1024]{1,0:T(8,128)(2,1)S(1)} copy-done((bf16[512,1024]{1,0:T(8,128)(2,1)S(1)}, bf16[512,1024]{1,0:T(8,128)(2,1)}, u32[]{:S(2)}) %copy-start) | copy-done | bytes 1048600
  32.8 4.0 %shard_map.64 = (f32[2048,512]{1,0:T(8,128)S(1)}, bf16[2048,1024]{1,0:T(8,128)(2,1)S(1)}) custom-call(bf16[512,1024]{1,0:T(8,128)(2,1)S(1)} %copy-done, bf16[512,1024]{1,0:T(8,128)(2,1)} %collective-permute-done.2.refs_1_, bf16[512,1024]{1,0:T(8,128)(2,1)S(1)} %collective-permute-done.3.refs_2_, bf16[512,1024]{1,0:T(8,128)(2,1)} %collective-permute-done.4.refs_3_), custom_call_target="tpu_custom_call" | custom-call | flops 2147483648 | bytes 5242880 | tf_op jit(solution)/shard_map/pallas_call | solution.py:60
  36.9 2.6 %collective-permute-start.6 = (f32[4,384]{1,0:T(4,128)S(1)}, f32[4,384]{1,0:T(4,128)S(1)}, u32[]{:S(2)}, u32[]{:S(2)}) collective-permute-start(f32[4,384]{1,0:T(4,128)S(1)} %get-tuple-element.17), channel_id=1, source_target_pairs={{0,8},{1,9},{2,10},{3,11},{4,12},{5,13},{6,14},{7,15},{8,4},{9,5},... | collective-permute-start | bytes 18440 | tf_op jit(solution)/shard_map/ppermute | solution.py:345
  39.5 1.6 %collective-permute-start.7 = (f32[4,384]{1,0:T(4,128)S(1)}, f32[4,384]{1,0:T(4,128)S(1)}, u32[]{:S(2)}, u32[]{:S(2)}) collective-permute-start(f32[4,384]{1,0:T(4,128)S(1)} %get-tuple-element.17), channel_id=1, source_target_pairs={{0,4},{1,5},{2,6},{3,7},{4,0},{5,1},{6,2},{7,3},{8,12},{9,13},{10,... | collective-permute-start | bytes 18440 | tf_op jit(solution)/shard_map/ppermute | solution.py:345
  41.4 8.7 %shard_map.66.after.own_classes = f32[16,512]{1,0:T(8,128)S(1)} custom-call(f32[4,1152]{1,0:T(4,128)S(1)} %get-tuple-element.15.told, f32[2048,512]{1,0:T(8,128)S(1)} %get-tuple-element.14.refs_3_.raw), custom_call_target="tpu_custom_call" | custom-call | tf_op jit(solution)/shard_map/pallas_call | solution.py:127
  50.1 2.4 %shard_map.67.refs_3_ = f32[512,2048]{1,0:T(8,128)S(1)} custom-call(bf16[512,1024]{1,0:T(8,128)(2,1)S(1)} %collective-permute-done.9.moving, bf16[2048,1024]{1,0:T(8,128)(2,1)S(1)} %get-tuple-element.16.plane, f32[16,512]{1,0:T(8,128)S(1)} %shard_map.66.after.own_classes), custom_call_target="tpu_custom_call" | custom-call | flops 2147483648 | bytes 5242880 | tf_op jit(solution)/shard_map/pallas_call | solution.py:78
  52.5 1.1 %collective-permute-done.5.moving = bf16[512,1024]{1,0:T(8,128)(2,1)S(1)} collective-permute-done((bf16[512,1024]{1,0:T(8,128)(2,1)}, bf16[512,1024]{1,0:T(8,128)(2,1)S(1)}, u32[]{:S(2)}, u32[]{:S(2)}) %collective-permute-start.5) | collective-permute-done | bytes 1048608 | tf_op jit(solution)/shard_map/ppermute | solution.py:345
  53.9 3.7 %shard_map.68 = (f32[1,512]{1,0:T(1,128)S(1)}, f32[1,512]{1,0:T(1,128)S(1)}, f32[1,512]{1,0:T(1,128)S(1)}, f32[1,512]{1,0:T(1,128)S(1)}, f32[1,512]{1,0:T(1,128)S(1)}) custom-call(s32[16,1]{1,0:T(8,128)S(1)} %fusion.1.device, f32[4,1152]{1,0:T(4,128)S(1)} %get-tuple-element.15.told, f32[16,512]{1,0:T(8,128)S(1)} %shard_map.66.after.own_classes, ...), custom_call_target="tpu_custom_call" | custom-call | flops 2147483648 | bytes 5242880 | tf_op jit(solution)/shard_map/pallas_call | solution.py:250
  57.6 2.6 %collective-permute-start.10 = (f32[1,512]{1,0:T(1,128)S(1)}, f32[1,512]{1,0:T(1,128)S(1)}, u32[]{:S(2)}, u32[]{:S(2)}) collective-permute-start(f32[1,512]{1,0:T(1,128)S(1)} %get-tuple-element.19), channel_id=1, source_target_pairs={{0,12},{1,13},{2,14},{3,15},{4,8},{5,9},{6,10},{7,11},{8,0},{9,1},... | collective-permute-start | bytes 6152 | tf_op jit(solution)/shard_map/ppermute | solution.py:345
  60.2 0.7 %collective-permute-start.12 = (f32[1,512]{1,0:T(1,128)S(1)}, f32[1,512]{1,0:T(1,128)S(1)}, u32[]{:S(2)}, u32[]{:S(2)}) collective-permute-start(f32[1,512]{1,0:T(1,128)S(1)} %get-tuple-element.21), channel_id=1, source_target_pairs={{0,2},{1,3},{2,0},{3,1},{4,6},{5,7},{6,4},{7,5},{8,10},{9,11},{10,... | collective-permute-start | bytes 6152 | tf_op jit(solution)/shard_map/ppermute | solution.py:345
  60.8 1.2 %collective-permute-start.13 = (f32[1,512]{1,0:T(1,128)S(1)}, f32[1,512]{1,0:T(1,128)S(1)}, u32[]{:S(2)}, u32[]{:S(2)}) collective-permute-start(f32[1,512]{1,0:T(1,128)S(1)} %get-tuple-element.22), channel_id=1, source_target_pairs={{0,1},{1,0},{2,3},{3,2},{4,5},{5,4},{6,7},{7,6},{8,9},{9,8},{10,11... | collective-permute-start | bytes 6152 | tf_op jit(solution)/shard_map/ppermute | solution.py:345
  62.1 1.0 %collective-permute-done.11 = f32[1,512]{1,0:T(1,128)S(1)} collective-permute-done((f32[1,512]{1,0:T(1,128)S(1)}, f32[1,512]{1,0:T(1,128)S(1)}, u32[]{:S(2)}, u32[]{:S(2)}) %collective-permute-start.11) | collective-permute-done | bytes 2080 | tf_op jit(solution)/shard_map/ppermute | solution.py:345
  63.2 0.6 collective-permute-done.12
  (24 shorter events, 2.1 us)
Async XLA Ops:
  0.0 26.3 %collective-permute-start.3 = (bf16[512,1024]{1,0:T(8,128)(2,1)}, bf16[512,1024]{1,0:T(8,128)(2,1)S(1)}, u32[]{:S(2)}, u32[]{:S(2)}) collective-permute-start(bf16[512,1024]{1,0:T(8,128)(2,1)} %refs_0_.1), channel_id=1, source_target_pairs={{0,2},{1,3},{2,0},{3,1},{4,6},{5,7},{6,4},{7,5},{8,10},{9,11},{10,... | collective-permute-start | bytes 3145736 | tf_op jit(solution)/shard_map/ppermute | solution.py:345
  3.0 28.6 %collective-permute-start.2 = (bf16[512,1024]{1,0:T(8,128)(2,1)}, bf16[512,1024]{1,0:T(8,128)(2,1)}, u32[]{:S(2)}, u32[]{:S(2)}) collective-permute-start(bf16[512,1024]{1,0:T(8,128)(2,1)} %refs_0_.1), channel_id=1, source_target_pairs={{0,1},{1,0},{2,3},{3,2},{4,5},{5,4},{6,7},{7,6},{8,9},{9,8},{10,11... | collective-permute-start | bytes 3145736 | tf_op jit(solution)/shard_map/ppermute | solution.py:345
  3.0 47.1 %collective-permute-start.9 = (bf16[512,1024]{1,0:T(8,128)(2,1)}, bf16[512,1024]{1,0:T(8,128)(2,1)S(1)}, u32[]{:S(2)}, u32[]{:S(2)}) collective-permute-start(bf16[512,1024]{1,0:T(8,128)(2,1)} %refs_0_.1), channel_id=1, source_target_pairs={{0,4},{1,5},{2,6},{3,7},{4,0},{5,1},{6,2},{7,3},{8,12},{9,13},{10,... | collective-permute-start | bytes 3145736 | tf_op jit(solution)/shard_map/ppermute | solution.py:345
  4.5 49.0 %collective-permute-start.5 = (bf16[512,1024]{1,0:T(8,128)(2,1)}, bf16[512,1024]{1,0:T(8,128)(2,1)S(1)}, u32[]{:S(2)}, u32[]{:S(2)}) collective-permute-start(bf16[512,1024]{1,0:T(8,128)(2,1)} %refs_0_.1), channel_id=1, source_target_pairs={{0,8},{1,9},{2,10},{3,11},{4,12},{5,13},{6,14},{7,15},{8,4},{9,5},... | collective-permute-start | bytes 3145736 | tf_op jit(solution)/shard_map/ppermute | solution.py:345
  26.3 5.2 %collective-permute-start.4 = (bf16[512,1024]{1,0:T(8,128)(2,1)S(1)}, bf16[512,1024]{1,0:T(8,128)(2,1)}, u32[]{:S(2)}, u32[]{:S(2)}) collective-permute-start(bf16[512,1024]{1,0:T(8,128)(2,1)S(1)} %collective-permute-done.3.refs_2_), channel_id=1, source_target_pairs={{0,1},{1,0},{2,3},{3,2},{4,5},{5,4},{6,7},{7,6},{8,9},{9,8},{10,11... | collective-permute-start | bytes 3145736 | tf_op jit(solution)/shard_map/ppermute | solution.py:345
  26.4 3.4 %collective-permute-start = (f32[1,1152]{1,0:T(1,128)S(1)}, f32[1,1152]{1,0:T(1,128)S(1)}, u32[]{:S(2)}, u32[]{:S(2)}) collective-permute-start(f32[1,1152]{1,0:T(1,128)S(1)} %broadcast_in_dim.25.refs_0_), channel_id=1, source_target_pairs={{0,1},{1,0},{2,3},{3,2},{4,5},{5,4},{6,7},{7,6},{8,9},{9,8},{10,11... | collective-permute-start | bytes 13832 | tf_op jit(solution)/shard_map/ppermute | solution.py:345
  29.7 7.1 %collective-permute-start.1 = (f32[2,1152]{1,0:T(2,128)S(1)}, f32[2,1152]{1,0:T(2,128)S(1)}, u32[]{:S(2)}, u32[]{:S(2)}) collective-permute-start(f32[2,1152]{1,0:T(2,128)S(1)} %pad_maximum_fusion), channel_id=1, source_target_pairs={{0,2},{1,3},{2,0},{3,1},{4,6},{5,7},{6,4},{7,5},{8,10},{9,11},{10,... | collective-permute-start | bytes 27656 | tf_op jit(solution)/shard_map/ppermute | solution.py:345
  31.6 1.2 %copy-start = (bf16[512,1024]{1,0:T(8,128)(2,1)S(1)}, bf16[512,1024]{1,0:T(8,128)(2,1)}, u32[]{:S(2)}) copy-start(bf16[512,1024]{1,0:T(8,128)(2,1)} %refs_0_.1) | copy-start | bytes 3145732
  36.9 16.8 %collective-permute-start.6 = (f32[4,384]{1,0:T(4,128)S(1)}, f32[4,384]{1,0:T(4,128)S(1)}, u32[]{:S(2)}, u32[]{:S(2)}) collective-permute-start(f32[4,384]{1,0:T(4,128)S(1)} %get-tuple-element.17), channel_id=1, source_target_pairs={{0,8},{1,9},{2,10},{3,11},{4,12},{5,13},{6,14},{7,15},{8,4},{9,5},... | collective-permute-start | bytes 18440 | tf_op jit(solution)/shard_map/ppermute | solution.py:345
  39.5 14.2 %collective-permute-start.7 = (f32[4,384]{1,0:T(4,128)S(1)}, f32[4,384]{1,0:T(4,128)S(1)}, u32[]{:S(2)}, u32[]{:S(2)}) collective-permute-start(f32[4,384]{1,0:T(4,128)S(1)} %get-tuple-element.17), channel_id=1, source_target_pairs={{0,4},{1,5},{2,6},{3,7},{4,0},{5,1},{6,2},{7,3},{8,12},{9,13},{10,... | collective-permute-start | bytes 18440 | tf_op jit(solution)/shard_map/ppermute | solution.py:345
  41.1 12.8 %collective-permute-start.8 = (f32[4,384]{1,0:T(4,128)S(1)}, f32[4,384]{1,0:T(4,128)S(1)}, u32[]{:S(2)}, u32[]{:S(2)}) collective-permute-start(f32[4,384]{1,0:T(4,128)S(1)} %get-tuple-element.17), channel_id=1, source_target_pairs={{0,12},{1,13},{2,14},{3,15},{4,8},{5,9},{6,10},{7,11},{8,0},{9,1},... | collective-permute-start | bytes 18440 | tf_op jit(solution)/shard_map/ppermute | solution.py:345
  57.6 4.5 %collective-permute-start.10 = (f32[1,512]{1,0:T(1,128)S(1)}, f32[1,512]{1,0:T(1,128)S(1)}, u32[]{:S(2)}, u32[]{:S(2)}) collective-permute-start(f32[1,512]{1,0:T(1,128)S(1)} %get-tuple-element.19), channel_id=1, source_target_pairs={{0,12},{1,13},{2,14},{3,15},{4,8},{5,9},{6,10},{7,11},{8,0},{9,1},... | collective-permute-start | bytes 6152 | tf_op jit(solution)/shard_map/ppermute | solution.py:345
  60.2 3.0 %collective-permute-start.11 = (f32[1,512]{1,0:T(1,128)S(1)}, f32[1,512]{1,0:T(1,128)S(1)}, u32[]{:S(2)}, u32[]{:S(2)}) collective-permute-start(f32[1,512]{1,0:T(1,128)S(1)} %get-tuple-element.20), channel_id=1, source_target_pairs={{0,3},{1,2},{2,1},{3,0},{4,7},{5,6},{6,5},{7,4},{8,11},{9,10},{10,... | collective-permute-start | bytes 6152 | tf_op jit(solution)/shard_map/ppermute | solution.py:345
  60.2 3.6 %collective-permute-start.12 = (f32[1,512]{1,0:T(1,128)S(1)}, f32[1,512]{1,0:T(1,128)S(1)}, u32[]{:S(2)}, u32[]{:S(2)}) collective-permute-start(f32[1,512]{1,0:T(1,128)S(1)} %get-tuple-element.21), channel_id=1, source_target_pairs={{0,2},{1,3},{2,0},{3,1},{4,6},{5,7},{6,4},{7,5},{8,10},{9,11},{10,... | collective-permute-start | bytes 6152 | tf_op jit(solution)/shard_map/ppermute | solution.py:345
  60.8 2.9 %collective-permute-start.13 = (f32[1,512]{1,0:T(1,128)S(1)}, f32[1,512]{1,0:T(1,128)S(1)}, u32[]{:S(2)}, u32[]{:S(2)}) collective-permute-start(f32[1,512]{1,0:T(1,128)S(1)} %get-tuple-element.22), channel_id=1, source_target_pairs={{0,1},{1,0},{2,3},{3,2},{4,5},{5,4},{6,7},{7,6},{8,9},{9,8},{10,11... | collective-permute-start | bytes 6152 | tf_op jit(solution)/shard_map/ppermute | solution.py:345

commit v5 on v4

--- a/solution.py
+++ b/solution.py
@@ -18,22 +18,24 @@
 def gather_kernel(count, *refs):
     blocks, out, plane, arrived = refs[:count], refs[count], refs[count + 1], refs[count + 2]
     rows = blocks[0].shape[0]
-    copies = [
-        pltpu.make_async_copy(block, plane.at[j * rows : (j + 1) * rows, :], arrived.at[j])
-        for j, block in enumerate(blocks)
-    ]
+    copies, at = [], 0
+    for j, block in enumerate(blocks):
+        copies.append(pltpu.make_async_copy(block, plane.at[at : at + block.shape[0], :], arrived.at[j]))
+        at += block.shape[0]
     for copy in copies:
         copy.start()
-    for copy in copies:
+    at = 0
+    for copy, block in zip(copies, blocks):
         copy.wait()
-    chunk = min(256, rows)
-    for first in range(0, plane.shape[0], chunk):
-        out[first : first + chunk, :] = lax.dot_general(
-            plane[first : first + chunk, :],
-            plane[:rows, :],
-            (((1,), (1,)), ((), ())),
-            preferred_element_type=jnp.float32,
-        )
+        chunk = min(256, block.shape[0])
+        for first in range(at, at + block.shape[0], chunk):
+            out[first : first + chunk, :] = lax.dot_general(
+                plane[first : first + chunk, :],
+                plane[:rows, :],
+                (((1,), (1,)), ((), ())),
+                preferred_element_type=jnp.float32,
+            )
+        at += block.shape[0]
 
 
 def product_kernel(moving, plane, after, out):
@@ -55,7 +57,7 @@
 
 def gathered_plane(blocks):
     rows, width = blocks[0].shape
-    others = rows * len(blocks)
+    others = sum(block.shape[0] for block in blocks)
     vmem = pl.BlockSpec(memory_space=pltpu.VMEM)
     return pl.pallas_call(
         functools.partial(gather_kernel, len(blocks)),
@@ -91,15 +93,16 @@
     return jnp.transpose(jnp.broadcast_to(value, (LANES, value.shape[1])))
 
 
-def classes_kernel(told, raw, out, scale_down, cluster_down):
+def classes_kernel(partners, told, raw, out, scale_down, cluster_down):
     count, rows = told.shape[0], raw.shape[1]
     strip = min(STRIP, rows)
     for j in range(count):
         here = slice(j * rows, (j + 1) * rows)
         scale_down[here, :] = along_sublanes(told[j : j + 1, 0:rows])
         cluster_down[here, :] = along_sublanes(told[j : j + 1, rows : 2 * rows])
-    subclusters = out.shape[0]
+    offsets = range(-partners, partners + 1)
     for first in range(0, rows, LANES):
+        mine = told[0:1, rows + first : rows + first + LANES]
 
         def step(i, best):
             here = pl.ds(pl.multiple_of(i * strip, strip), strip)
@@ -107,26 +110,26 @@
             across = lax.broadcasted_iota(jnp.int32, (strip, LANES), 1) + first
             value = raw[here, first : first + LANES] * scale_down[here, :]
             value = jnp.where(down == across, LOWEST, value)
-            cluster = cluster_down[here, :]
+            ahead = cluster_down[here, :] - mine
             found = []
-            for a in range(subclusters):
-                one = jnp.where(cluster == float(a), value, LOWEST)
+            for before, offset in zip(best, offsets):
+                one = jnp.where(ahead == float(offset), value, LOWEST)
                 one = jnp.max(one.reshape(strip // SUBLANES, SUBLANES, LANES), axis=0)
-                found.append(jnp.maximum(best[a], one))
+                found.append(jnp.maximum(before, one))
             return tuple(found)
 
-        start = tuple(jnp.full((SUBLANES, LANES), LOWEST, jnp.float32) for _ in range(subclusters))
+        start = tuple(jnp.full((SUBLANES, LANES), LOWEST, jnp.float32) for _ in offsets)
         best = lax.fori_loop(0, raw.shape[0] // strip, step, start)
-        for a in range(subclusters):
-            out[a : a + 1, first : first + LANES] = jnp.max(best[a], axis=0, keepdims=True)
-
-
-def classes(told, raw, subclusters):
+        for k, one in enumerate(best):
+            out[k : k + 1, first : first + LANES] = jnp.max(one, axis=0, keepdims=True)
+
+
+def classes(told, raw, partners):
     others, rows = raw.shape
     vmem = pl.BlockSpec(memory_space=pltpu.VMEM)
     return pl.pallas_call(
-        classes_kernel,
-        out_shape=jax.ShapeDtypeStruct((subclusters, rows), jnp.float32),
+        functools.partial(classes_kernel, partners),
+        out_shape=jax.ShapeDtypeStruct((2 * partners + 1, rows), jnp.float32),
         in_specs=[vmem, vmem],
         out_specs=vmem,
         scratch_shapes=[pltpu.VMEM((others, LANES), jnp.float32)] * 2,
@@ -225,12 +228,14 @@
             column_outs.pop(0)[...] = column_of(r)
     own_bits = bits_of(facts[0][1])
     own_best = jnp.full((1, rows), LOWEST, jnp.float32)
-    for w in range(words):
-        first = w * WORD
-        part = own_classes[first : min(first + WORD, shards), :]
-        bit = jnp.int32(1) << lax.broadcasted_iota(jnp.int32, part.shape, 0)
-        part = jnp.where((own_bits[w] & bit) != 0, part, LOWEST)
-        own_best = jnp.maximum(own_best, jnp.max(part, axis=0, keepdims=True))
+    named = facts[0][1].astype(jnp.int32)
+    for k in range(2 * partners + 1):
+        met = jnp.int32(0)
+        other = named + (k - partners)
+        for w in range(words):
+            bit = jnp.where((other >= 0) & (other // WORD == w), jnp.int32(1) << (other % WORD), 0)
+            met = met | (own_bits[w] & bit)
+        own_best = jnp.maximum(own_best, jnp.where(met != 0, own_classes[k : k + 1, :], LOWEST))
     own_best = own_best * lane_scale[0]
     for j in range(count):
         for at in range(per_block):
@@ -287,6 +292,21 @@
     return table
 
 
+def kept_kernel(value, after, out):
+    out[...] = value[...]
+
+
+def kept(value, after):
+    vmem = pl.BlockSpec(memory_space=pltpu.VMEM)
+    return pl.pallas_call(
+        kept_kernel,
+        out_shape=jax.ShapeDtypeStruct(value.shape, value.dtype),
+        in_specs=[vmem, pl.BlockSpec(memory_space=pl.ANY)],
+        out_specs=vmem,
+        compiler_params=pltpu.CompilerParams(vmem_limit_bytes=2**20),
+    )(value, after)
+
+
 def joined_kernel(plane, *refs):
     pieces, told, packed = refs[:-3], refs[-2], refs[-1]
     at = 0
@@ -357,16 +377,25 @@
     arrived = {}
     for distance in range(1, half + 1):
         arrived[distance] = permuted(embeddings, along(distance))
-    held = {0: embeddings}
+    parts = 2
+    size = rows // parts
+    held = {(0, p): embeddings[p * size : (p + 1) * size] for p in range(parts)}
+    whole_block = {0: embeddings}
     bit = plane // 2
     while bit:
-        for j in sorted(held):
-            held[j | bit] = permuted(held[j], across(bit))
+        for j, p in sorted(held):
+            if bit == 1 and j == 0:
+                continue
+            held[j | bit, p] = permuted(held[j, p], across(bit))
         bit //= 2
-    blocks = [held[j] for j in range(plane)]
+    whole_block[1] = permuted(embeddings, across(1))
+    blocks = []
+    for j in range(plane):
+        blocks += [whole_block[j]] if j in whole_block else [held[j, p] for p in range(parts)]
 
     pairs = jnp.pad(pair_listed.reshape(-1).astype(jnp.float32), (0, -(owned * partners) % LANES))
     told = jnp.concatenate([scales.astype(jnp.float32), cluster[:, 0].astype(jnp.float32), pairs])[None, :]
+    told = kept(told, held[plane // 2, 0])
     pieces, bit = [told], 1
     while bit < plane:
         mine = pieces[0] if len(pieces) == 1 else jnp.concatenate(pieces, axis=0)
@@ -378,7 +407,7 @@
     device = device_table(shards, plane, planes, order, place_of, here)
     distances = range(1, half + 1)
     two_sided = [2 * distance != planes for distance in distances]
-    own_classes = classes(told, raw, shards)
+    own_classes = classes(told, raw, partners)
     given = [products(arrived[distance], whole, own_classes) for distance in distances[1:]]
     found = maxima(device, told, own_classes, distant, partners, arrived[1], whole, given, two_sided)
     gathered, columns = found[:plane], list(found[plane:])

time: 64.6 us -> 64.5 us (level)
  local copies, waits for them, and re-layouts: 1.32 us -> 3.58 us
  Pallas kernels: 18.8 us -> 16.9 us
  starting transfers between devices: 18.5 us -> 16.7 us
  waiting for transfers between devices: 20.3 us -> 21.6 us
    slice x0 -> x1, local copies, waits for them, and re-layouts: none -> 2.26 us  [per_device(): held = {(0, p): embeddings[p * size:(p + 1) * size] for p in range(parts)}]
    pallas_call x1 -> x2, Pallas kernels: 8.71 us -> 6.78 us  [the longest x1 6.77 us: classes(): pl.pallas_call(functools.partial(classes_kernel, partners), out_shape=jax...]
    ppermute x14 -> x16, starting transfers between devices: 18.5 us -> 16.7 us  [permuted(): return lax.ppermute(value, 'shard', [(s, target(s)) for s in range(shards)])]
    ppermute x14 -> x16, waiting for transfers between devices: 20.3 us -> 21.6 us  [permuted(): return lax.ppermute(value, 'shard', [(s, target(s)) for s in range(shards)])]
  transfers between devices with their start and end apart: 14 -> 16, of which waited for: 7 -> 6; matrix products, arithmetic and copies ran while one was open for 8% -> 11% of each run, Pallas kernels for 23% -> 20%
where the time goes in v5:
time: 64.5 us; the launch traced here: 64.2 us
  waiting for transfers between devices  21.6 us (33%)
  Pallas kernels  16.9 us (26%)
  starting transfers between devices  16.7 us (26%)
  other arithmetic  5.33 us (8%)
  local copies, waits for them, and re-layouts  3.58 us (6%)
    ppermute x16, waiting for transfers between devices, permuted(): return lax.ppermute(value, 'shard', [(s, target(s)) for s in range(shards)])  21.6 us
    ppermute x16, starting transfers between devices, permuted(): return lax.ppermute(value, 'shard', [(s, target(s)) for s in range(shards)])  16.7 us
    pallas_call x1, Pallas kernels, classes(): pl.pallas_call(functools.partial(classes_kernel, partners), out_shape=jax...  6.77 us
    pallas_call x1, Pallas kernels, gathered_plane(): pl.pallas_call(functools.partial(gather_kernel, len(blocks)), out_shape=[...  3.97 us
    pallas_call x1, Pallas kernels, maxima(): pl.pallas_call(functools.partial(maxima_kernel, partners, count, len(dist...  3.74 us
    pallas_call x1, Pallas kernels, products(): pl.pallas_call(product_kernel, out_shape=jax.ShapeDtypeStruct((rows, othe...  2.38 us
    slice x1, local copies, waits for them, and re-layouts, per_device(): held = {(0, p): embeddings[p * size:(p + 1) * size] for p in range(parts)}  2.26 us
    reduce_sum x1, other arithmetic, device_table(): jnp.sum(jnp.where(jnp.arange(planes) == here // plane, jnp.asarray(place_...  1.3 us
  transfers between devices with their start and end apart: 16, of which 6 were waited for; matrix products, arithmetic and copies ran while one was open for 11% of the time, Pallas kernels for 20%

profile of v5, /device:TPU:0, one launch (start us, length us, event | category | flops | bytes accessed | tf_op | source)
XLA Modules:
  0.0 64.2 jit_solution(6705568357969040758)
XLA Ops:
  0.5 2.6 %collective-permute-start.11 = (bf16[512,1024]{1,0:T(8,128)(2,1)}, bf16[512,1024]{1,0:T(8,128)(2,1)S(1)}, u32[]{:S(2)}, u32[]{:S(2)}) collective-permute-start(bf16[512,1024]{1,0:T(8,128)(2,1)} %refs_0_.1), channel_id=1, source_target_pairs={{0,4},{1,5},{2,6},{3,7},{4,0},{5,1},{6,2},{7,3},{8,12},{9,13},{10,... | collective-permute-start | bytes 3145736 | tf_op jit(solution)/shard_map/ppermute | solution.py:365
  3.0 2.6 %collective-permute-start.7 = (bf16[512,1024]{1,0:T(8,128)(2,1)}, bf16[512,1024]{1,0:T(8,128)(2,1)S(1)}, u32[]{:S(2)}, u32[]{:S(2)}) collective-permute-start(bf16[512,1024]{1,0:T(8,128)(2,1)} %refs_0_.1), channel_id=1, source_target_pairs={{0,8},{1,9},{2,10},{3,11},{4,12},{5,13},{6,14},{7,15},{8,4},{9,5},... | collective-permute-start | bytes 3145736 | tf_op jit(solution)/shard_map/ppermute | solution.py:365
  5.6 2.3 %fusion.8 = (bf16[256,1024]{1,0:T(8,128)(2,1)}, bf16[256,1024]{1,0:T(8,128)(2,1)}) fusion(bf16[512,1024]{1,0:T(8,128)(2,1)} %refs_0_.1), kind=kLoop, calls=%fused_computation.26 | loop fusion | bytes 2097152 | tf_op jit(solution)/shard_map/slice | solution.py:382
  7.9 1.5 %collective-permute-start = (bf16[256,1024]{1,0:T(8,128)(2,1)}, bf16[256,1024]{1,0:T(8,128)(2,1)S(1)}, u32[]{:S(2)}, u32[]{:S(2)}) collective-permute-start(bf16[256,1024]{1,0:T(8,128)(2,1)} %get-tuple-element.24), channel_id=1, source_target_pairs={{0,2},{1,3},{2,0},{3,1},{4,6},{5,7},{6,4},{7,5},{8,10},{9,11},{10,... | collective-permute-start | bytes 1572872 | tf_op jit(solution)/shard_map/ppermute | solution.py:365
  9.9 0.7 %convert_bitcast_fusion = f32[5]{0:T(128)S(1)} fusion(s32[1,5]{1,0:T(1,128)} %param.9), kind=kLoop, calls=%fused_computation.24 | loop fusion | flops 5 | bytes 40 | tf_op jit(solution)/shard_map/convert_element_type | solution.py:396
  10.6 0.7 %convert_element_type.18 = f32[512,1]{0,1:T(1,128)S(1)} convert(s32[512,1]{0,1:T(1,128)} %param.8) | non-fusion elementwise | flops 512 | bytes 4096 | tf_op jit(solution)/shard_map/convert_element_type | solution.py:397
  11.2 0.7 %convert_element_type.17 = f32[512]{0:T(512)S(1)} convert(bf16[512]{0:T(512)(128)(2,1)} %param.7) | non-fusion elementwise | flops 512 | bytes 3072 | tf_op jit(solution)/shard_map/convert_element_type | solution.py:397
  12.0 1.3 %fusion.6 = s32[]{:T(128)} fusion(s32[4]{0:T(128)} %constant.61.clone, s32[]{:T(128)S(6)} %select_n.49), kind=kLoop, calls=%fused_computation.22 | loop fusion | flops 11 | bytes 24 | tf_op jit(solution)/shard_map/reduce_sum | solution.py:344
  13.9 9.0 %collective-permute-done.after.refs_2_ = bf16[256,1024]{1,0:T(8,128)(2,1)S(1)} collective-permute-done((bf16[256,1024]{1,0:T(8,128)(2,1)}, bf16[256,1024]{1,0:T(8,128)(2,1)S(1)}, u32[]{:S(2)}, u32[]{:S(2)}) %collective-permute-start) | collective-permute-done | bytes 524320 | tf_op jit(solution)/shard_map/ppermute | solution.py:365
  22.9 0.7 %select_reduce_fusion = s32[16]{0:T(128)S(1)} fusion(s32[4]{0:T(128)} %constant.61.clone, s32[16]{0:T(128)S(1)} %and_select_fusion), kind=kLoop, calls=%fused_computation.13 | loop fusion | flops 176 | bytes 144 | tf_op jit(solution)/shard_map/reduce_sum | solution.py:346
  23.6 9.5 %collective-permute-done.4.refs_3_ = bf16[256,1024]{1,0:T(8,128)(2,1)S(1)} collective-permute-done((bf16[256,1024]{1,0:T(8,128)(2,1)}, bf16[256,1024]{1,0:T(8,128)(2,1)S(1)}, u32[]{:S(2)}, u32[]{:S(2)}) %collective-permute-start.4) | collective-permute-done | bytes 524320 | tf_op jit(solution)/shard_map/ppermute | solution.py:365
  33.7 1.4 %collective-permute-done.5.refs_4_ = bf16[256,1024]{1,0:T(8,128)(2,1)} collective-permute-done((bf16[256,1024]{1,0:T(8,128)(2,1)S(1)}, bf16[256,1024]{1,0:T(8,128)(2,1)}, u32[]{:S(2)}, u32[]{:S(2)}) %collective-permute-start.5) | collective-permute-done | bytes 524320 | tf_op jit(solution)/shard_map/ppermute | solution.py:365
  35.1 1.5 %collective-permute-start.2 = (f32[2,1152]{1,0:T(2,128)S(1)}, f32[2,1152]{1,0:T(2,128)S(1)}, u32[]{:S(2)}, u32[]{:S(2)}) collective-permute-start(f32[2,1152]{1,0:T(2,128)S(1)} %pad_maximum_fusion), channel_id=1, source_target_pairs={{0,2},{1,3},{2,0},{3,1},{4,6},{5,7},{6,4},{7,5},{8,10},{9,11},{10,... | collective-permute-start | bytes 27656 | tf_op jit(solution)/shard_map/ppermute | solution.py:365
  36.7 1.2 %copy-done = bf16[512,1024]{1,0:T(8,128)(2,1)S(1)} copy-done((bf16[512,1024]{1,0:T(8,128)(2,1)S(1)}, bf16[512,1024]{1,0:T(8,128)(2,1)}, u32[]{:S(2)}) %copy-start) | copy-done | bytes 1048600
  37.9 4.0 %shard_map.65 = (f32[2048,512]{1,0:T(8,128)S(1)}, bf16[2048,1024]{1,0:T(8,128)(2,1)S(1)}) custom-call(bf16[512,1024]{1,0:T(8,128)(2,1)S(1)} %copy-done, bf16[512,1024]{1,0:T(8,128)(2,1)} %collective-permute-done.3.refs_1_, bf16[256,1024]{1,0:T(8,128)(2,1)S(1)} %collective-permute-done.after.refs_2_, bf16[256,1024]{1,0:T(8,128)(2,1)S(1)} %collective-permute-done.4.refs_3_, ...), custom_call_target="tpu_custom_call" | custom-call | flops 2147483648 | bytes 5242880 | tf_op jit(solution)/shard_map/pallas_call | solution.py:62
  41.9 1.3 %collective-permute-start.10 = (f32[4,384]{1,0:T(4,128)S(1)}, f32[4,384]{1,0:T(4,128)S(1)}, u32[]{:S(2)}, u32[]{:S(2)}) collective-permute-start(f32[4,384]{1,0:T(4,128)S(1)} %get-tuple-element.17), channel_id=1, source_target_pairs={{0,12},{1,13},{2,14},{3,15},{4,8},{5,9},{6,10},{7,11},{8,0},{9,1},... | collective-permute-start | bytes 18440 | tf_op jit(solution)/shard_map/ppermute | solution.py:365
  43.2 1.7 %collective-permute-start.8 = (f32[4,384]{1,0:T(4,128)S(1)}, f32[4,384]{1,0:T(4,128)S(1)}, u32[]{:S(2)}, u32[]{:S(2)}) collective-permute-start(f32[4,384]{1,0:T(4,128)S(1)} %get-tuple-element.17), channel_id=1, source_target_pairs={{0,8},{1,9},{2,10},{3,11},{4,12},{5,13},{6,14},{7,15},{8,4},{9,5},... | collective-permute-start | bytes 18440 | tf_op jit(solution)/shard_map/ppermute | solution.py:365
  45.3 6.8 %shard_map.67.after.own_classes = f32[11,512]{1,0:T(8,128)S(1)} custom-call(f32[4,1152]{1,0:T(4,128)S(1)} %get-tuple-element.15.told, f32[2048,512]{1,0:T(8,128)S(1)} %get-tuple-element.14.refs_3_.raw), custom_call_target="tpu_custom_call" | custom-call | tf_op jit(solution)/shard_map/pallas_call | solution.py:130
  52.1 2.4 %shard_map.68.refs_3_ = f32[512,2048]{1,0:T(8,128)S(1)} custom-call(bf16[512,1024]{1,0:T(8,128)(2,1)S(1)} %collective-permute-done.11.moving, bf16[2048,1024]{1,0:T(8,128)(2,1)S(1)} %get-tuple-element.16.plane, f32[11,512]{1,0:T(8,128)S(1)} %shard_map.67.after.own_classes), custom_call_target="tpu_custom_call" | custom-call | flops 2147483648 | bytes 5242880 | tf_op jit(solution)/shard_map/pallas_call | solution.py:80
  54.6 3.7 %shard_map.69 = (f32[1,512]{1,0:T(1,128)S(1)}, f32[1,512]{1,0:T(1,128)S(1)}, f32[1,512]{1,0:T(1,128)S(1)}, f32[1,512]{1,0:T(1,128)S(1)}, f32[1,512]{1,0:T(1,128)S(1)}) custom-call(s32[16,1]{1,0:T(8,128)S(1)} %fusion.1.device, f32[4,1152]{1,0:T(4,128)S(1)} %get-tuple-element.15.told, f32[11,512]{1,0:T(8,128)S(1)} %shard_map.67.after.own_classes, ...), custom_call_target="tpu_custom_call" | custom-call | flops 2147483648 | bytes 5242880 | tf_op jit(solution)/shard_map/pallas_call | solution.py:255
  58.3 1.7 %collective-permute-start.12 = (f32[1,512]{1,0:T(1,128)S(1)}, f32[1,512]{1,0:T(1,128)S(1)}, u32[]{:S(2)}, u32[]{:S(2)}) collective-permute-start(f32[1,512]{1,0:T(1,128)S(1)} %get-tuple-element.19), channel_id=1, source_target_pairs={{0,12},{1,13},{2,14},{3,15},{4,8},{5,9},{6,10},{7,11},{8,0},{9,1},... | collective-permute-start | bytes 6152 | tf_op jit(solution)/shard_map/ppermute | solution.py:365
  60.0 0.8 %collective-permute-start.14 = (f32[1,512]{1,0:T(1,128)S(1)}, f32[1,512]{1,0:T(1,128)S(1)}, u32[]{:S(2)}, u32[]{:S(2)}) collective-permute-start(f32[1,512]{1,0:T(1,128)S(1)} %get-tuple-element.21), channel_id=1, source_target_pairs={{0,2},{1,3},{2,0},{3,1},{4,6},{5,7},{6,4},{7,5},{8,10},{9,11},{10,... | collective-permute-start | bytes 6152 | tf_op jit(solution)/shard_map/ppermute | solution.py:365
  60.8 1.1 %collective-permute-start.15 = (f32[1,512]{1,0:T(1,128)S(1)}, f32[1,512]{1,0:T(1,128)S(1)}, u32[]{:S(2)}, u32[]{:S(2)}) collective-permute-start(f32[1,512]{1,0:T(1,128)S(1)} %get-tuple-element.22), channel_id=1, source_target_pairs={{0,1},{1,0},{2,3},{3,2},{4,5},{5,4},{6,7},{7,6},{8,9},{9,8},{10,11... | collective-permute-start | bytes 6152 | tf_op jit(solution)/shard_map/ppermute | solution.py:365
  61.9 0.9 %collective-permute-done.12 = f32[1,512]{1,0:T(1,128)S(1)} collective-permute-done((f32[1,512]{1,0:T(1,128)S(1)}, f32[1,512]{1,0:T(1,128)S(1)}, u32[]{:S(2)}, u32[]{:S(2)}) %collective-permute-start.12) | collective-permute-done | bytes 2080 | tf_op jit(solution)/shard_map/ppermute | solution.py:365
  (30 shorter events, 4.2 us)
Async XLA Ops:
  0.0 36.7 %collective-permute-start.3 = (bf16[512,1024]{1,0:T(8,128)(2,1)}, bf16[512,1024]{1,0:T(8,128)(2,1)}, u32[]{:S(2)}, u32[]{:S(2)}) collective-permute-start(bf16[512,1024]{1,0:T(8,128)(2,1)} %refs_0_.1), channel_id=1, source_target_pairs={{0,1},{1,0},{2,3},{3,2},{4,5},{5,4},{6,7},{7,6},{8,9},{9,8},{10,11... | collective-permute-start | bytes 3145736 | tf_op jit(solution)/shard_map/ppermute | solution.py:365
  0.5 51.7 %collective-permute-start.11 = (bf16[512,1024]{1,0:T(8,128)(2,1)}, bf16[512,1024]{1,0:T(8,128)(2,1)S(1)}, u32[]{:S(2)}, u32[]{:S(2)}) collective-permute-start(bf16[512,1024]{1,0:T(8,128)(2,1)} %refs_0_.1), channel_id=1, source_target_pairs={{0,4},{1,5},{2,6},{3,7},{4,0},{5,1},{6,2},{7,3},{8,12},{9,13},{10,... | collective-permute-start | bytes 3145736 | tf_op jit(solution)/shard_map/ppermute | solution.py:365
  3.0 51.5 %collective-permute-start.7 = (bf16[512,1024]{1,0:T(8,128)(2,1)}, bf16[512,1024]{1,0:T(8,128)(2,1)S(1)}, u32[]{:S(2)}, u32[]{:S(2)}) collective-permute-start(bf16[512,1024]{1,0:T(8,128)(2,1)} %refs_0_.1), channel_id=1, source_target_pairs={{0,8},{1,9},{2,10},{3,11},{4,12},{5,13},{6,14},{7,15},{8,4},{9,5},... | collective-permute-start | bytes 3145736 | tf_op jit(solution)/shard_map/ppermute | solution.py:365
  7.9 15.0 %collective-permute-start = (bf16[256,1024]{1,0:T(8,128)(2,1)}, bf16[256,1024]{1,0:T(8,128)(2,1)S(1)}, u32[]{:S(2)}, u32[]{:S(2)}) collective-permute-start(bf16[256,1024]{1,0:T(8,128)(2,1)} %get-tuple-element.24), channel_id=1, source_target_pairs={{0,2},{1,3},{2,0},{3,1},{4,6},{5,7},{6,4},{7,5},{8,10},{9,11},{10,... | collective-permute-start | bytes 1572872 | tf_op jit(solution)/shard_map/ppermute | solution.py:365
  9.4 23.7 %collective-permute-start.4 = (bf16[256,1024]{1,0:T(8,128)(2,1)}, bf16[256,1024]{1,0:T(8,128)(2,1)S(1)}, u32[]{:S(2)}, u32[]{:S(2)}) collective-permute-start(bf16[256,1024]{1,0:T(8,128)(2,1)} %get-tuple-element.23), channel_id=1, source_target_pairs={{0,2},{1,3},{2,0},{3,1},{4,6},{5,7},{6,4},{7,5},{8,10},{9,11},{10,... | collective-permute-start | bytes 1572872 | tf_op jit(solution)/shard_map/ppermute | solution.py:365
  22.9 10.2 %collective-permute-start.1 = (f32[1,1152]{1,0:T(1,128)S(1)}, f32[1,1152]{1,0:T(1,128)S(1)}, u32[]{:S(2)}, u32[]{:S(2)}) collective-permute-start(f32[1,1152]{1,0:T(1,128)S(1)} %shard_map.64.refs_0_), channel_id=1, source_target_pairs={{0,1},{1,0},{2,3},{3,2},{4,5},{5,4},{6,7},{7,6},{8,9},{9,8},{10,11... | collective-permute-start | bytes 13832 | tf_op jit(solution)/shard_map/ppermute | solution.py:365
  33.1 2.0 %collective-permute-start.5 = (bf16[256,1024]{1,0:T(8,128)(2,1)S(1)}, bf16[256,1024]{1,0:T(8,128)(2,1)}, u32[]{:S(2)}, u32[]{:S(2)}) collective-permute-start(bf16[256,1024]{1,0:T(8,128)(2,1)S(1)} %collective-permute-done.after.refs_2_), channel_id=1, source_target_pairs={{0,1},{1,0},{2,3},{3,2},{4,5},{5,4},{6,7},{7,6},{8,9},{9,8},{10,11... | collective-permute-start | bytes 1572872 | tf_op jit(solution)/shard_map/ppermute | solution.py:365
  33.1 3.6 %collective-permute-start.6 = (bf16[256,1024]{1,0:T(8,128)(2,1)S(1)}, bf16[256,1024]{1,0:T(8,128)(2,1)}, u32[]{:S(2)}, u32[]{:S(2)}) collective-permute-start(bf16[256,1024]{1,0:T(8,128)(2,1)S(1)} %collective-permute-done.4.refs_3_), channel_id=1, source_target_pairs={{0,1},{1,0},{2,3},{3,2},{4,5},{5,4},{6,7},{7,6},{8,9},{9,8},{10,11... | collective-permute-start | bytes 1572872 | tf_op jit(solution)/shard_map/ppermute | solution.py:365
  35.1 6.7 %collective-permute-start.2 = (f32[2,1152]{1,0:T(2,128)S(1)}, f32[2,1152]{1,0:T(2,128)S(1)}, u32[]{:S(2)}, u32[]{:S(2)}) collective-permute-start(f32[2,1152]{1,0:T(2,128)S(1)} %pad_maximum_fusion), channel_id=1, source_target_pairs={{0,2},{1,3},{2,0},{3,1},{4,6},{5,7},{6,4},{7,5},{8,10},{9,11},{10,... | collective-permute-start | bytes 27656 | tf_op jit(solution)/shard_map/ppermute | solution.py:365
  36.7 1.2 %copy-start = (bf16[512,1024]{1,0:T(8,128)(2,1)S(1)}, bf16[512,1024]{1,0:T(8,128)(2,1)}, u32[]{:S(2)}) copy-start(bf16[512,1024]{1,0:T(8,128)(2,1)} %refs_0_.1) | copy-start | bytes 3145732
  41.9 12.6 %collective-permute-start.10 = (f32[4,384]{1,0:T(4,128)S(1)}, f32[4,384]{1,0:T(4,128)S(1)}, u32[]{:S(2)}, u32[]{:S(2)}) collective-permute-start(f32[4,384]{1,0:T(4,128)S(1)} %get-tuple-element.17), channel_id=1, source_target_pairs={{0,12},{1,13},{2,14},{3,15},{4,8},{5,9},{6,10},{7,11},{8,0},{9,1},... | collective-permute-start | bytes 18440 | tf_op jit(solution)/shard_map/ppermute | solution.py:365
  43.2 11.3 %collective-permute-start.8 = (f32[4,384]{1,0:T(4,128)S(1)}, f32[4,384]{1,0:T(4,128)S(1)}, u32[]{:S(2)}, u32[]{:S(2)}) collective-permute-start(f32[4,384]{1,0:T(4,128)S(1)} %get-tuple-element.17), channel_id=1, source_target_pairs={{0,8},{1,9},{2,10},{3,11},{4,12},{5,13},{6,14},{7,15},{8,4},{9,5},... | collective-permute-start | bytes 18440 | tf_op jit(solution)/shard_map/ppermute | solution.py:365
  44.9 9.7 %collective-permute-start.9 = (f32[4,384]{1,0:T(4,128)S(1)}, f32[4,384]{1,0:T(4,128)S(1)}, u32[]{:S(2)}, u32[]{:S(2)}) collective-permute-start(f32[4,384]{1,0:T(4,128)S(1)} %get-tuple-element.17), channel_id=1, source_target_pairs={{0,4},{1,5},{2,6},{3,7},{4,0},{5,1},{6,2},{7,3},{8,12},{9,13},{10,... | collective-permute-start | bytes 18440 | tf_op jit(solution)/shard_map/ppermute | solution.py:365
  58.3 4.5 %collective-permute-start.12 = (f32[1,512]{1,0:T(1,128)S(1)}, f32[1,512]{1,0:T(1,128)S(1)}, u32[]{:S(2)}, u32[]{:S(2)}) collective-permute-start(f32[1,512]{1,0:T(1,128)S(1)} %get-tuple-element.19), channel_id=1, source_target_pairs={{0,12},{1,13},{2,14},{3,15},{4,8},{5,9},{6,10},{7,11},{8,0},{9,1},... | collective-permute-start | bytes 6152 | tf_op jit(solution)/shard_map/ppermute | solution.py:365
  60.0 3.0 %collective-permute-start.13 = (f32[1,512]{1,0:T(1,128)S(1)}, f32[1,512]{1,0:T(1,128)S(1)}, u32[]{:S(2)}, u32[]{:S(2)}) collective-permute-start(f32[1,512]{1,0:T(1,128)S(1)} %get-tuple-element.20), channel_id=1, source_target_pairs={{0,3},{1,2},{2,1},{3,0},{4,7},{5,6},{6,5},{7,4},{8,11},{9,10},{10,... | collective-permute-start | bytes 6152 | tf_op jit(solution)/shard_map/ppermute | solution.py:365
  60.0 3.6 %collective-permute-start.14 = (f32[1,512]{1,0:T(1,128)S(1)}, f32[1,512]{1,0:T(1,128)S(1)}, u32[]{:S(2)}, u32[]{:S(2)}) collective-permute-start(f32[1,512]{1,0:T(1,128)S(1)} %get-tuple-element.21), channel_id=1, source_target_pairs={{0,2},{1,3},{2,0},{3,1},{4,6},{5,7},{6,4},{7,5},{8,10},{9,11},{10,... | collective-permute-start | bytes 6152 | tf_op jit(solution)/shard_map/ppermute | solution.py:365
  60.8 2.8 %collective-permute-start.15 = (f32[1,512]{1,0:T(1,128)S(1)}, f32[1,512]{1,0:T(1,128)S(1)}, u32[]{:S(2)}, u32[]{:S(2)}) collective-permute-start(f32[1,512]{1,0:T(1,128)S(1)} %get-tuple-element.22), channel_id=1, source_target_pairs={{0,1},{1,0},{2,3},{3,2},{4,5},{5,4},{6,7},{7,6},{8,9},{9,8},{10,11... | collective-permute-start | bytes 6152 | tf_op jit(solution)/shard_map/ppermute | solution.py:365

commit v6 on v3

--- a/solution.py
+++ b/solution.py
@@ -18,10 +18,10 @@
 def gather_kernel(count, *refs):
     blocks, out, plane, arrived = refs[:count], refs[count], refs[count + 1], refs[count + 2]
     rows = blocks[0].shape[0]
-    copies = [
-        pltpu.make_async_copy(block, plane.at[j * rows : (j + 1) * rows, :], arrived.at[j])
-        for j, block in enumerate(blocks)
-    ]
+    copies, at = [], 0
+    for j, block in enumerate(blocks):
+        copies.append(pltpu.make_async_copy(block, plane.at[at : at + block.shape[0], :], arrived.at[j]))
+        at += block.shape[0]
     for copy in copies:
         copy.start()
     for copy in copies:
@@ -48,7 +48,7 @@
 
 def gathered_plane(blocks):
     rows, width = blocks[0].shape
-    others = rows * len(blocks)
+    others = sum(block.shape[0] for block in blocks)
     vmem = pl.BlockSpec(memory_space=pltpu.VMEM)
     return pl.pallas_call(
         functools.partial(gather_kernel, len(blocks)),
@@ -80,8 +80,9 @@
     )(moving, plane)
 
 
-def maxima_kernel(partners, count, two_sided, device, everyone, moving, plane, *refs):
+def maxima_kernel(partners, count, others, two_sided, device, told, moving, plane, *refs):
     tiles = 1 + len(two_sided)
+    distant, refs = refs[:others], refs[others:]
     given = dict(zip([0, *range(2, tiles)], refs))
     row_outs = refs[len(given) : len(given) + count]
     column_outs = list(refs[len(given) + count : -2])
@@ -92,32 +93,34 @@
     chunk = fresh.shape[2]
     per_chunk = chunk // LANES
     chunks = plane.shape[0] // chunk
-    shards = everyone.shape[0]
+    shards = device.shape[0]
     words = -(-shards // WORD)
     source = device[...]
-    table = pair_words(everyone[:, 2 * rows :], source, partners, words)
-
-    def scale_of(at):
-        return everyone[at : at + 1, 0:rows]
-
-    def cluster_of(at):
-        return everyone[at : at + 1, rows : 2 * rows].astype(jnp.int32)
-
-    def bits_of(at):
-        named = cluster_of(at) == source
+    pairs = [told[:, 2 * rows :]] + [d[0:count, 2 * LANES :] for d in distant]
+    table = pair_words(jnp.concatenate(pairs, axis=0), source, partners, words)
+
+    def facts_of(r):
+        if r == 0:
+            return told[0:1, 0:rows], told[0:1, rows : 2 * rows]
+        parts = [distant[r - 1][p : p + 1, 0 : 2 * LANES] for p in range(rows // LANES)]
+        return [jnp.concatenate([p[:, at : at + LANES] for p in parts], axis=1) for at in (0, LANES)]
+
+    def bits_of(clusters):
+        named = clusters.astype(jnp.int32) == source
         return [jnp.sum(jnp.where(named, t, 0.0), axis=0, keepdims=True).astype(jnp.int32) for t in table]
 
     def ones_of(at):
-        named = cluster_of(at)
+        named = told[at : at + 1, rows : 2 * rows].astype(jnp.int32)
         return [jnp.where(named // WORD == w, jnp.int32(1) << (named % WORD), 0) for w in range(words)]
 
     def along_sublanes(value):
         return jnp.transpose(jnp.broadcast_to(value, (LANES, rows)))
 
-    lane_scale = [scale_of(j) for j in range(count)]
+    lane_scale = [told[j : j + 1, 0:rows] for j in range(count)]
     lane_ones = [ones_of(j) for j in range(count)]
-    scale_down = [along_sublanes(scale_of(r * count)) for r in range(tiles)]
-    bits_down = [[along_sublanes(b) for b in bits_of(r * count)] for r in range(tiles)]
+    facts = [facts_of(r) for r in range(tiles)]
+    scale_down = [along_sublanes(scales) for scales, _ in facts]
+    bits_down = [[along_sublanes(b) for b in bits_of(clusters)] for _, clusters in facts]
 
     def lanes_of(per, g):
         first = g % per_block * LANES
@@ -177,7 +180,7 @@
     for r in range(1, tiles):
         if two_sided[r - 1]:
             column_outs.pop(0)[...] = column_of(r)
-    own_best = column_of(0) * scale_of(0)
+    own_best = column_of(0) * lane_scale[0]
     for j in range(count):
         for at in range(per_block):
             here = slice(at * LANES, (at + 1) * LANES)
@@ -187,16 +190,16 @@
             row_outs[j][:, here] = found
 
 
-def maxima(device, everyone, partners, moving, plane, given, two_sided):
+def maxima(device, told, distant, partners, moving, plane, given, two_sided):
     rows, width = moving.shape
     count = plane.shape[0] // rows
     chunk = min(256, rows)
     vmem = pl.BlockSpec(memory_space=pltpu.VMEM)
     outs = count + sum(two_sided)
     return pl.pallas_call(
-        functools.partial(maxima_kernel, partners, count, tuple(two_sided)),
+        functools.partial(maxima_kernel, partners, count, len(distant), tuple(two_sided)),
         out_shape=[jax.ShapeDtypeStruct((1, rows), jnp.float32)] * outs,
-        in_specs=[vmem] * (4 + len(given)),
+        in_specs=[vmem] * (4 + len(distant) + len(given)),
         out_specs=[vmem] * outs,
         scratch_shapes=[
             pltpu.VMEM((2, rows, chunk), jnp.float32),
@@ -208,7 +211,7 @@
             + 2 * VMEM_SPARE
         ),
         cost_estimate=cost_of(rows, width, plane.shape[0]),
-    )(device, everyone, moving, plane, *given)
+    )(device, told, moving, plane, *distant, *given)
 
 
 def pair_words(listed, source, partners, words):
@@ -233,21 +236,49 @@
     return table
 
 
-def joined_kernel(*refs):
-    pieces, out = refs[:-2], refs[-1]
+def kept_kernel(value, after, out):
+    out[...] = value[...]
+
+
+def kept(value, after):
+    vmem = pl.BlockSpec(memory_space=pltpu.VMEM)
+    return pl.pallas_call(
+        kept_kernel,
+        out_shape=jax.ShapeDtypeStruct(value.shape, value.dtype),
+        in_specs=[vmem, pl.BlockSpec(memory_space=pl.ANY)],
+        out_specs=vmem,
+        compiler_params=pltpu.CompilerParams(vmem_limit_bytes=2**20),
+    )(value, after)
+
+
+def joined_kernel(plane, *refs):
+    pieces, told, packed = refs[:-3], refs[-2], refs[-1]
     at = 0
     for piece in pieces:
-        out[at : at + piece.shape[0], :] = piece[...]
+        told[at : at + piece.shape[0], :] = piece[...]
         at += piece.shape[0]
-
-
-def joined(pieces, after):
-    vmem = pl.BlockSpec(memory_space=pltpu.VMEM)
-    return pl.pallas_call(
-        joined_kernel,
-        out_shape=jax.ShapeDtypeStruct((sum(p.shape[0] for p in pieces), pieces[0].shape[1]), jnp.float32),
+    rows = packed.shape[1] - 2 * LANES
+    facts = (pieces[0].shape[1] - rows) // 2
+    packed[...] = jnp.zeros(packed.shape, packed.dtype)
+    for part in range(facts // LANES):
+        here = slice(part * LANES, (part + 1) * LANES)
+        packed[part : part + 1, 0:LANES] = pieces[0][0:1, here]
+        packed[part : part + 1, LANES : 2 * LANES] = pieces[0][0:1, facts + part * LANES : facts + (part + 1) * LANES]
+    packed[0:plane, 2 * LANES :] = told[0:plane, 2 * facts :]
+
+
+def joined(pieces, facts, after):
+    vmem = pl.BlockSpec(memory_space=pltpu.VMEM)
+    length = pieces[0].shape[1]
+    plane = sum(p.shape[0] for p in pieces)
+    return pl.pallas_call(
+        functools.partial(joined_kernel, plane),
+        out_shape=[
+            jax.ShapeDtypeStruct((plane, length), jnp.float32),
+            jax.ShapeDtypeStruct((max(plane, facts // LANES), length - 2 * facts + 2 * LANES), jnp.float32),
+        ],
         in_specs=[vmem] * len(pieces) + [pl.BlockSpec(memory_space=pl.ANY)],
-        out_specs=vmem,
+        out_specs=[vmem, vmem],
         compiler_params=pltpu.CompilerParams(vmem_limit_bytes=2**20),
     )(*pieces, after)
 
@@ -290,29 +321,38 @@
     arrived = {}
     for distance in range(1, half + 1):
         arrived[distance] = permuted(embeddings, along(distance))
-    held = {0: embeddings}
+    parts = 2
+    size = rows // parts
+    held = {(0, p): embeddings[p * size : (p + 1) * size] for p in range(parts)}
+    whole_block = {0: embeddings}
     bit = plane // 2
     while bit:
-        for j in sorted(held):
-            held[j | bit] = permuted(held[j], across(bit))
+        for j, p in sorted(held):
+            if bit == 1 and j == 0:
+                continue
+            held[j | bit, p] = permuted(held[j, p], across(bit))
         bit //= 2
-    blocks = [held[j] for j in range(plane)]
+    whole_block[1] = permuted(embeddings, across(1))
+    blocks = []
+    for j in range(plane):
+        blocks += [whole_block[j]] if j in whole_block else [held[j, p] for p in range(parts)]
 
     pairs = jnp.pad(pair_listed.reshape(-1).astype(jnp.float32), (0, -(owned * partners) % LANES))
     told = jnp.concatenate([scales.astype(jnp.float32), cluster[:, 0].astype(jnp.float32), pairs])[None, :]
+    told = kept(told, held[plane // 2, 0])
     pieces, bit = [told], 1
     while bit < plane:
         mine = pieces[0] if len(pieces) == 1 else jnp.concatenate(pieces, axis=0)
         pieces.append(permuted(mine, across(bit)))
         bit *= 2
     raw, whole = gathered_plane(blocks)
-    told = joined(pieces, raw)
-    everyone = jnp.concatenate([told] + [permuted(told, along(t)) for t in range(1, planes)], axis=0)
+    told, packed = joined(pieces, rows, raw)
+    distant = [permuted(packed, along(t)) for t in range(1, planes)]
     device = device_table(shards, plane, planes, order, place_of, here)
     distances = range(1, half + 1)
     two_sided = [2 * distance != planes for distance in distances]
     given = [raw] + [products(arrived[distance], whole) for distance in distances[1:]]
-    found = maxima(device, everyone, partners, arrived[1], whole, given, two_sided)
+    found = maxima(device, told, distant, partners, arrived[1], whole, given, two_sided)
     gathered, columns = found[:plane], list(found[plane:])
 
     result = gathered[0]

time: 66.2 us -> 64.1 us (0.968)
  waiting for transfers between devices: 30.1 us -> 26.3 us
  local copies, waits for them, and re-layouts: 1.32 us -> 3.58 us
    ppermute x14 -> x16, waiting for transfers between devices: 30.1 us -> 26.3 us  [permuted(): return lax.ppermute(value, 'shard', [(s, target(s)) for s in range(shards)])]
    slice x0 -> x1, local copies, waits for them, and re-layouts: none -> 2.26 us  [per_device(): held = {(0, p): embeddings[p * size:(p + 1) * size] for p in range(parts)}]
    ppermute x14 -> x16, starting transfers between devices: 18.3 us -> 17.7 us  [permuted(): return lax.ppermute(value, 'shard', [(s, target(s)) for s in range(shards)])]
    pallas_call x2 -> x3, Pallas kernels: 4.28 us -> 4.43 us  [the longest x1 4.42 us: maxima(): pl.pallas_call(functools.partial(maxima_kernel, partners, count, len(dist...]
  transfers between devices with their start and end apart: 14 -> 16, of which waited for: 6 -> 7; matrix products, arithmetic and copies ran while one was open for 7% -> 11% of each run, Pallas kernels for 10% -> 10%
where the time goes in v6:
time: 64.1 us; the launch traced here: 63.9 us
  waiting for transfers between devices  26.3 us (41%)
  starting transfers between devices  17.7 us (28%)
  Pallas kernels  10.8 us (17%)
  other arithmetic  5.33 us (8%)
  local copies, waits for them, and re-layouts  3.58 us (6%)
    ppermute x16, waiting for transfers between devices, permuted(): return lax.ppermute(value, 'shard', [(s, target(s)) for s in range(shards)])  26.3 us
    ppermute x16, starting transfers between devices, permuted(): return lax.ppermute(value, 'shard', [(s, target(s)) for s in range(shards)])  17.7 us
    pallas_call x1, Pallas kernels, maxima(): pl.pallas_call(functools.partial(maxima_kernel, partners, count, len(dist...  4.42 us
    pallas_call x1, Pallas kernels, gathered_plane(): pl.pallas_call(functools.partial(gather_kernel, len(blocks)), out_shape=[...  4.02 us
    pallas_call x1, Pallas kernels, products(): pl.pallas_call(times_plane, out_shape=jax.ShapeDtypeStruct((rows, others)...  2.38 us
    slice x1, local copies, waits for them, and re-layouts, per_device(): held = {(0, p): embeddings[p * size:(p + 1) * size] for p in range(parts)}  2.26 us
    reduce_sum x1, other arithmetic, device_table(): jnp.sum(jnp.where(jnp.arange(planes) == here // plane, jnp.asarray(place_...  1.3 us
  transfers between devices with their start and end apart: 16, of which 7 were waited for; matrix products, arithmetic and copies ran while one was open for 11% of the time, Pallas kernels for 10%

profile of v6, /device:TPU:0, one launch (start us, length us, event | category | flops | bytes accessed | tf_op | source)
XLA Modules:
  0.0 63.9 jit_solution(7410860826145025111)
XLA Ops:
  0.5 2.6 %collective-permute-start.11 = (bf16[512,1024]{1,0:T(8,128)(2,1)}, bf16[512,1024]{1,0:T(8,128)(2,1)S(1)}, u32[]{:S(2)}, u32[]{:S(2)}) collective-permute-start(bf16[512,1024]{1,0:T(8,128)(2,1)} %refs_0_.1), channel_id=1, source_target_pairs={{0,4},{1,5},{2,6},{3,7},{4,0},{5,1},{6,2},{7,3},{8,12},{9,13},{10,... | collective-permute-start | bytes 3145736 | tf_op jit(solution)/shard_map/ppermute | solution.py:309
  3.0 2.6 %collective-permute-start.7 = (bf16[512,1024]{1,0:T(8,128)(2,1)}, bf16[512,1024]{1,0:T(8,128)(2,1)S(1)}, u32[]{:S(2)}, u32[]{:S(2)}) collective-permute-start(bf16[512,1024]{1,0:T(8,128)(2,1)} %refs_0_.1), channel_id=1, source_target_pairs={{0,8},{1,9},{2,10},{3,11},{4,12},{5,13},{6,14},{7,15},{8,4},{9,5},... | collective-permute-start | bytes 3145736 | tf_op jit(solution)/shard_map/ppermute | solution.py:309
  5.6 2.3 %fusion.8 = (bf16[256,1024]{1,0:T(8,128)(2,1)}, bf16[256,1024]{1,0:T(8,128)(2,1)}) fusion(bf16[512,1024]{1,0:T(8,128)(2,1)} %refs_0_.1), kind=kLoop, calls=%fused_computation.26 | loop fusion | bytes 2097152 | tf_op jit(solution)/shard_map/slice | solution.py:326
  7.9 1.5 %collective-permute-start = (bf16[256,1024]{1,0:T(8,128)(2,1)}, bf16[256,1024]{1,0:T(8,128)(2,1)S(1)}, u32[]{:S(2)}, u32[]{:S(2)}) collective-permute-start(bf16[256,1024]{1,0:T(8,128)(2,1)} %get-tuple-element.24), channel_id=1, source_target_pairs={{0,2},{1,3},{2,0},{3,1},{4,6},{5,7},{6,4},{7,5},{8,10},{9,11},{10,... | collective-permute-start | bytes 1572872 | tf_op jit(solution)/shard_map/ppermute | solution.py:309
  9.9 0.7 %convert_bitcast_fusion = f32[5]{0:T(128)S(1)} fusion(s32[1,5]{1,0:T(1,128)} %param.9), kind=kLoop, calls=%fused_computation.24 | loop fusion | flops 5 | bytes 40 | tf_op jit(solution)/shard_map/convert_element_type | solution.py:340
  10.6 0.7 %convert_element_type.18 = f32[512,1]{0,1:T(1,128)S(1)} convert(s32[512,1]{0,1:T(1,128)} %param.8) | non-fusion elementwise | flops 512 | bytes 4096 | tf_op jit(solution)/shard_map/convert_element_type | solution.py:341
  11.2 0.7 %convert_element_type.17 = f32[512]{0:T(512)S(1)} convert(bf16[512]{0:T(512)(128)(2,1)} %param.7) | non-fusion elementwise | flops 512 | bytes 3072 | tf_op jit(solution)/shard_map/convert_element_type | solution.py:341
  12.0 1.3 %fusion.6 = s32[]{:T(128)} fusion(s32[4]{0:T(128)} %constant.61.clone, s32[]{:T(128)S(6)} %select_n.49), kind=kLoop, calls=%fused_computation.22 | loop fusion | flops 11 | bytes 24 | tf_op jit(solution)/shard_map/reduce_sum | solution.py:288
  13.9 9.0 %collective-permute-done.after.refs_2_ = bf16[256,1024]{1,0:T(8,128)(2,1)S(1)} collective-permute-done((bf16[256,1024]{1,0:T(8,128)(2,1)}, bf16[256,1024]{1,0:T(8,128)(2,1)S(1)}, u32[]{:S(2)}, u32[]{:S(2)}) %collective-permute-start) | collective-permute-done | bytes 524320 | tf_op jit(solution)/shard_map/ppermute | solution.py:309
  22.9 0.7 %select_reduce_fusion = s32[16]{0:T(128)S(1)} fusion(s32[4]{0:T(128)} %constant.61.clone, s32[16]{0:T(128)S(1)} %and_select_fusion), kind=kLoop, calls=%fused_computation.13 | loop fusion | flops 176 | bytes 144 | tf_op jit(solution)/shard_map/reduce_sum | solution.py:290
  23.6 9.5 %collective-permute-done.4.refs_3_ = bf16[256,1024]{1,0:T(8,128)(2,1)S(1)} collective-permute-done((bf16[256,1024]{1,0:T(8,128)(2,1)}, bf16[256,1024]{1,0:T(8,128)(2,1)S(1)}, u32[]{:S(2)}, u32[]{:S(2)}) %collective-permute-start.4) | collective-permute-done | bytes 524320 | tf_op jit(solution)/shard_map/ppermute | solution.py:309
  33.7 1.4 %collective-permute-done.5.refs_4_ = bf16[256,1024]{1,0:T(8,128)(2,1)} collective-permute-done((bf16[256,1024]{1,0:T(8,128)(2,1)S(1)}, bf16[256,1024]{1,0:T(8,128)(2,1)}, u32[]{:S(2)}, u32[]{:S(2)}) %collective-permute-start.5) | collective-permute-done | bytes 524320 | tf_op jit(solution)/shard_map/ppermute | solution.py:309
  35.1 1.5 %collective-permute-start.2 = (f32[2,1152]{1,0:T(2,128)S(1)}, f32[2,1152]{1,0:T(2,128)S(1)}, u32[]{:S(2)}, u32[]{:S(2)}) collective-permute-start(f32[2,1152]{1,0:T(2,128)S(1)} %pad_maximum_fusion), channel_id=1, source_target_pairs={{0,2},{1,3},{2,0},{3,1},{4,6},{5,7},{6,4},{7,5},{8,10},{9,11},{10,... | collective-permute-start | bytes 27656 | tf_op jit(solution)/shard_map/ppermute | solution.py:309
  36.7 1.2 %copy-done = bf16[512,1024]{1,0:T(8,128)(2,1)S(1)} copy-done((bf16[512,1024]{1,0:T(8,128)(2,1)S(1)}, bf16[512,1024]{1,0:T(8,128)(2,1)}, u32[]{:S(2)}) %copy-start) | copy-done | bytes 1048600
  37.9 4.0 %shard_map.65 = (f32[512,2048]{1,0:T(8,128)S(1)}, bf16[2048,1024]{1,0:T(8,128)(2,1)S(1)}) custom-call(bf16[512,1024]{1,0:T(8,128)(2,1)S(1)} %copy-done, bf16[512,1024]{1,0:T(8,128)(2,1)} %collective-permute-done.3.refs_1_, bf16[256,1024]{1,0:T(8,128)(2,1)S(1)} %collective-permute-done.after.refs_2_, bf16[256,1024]{1,0:T(8,128)(2,1)S(1)} %collective-permute-done.4.refs_3_, ...), custom_call_target="tpu_custom_call" | custom-call | flops 2147483648 | bytes 5242880 | tf_op jit(solution)/shard_map/pallas_call | solution.py:53
  42.0 1.3 %collective-permute-start.10 = (f32[4,384]{1,0:T(4,128)S(1)}, f32[4,384]{1,0:T(4,128)S(1)}, u32[]{:S(2)}, u32[]{:S(2)}) collective-permute-start(f32[4,384]{1,0:T(4,128)S(1)} %get-tuple-element.17), channel_id=1, source_target_pairs={{0,12},{1,13},{2,14},{3,15},{4,8},{5,9},{6,10},{7,11},{8,0},{9,1},... | collective-permute-start | bytes 18440 | tf_op jit(solution)/shard_map/ppermute | solution.py:309
  43.2 1.7 %collective-permute-start.8 = (f32[4,384]{1,0:T(4,128)S(1)}, f32[4,384]{1,0:T(4,128)S(1)}, u32[]{:S(2)}, u32[]{:S(2)}) collective-permute-start(f32[4,384]{1,0:T(4,128)S(1)} %get-tuple-element.17), channel_id=1, source_target_pairs={{0,8},{1,9},{2,10},{3,11},{4,12},{5,13},{6,14},{7,15},{8,4},{9,5},... | collective-permute-start | bytes 18440 | tf_op jit(solution)/shard_map/ppermute | solution.py:309
  45.4 2.4 %shard_map.67.refs_4_ = f32[512,2048]{1,0:T(8,128)S(1)} custom-call(bf16[512,1024]{1,0:T(8,128)(2,1)S(1)} %collective-permute-done.11.moving, bf16[2048,1024]{1,0:T(8,128)(2,1)S(1)} %get-tuple-element.16.plane), custom_call_target="tpu_custom_call" | custom-call | flops 2147483648 | bytes 5242880 | tf_op jit(solution)/shard_map/pallas_call | solution.py:71
  47.8 4.3 %collective-permute-done.7.moving = bf16[512,1024]{1,0:T(8,128)(2,1)S(1)} collective-permute-done((bf16[512,1024]{1,0:T(8,128)(2,1)}, bf16[512,1024]{1,0:T(8,128)(2,1)S(1)}, u32[]{:S(2)}, u32[]{:S(2)}) %collective-permute-start.7) | collective-permute-done | bytes 1048608 | tf_op jit(solution)/shard_map/ppermute | solution.py:309
  52.3 4.4 %shard_map.68 = (f32[1,512]{1,0:T(1,128)S(1)}, f32[1,512]{1,0:T(1,128)S(1)}, f32[1,512]{1,0:T(1,128)S(1)}, f32[1,512]{1,0:T(1,128)S(1)}, f32[1,512]{1,0:T(1,128)S(1)}) custom-call(s32[16,1]{1,0:T(8,128)S(1)} %fusion.1.device, f32[4,1152]{1,0:T(4,128)S(1)} %get-tuple-element.15.told, bf16[512,1024]{1,0:T(8,128)(2,1)S(1)} %collective-permute-done.7.moving, ...), custom_call_target="tpu_custom_call" | custom-call | flops 2147483648 | bytes 5242880 | tf_op jit(solution)/shard_map/pallas_call | solution.py:199
  56.7 2.7 %collective-permute-start.12 = (f32[1,512]{1,0:T(1,128)S(1)}, f32[1,512]{1,0:T(1,128)S(1)}, u32[]{:S(2)}, u32[]{:S(2)}) collective-permute-start(f32[1,512]{1,0:T(1,128)S(1)} %get-tuple-element.19), channel_id=1, source_target_pairs={{0,12},{1,13},{2,14},{3,15},{4,8},{5,9},{6,10},{7,11},{8,0},{9,1},... | collective-permute-start | bytes 6152 | tf_op jit(solution)/shard_map/ppermute | solution.py:309
  59.7 1.3 %collective-permute-start.14 = (f32[1,512]{1,0:T(1,128)S(1)}, f32[1,512]{1,0:T(1,128)S(1)}, u32[]{:S(2)}, u32[]{:S(2)}) collective-permute-start(f32[1,512]{1,0:T(1,128)S(1)} %get-tuple-element.21), channel_id=1, source_target_pairs={{0,2},{1,3},{2,0},{3,1},{4,6},{5,7},{6,4},{7,5},{8,10},{9,11},{10,... | collective-permute-start | bytes 6152 | tf_op jit(solution)/shard_map/ppermute | solution.py:309
  61.3 1.1 %collective-permute-done.13 = f32[1,512]{1,0:T(1,128)S(1)} collective-permute-done((f32[1,512]{1,0:T(1,128)S(1)}, f32[1,512]{1,0:T(1,128)S(1)}, u32[]{:S(2)}, u32[]{:S(2)}) %collective-permute-start.13) | collective-permute-done | bytes 2080 | tf_op jit(solution)/shard_map/ppermute | solution.py:309
  62.4 0.8 %collective-permute-done.14 = f32[1,512]{1,0:T(1,128)S(1)} collective-permute-done((f32[1,512]{1,0:T(1,128)S(1)}, f32[1,512]{1,0:T(1,128)S(1)}, u32[]{:S(2)}, u32[]{:S(2)}) %collective-permute-start.14) | collective-permute-done | bytes 2080 | tf_op jit(solution)/shard_map/ppermute | solution.py:309
  (29 shorter events, 4.1 us)
Async XLA Ops:
  0.0 36.7 %collective-permute-start.3 = (bf16[512,1024]{1,0:T(8,128)(2,1)}, bf16[512,1024]{1,0:T(8,128)(2,1)}, u32[]{:S(2)}, u32[]{:S(2)}) collective-permute-start(bf16[512,1024]{1,0:T(8,128)(2,1)} %refs_0_.1), channel_id=1, source_target_pairs={{0,1},{1,0},{2,3},{3,2},{4,5},{5,4},{6,7},{7,6},{8,9},{9,8},{10,11... | collective-permute-start | bytes 3145736 | tf_op jit(solution)/shard_map/ppermute | solution.py:309
  0.5 44.9 %collective-permute-start.11 = (bf16[512,1024]{1,0:T(8,128)(2,1)}, bf16[512,1024]{1,0:T(8,128)(2,1)S(1)}, u32[]{:S(2)}, u32[]{:S(2)}) collective-permute-start(bf16[512,1024]{1,0:T(8,128)(2,1)} %refs_0_.1), channel_id=1, source_target_pairs={{0,4},{1,5},{2,6},{3,7},{4,0},{5,1},{6,2},{7,3},{8,12},{9,13},{10,... | collective-permute-start | bytes 3145736 | tf_op jit(solution)/shard_map/ppermute | solution.py:309
  3.0 49.0 %collective-permute-start.7 = (bf16[512,1024]{1,0:T(8,128)(2,1)}, bf16[512,1024]{1,0:T(8,128)(2,1)S(1)}, u32[]{:S(2)}, u32[]{:S(2)}) collective-permute-start(bf16[512,1024]{1,0:T(8,128)(2,1)} %refs_0_.1), channel_id=1, source_target_pairs={{0,8},{1,9},{2,10},{3,11},{4,12},{5,13},{6,14},{7,15},{8,4},{9,5},... | collective-permute-start | bytes 3145736 | tf_op jit(solution)/shard_map/ppermute | solution.py:309
  7.9 15.0 %collective-permute-start = (bf16[256,1024]{1,0:T(8,128)(2,1)}, bf16[256,1024]{1,0:T(8,128)(2,1)S(1)}, u32[]{:S(2)}, u32[]{:S(2)}) collective-permute-start(bf16[256,1024]{1,0:T(8,128)(2,1)} %get-tuple-element.24), channel_id=1, source_target_pairs={{0,2},{1,3},{2,0},{3,1},{4,6},{5,7},{6,4},{7,5},{8,10},{9,11},{10,... | collective-permute-start | bytes 1572872 | tf_op jit(solution)/shard_map/ppermute | solution.py:309
  9.4 23.7 %collective-permute-start.4 = (bf16[256,1024]{1,0:T(8,128)(2,1)}, bf16[256,1024]{1,0:T(8,128)(2,1)S(1)}, u32[]{:S(2)}, u32[]{:S(2)}) collective-permute-start(bf16[256,1024]{1,0:T(8,128)(2,1)} %get-tuple-element.23), channel_id=1, source_target_pairs={{0,2},{1,3},{2,0},{3,1},{4,6},{5,7},{6,4},{7,5},{8,10},{9,11},{10,... | collective-permute-start | bytes 1572872 | tf_op jit(solution)/shard_map/ppermute | solution.py:309
  22.9 10.2 %collective-permute-start.1 = (f32[1,1152]{1,0:T(1,128)S(1)}, f32[1,1152]{1,0:T(1,128)S(1)}, u32[]{:S(2)}, u32[]{:S(2)}) collective-permute-start(f32[1,1152]{1,0:T(1,128)S(1)} %shard_map.64.refs_0_), channel_id=1, source_target_pairs={{0,1},{1,0},{2,3},{3,2},{4,5},{5,4},{6,7},{7,6},{8,9},{9,8},{10,11... | collective-permute-start | bytes 13832 | tf_op jit(solution)/shard_map/ppermute | solution.py:309
  33.1 2.0 %collective-permute-start.5 = (bf16[256,1024]{1,0:T(8,128)(2,1)S(1)}, bf16[256,1024]{1,0:T(8,128)(2,1)}, u32[]{:S(2)}, u32[]{:S(2)}) collective-permute-start(bf16[256,1024]{1,0:T(8,128)(2,1)S(1)} %collective-permute-done.after.refs_2_), channel_id=1, source_target_pairs={{0,1},{1,0},{2,3},{3,2},{4,5},{5,4},{6,7},{7,6},{8,9},{9,8},{10,11... | collective-permute-start | bytes 1572872 | tf_op jit(solution)/shard_map/ppermute | solution.py:309
  33.1 3.6 %collective-permute-start.6 = (bf16[256,1024]{1,0:T(8,128)(2,1)S(1)}, bf16[256,1024]{1,0:T(8,128)(2,1)}, u32[]{:S(2)}, u32[]{:S(2)}) collective-permute-start(bf16[256,1024]{1,0:T(8,128)(2,1)S(1)} %collective-permute-done.4.refs_3_), channel_id=1, source_target_pairs={{0,1},{1,0},{2,3},{3,2},{4,5},{5,4},{6,7},{7,6},{8,9},{9,8},{10,11... | collective-permute-start | bytes 1572872 | tf_op jit(solution)/shard_map/ppermute | solution.py:309
  35.1 6.8 %collective-permute-start.2 = (f32[2,1152]{1,0:T(2,128)S(1)}, f32[2,1152]{1,0:T(2,128)S(1)}, u32[]{:S(2)}, u32[]{:S(2)}) collective-permute-start(f32[2,1152]{1,0:T(2,128)S(1)} %pad_maximum_fusion), channel_id=1, source_target_pairs={{0,2},{1,3},{2,0},{3,1},{4,6},{5,7},{6,4},{7,5},{8,10},{9,11},{10,... | collective-permute-start | bytes 27656 | tf_op jit(solution)/shard_map/ppermute | solution.py:309
  36.7 1.2 %copy-start = (bf16[512,1024]{1,0:T(8,128)(2,1)S(1)}, bf16[512,1024]{1,0:T(8,128)(2,1)}, u32[]{:S(2)}) copy-start(bf16[512,1024]{1,0:T(8,128)(2,1)} %refs_0_.1) | copy-start | bytes 3145732
  42.0 10.3 %collective-permute-start.10 = (f32[4,384]{1,0:T(4,128)S(1)}, f32[4,384]{1,0:T(4,128)S(1)}, u32[]{:S(2)}, u32[]{:S(2)}) collective-permute-start(f32[4,384]{1,0:T(4,128)S(1)} %get-tuple-element.17), channel_id=1, source_target_pairs={{0,12},{1,13},{2,14},{3,15},{4,8},{5,9},{6,10},{7,11},{8,0},{9,1},... | collective-permute-start | bytes 18440 | tf_op jit(solution)/shard_map/ppermute | solution.py:309
  43.2 9.0 %collective-permute-start.8 = (f32[4,384]{1,0:T(4,128)S(1)}, f32[4,384]{1,0:T(4,128)S(1)}, u32[]{:S(2)}, u32[]{:S(2)}) collective-permute-start(f32[4,384]{1,0:T(4,128)S(1)} %get-tuple-element.17), channel_id=1, source_target_pairs={{0,8},{1,9},{2,10},{3,11},{4,12},{5,13},{6,14},{7,15},{8,4},{9,5},... | collective-permute-start | bytes 18440 | tf_op jit(solution)/shard_map/ppermute | solution.py:309
  44.9 7.3 %collective-permute-start.9 = (f32[4,384]{1,0:T(4,128)S(1)}, f32[4,384]{1,0:T(4,128)S(1)}, u32[]{:S(2)}, u32[]{:S(2)}) collective-permute-start(f32[4,384]{1,0:T(4,128)S(1)} %get-tuple-element.17), channel_id=1, source_target_pairs={{0,4},{1,5},{2,6},{3,7},{4,0},{5,1},{6,2},{7,3},{8,12},{9,13},{10,... | collective-permute-start | bytes 18440 | tf_op jit(solution)/shard_map/ppermute | solution.py:309
  56.7 4.6 %collective-permute-start.12 = (f32[1,512]{1,0:T(1,128)S(1)}, f32[1,512]{1,0:T(1,128)S(1)}, u32[]{:S(2)}, u32[]{:S(2)}) collective-permute-start(f32[1,512]{1,0:T(1,128)S(1)} %get-tuple-element.19), channel_id=1, source_target_pairs={{0,12},{1,13},{2,14},{3,15},{4,8},{5,9},{6,10},{7,11},{8,0},{9,1},... | collective-permute-start | bytes 6152 | tf_op jit(solution)/shard_map/ppermute | solution.py:309
  59.4 3.0 %collective-permute-start.13 = (f32[1,512]{1,0:T(1,128)S(1)}, f32[1,512]{1,0:T(1,128)S(1)}, u32[]{:S(2)}, u32[]{:S(2)}) collective-permute-start(f32[1,512]{1,0:T(1,128)S(1)} %get-tuple-element.20), channel_id=1, source_target_pairs={{0,3},{1,2},{2,1},{3,0},{4,7},{5,6},{6,5},{7,4},{8,11},{9,10},{10,... | collective-permute-start | bytes 6152 | tf_op jit(solution)/shard_map/ppermute | solution.py:309
  59.7 3.6 %collective-permute-start.14 = (f32[1,512]{1,0:T(1,128)S(1)}, f32[1,512]{1,0:T(1,128)S(1)}, u32[]{:S(2)}, u32[]{:S(2)}) collective-permute-start(f32[1,512]{1,0:T(1,128)S(1)} %get-tuple-element.21), channel_id=1, source_target_pairs={{0,2},{1,3},{2,0},{3,1},{4,6},{5,7},{6,4},{7,5},{8,10},{9,11},{10,... | collective-permute-start | bytes 6152 | tf_op jit(solution)/shard_map/ppermute | solution.py:309
  61.0 2.3 %collective-permute-start.15 = (f32[1,512]{1,0:T(1,128)S(1)}, f32[1,512]{1,0:T(1,128)S(1)}, u32[]{:S(2)}, u32[]{:S(2)}) collective-permute-start(f32[1,512]{1,0:T(1,128)S(1)} %get-tuple-element.22), channel_id=1, source_target_pairs={{0,1},{1,0},{2,3},{3,2},{4,5},{5,4},{6,7},{7,6},{8,9},{9,8},{10,11... | collective-permute-start | bytes 6152 | tf_op jit(solution)/shard_map/ppermute | solution.py:309

commit v7 on v5

--- a/solution.py
+++ b/solution.py
@@ -16,7 +16,8 @@
 
 
 def gather_kernel(count, *refs):
-    blocks, out, plane, arrived = refs[:count], refs[count], refs[count + 1], refs[count + 2]
+    blocks = refs[:count]
+    out, turned, plane, arrived = refs[count:]
     rows = blocks[0].shape[0]
     copies, at = [], 0
     for j, block in enumerate(blocks):
@@ -24,21 +25,25 @@
         at += block.shape[0]
     for copy in copies:
         copy.start()
-    at = 0
-    for copy, block in zip(copies, blocks):
+    for copy in copies:
         copy.wait()
-        chunk = min(256, block.shape[0])
-        for first in range(at, at + block.shape[0], chunk):
-            out[first : first + chunk, :] = lax.dot_general(
-                plane[first : first + chunk, :],
-                plane[:rows, :],
-                (((1,), (1,)), ((), ())),
-                preferred_element_type=jnp.float32,
-            )
-        at += block.shape[0]
+    first_part = out.shape[1]
+    times_plane(plane.at[:rows, :], plane.at[:first_part, :], out)
+    chunk = min(256, rows)
+    for first in range(first_part, plane.shape[0], chunk):
+        turned[first - first_part : first - first_part + chunk, :] = lax.dot_general(
+            plane[first : first + chunk, :],
+            plane[:rows, :],
+            (((1,), (1,)), ((), ())),
+            preferred_element_type=jnp.float32,
+        )
 
 
 def product_kernel(moving, plane, after, out):
+    times_plane(moving, plane, out)
+
+
+def times_plane(moving, plane, out):
     chunk = min(256, moving.shape[0])
     for first in range(0, plane.shape[0], chunk):
         out[:, first : first + chunk] = lax.dot_general(
@@ -62,11 +67,12 @@
     return pl.pallas_call(
         functools.partial(gather_kernel, len(blocks)),
         out_shape=[
-            jax.ShapeDtypeStruct((others, rows), jnp.float32),
+            jax.ShapeDtypeStruct((rows, others // 2), jnp.float32),
+            jax.ShapeDtypeStruct((others - others // 2, rows), jnp.float32),
             jax.ShapeDtypeStruct((others, width), blocks[0].dtype),
         ],
         in_specs=[pl.BlockSpec(memory_space=pl.ANY)] * len(blocks),
-        out_specs=[vmem, vmem],
+        out_specs=[vmem] * 3,
         scratch_shapes=[pltpu.SemaphoreType.DMA((len(blocks),))],
         compiler_params=pltpu.CompilerParams(vmem_limit_bytes=4 * rows * others + 2 * others * width + VMEM_SPARE),
         cost_estimate=cost_of(rows, width, others),
@@ -96,8 +102,10 @@
 def classes_kernel(partners, told, raw, out, scale_down, cluster_down):
     count, rows = told.shape[0], raw.shape[1]
     strip = min(STRIP, rows)
-    for j in range(count):
-        here = slice(j * rows, (j + 1) * rows)
+    blocks = raw.shape[0] // rows
+    for i in range(blocks):
+        j = count - blocks + i
+        here = slice(i * rows, (i + 1) * rows)
         scale_down[here, :] = along_sublanes(told[j : j + 1, 0:rows])
         cluster_down[here, :] = along_sublanes(told[j : j + 1, rows : 2 * rows])
     offsets = range(-partners, partners + 1)
@@ -106,10 +114,7 @@
 
         def step(i, best):
             here = pl.ds(pl.multiple_of(i * strip, strip), strip)
-            down = lax.broadcasted_iota(jnp.int32, (strip, LANES), 0) + i * strip
-            across = lax.broadcasted_iota(jnp.int32, (strip, LANES), 1) + first
             value = raw[here, first : first + LANES] * scale_down[here, :]
-            value = jnp.where(down == across, LOWEST, value)
             ahead = cluster_down[here, :] - mine
             found = []
             for before, offset in zip(best, offsets):
@@ -140,7 +145,7 @@
 def maxima_kernel(partners, count, others, two_sided, device, told, own_classes, moving, plane, *refs):
     tiles = 1 + len(two_sided)
     distant, refs = refs[:others], refs[others:]
-    given = dict(zip(range(2, tiles), refs))
+    given = dict(zip([0, *range(2, tiles)], refs))
     row_outs = refs[len(given) : len(given) + count]
     column_outs = list(refs[len(given) + count : -2])
     fresh, column_best = refs[-2:]
@@ -173,8 +178,8 @@
     lane_scale = [told[j : j + 1, 0:rows] for j in range(count)]
     lane_ones = [ones_of(j) for j in range(count)]
     facts = [facts_of(r) for r in range(tiles)]
-    scale_down = {r: along_sublanes(facts[r][0]) for r in range(1, tiles)}
-    bits_down = {r: [along_sublanes(b) for b in bits_of(facts[r][1])] for r in range(1, tiles)}
+    scale_down = [along_sublanes(scales) for scales, _ in facts]
+    bits_down = [[along_sublanes(b) for b in bits_of(clusters)] for _, clusters in facts]
 
     def lanes_of(per, g):
         first = g % per_block * LANES
@@ -183,7 +188,8 @@
     row_part = {}
 
     def passed(r, c):
-        wants_column = two_sided[r - 1]
+        wants_row = r > 0
+        wants_column = r == 0 or two_sided[r - 1]
         for first in range(0, rows, strip):
             here = slice(first, first + strip)
             best = None
@@ -197,11 +203,18 @@
                 for w in range(1, words):
                     met = met | (bits_down[r][w][here] & lanes_of([o[w] for o in lane_ones], g))
                 keep = met != 0
-                value = jnp.where(keep, value * scale_down[r][here], LOWEST)
-                part = jnp.max(value.reshape(strip // SUBLANES, SUBLANES, LANES), axis=0)
-                row_part[g] = jnp.maximum(row_part[g], part) if g in row_part else part
-                if wants_column:
-                    value = value * lanes_of(lane_scale, g)
+                if r == 0 and g < per_block and g * LANES < first + strip and first < (g + 1) * LANES:
+                    down = lax.broadcasted_iota(jnp.int32, value.shape, 0) + first
+                    across = lax.broadcasted_iota(jnp.int32, value.shape, 1) + g * LANES
+                    keep = keep & (down != across)
+                if wants_row:
+                    value = jnp.where(keep, value * scale_down[r][here], LOWEST)
+                    part = jnp.max(value.reshape(strip // SUBLANES, SUBLANES, LANES), axis=0)
+                    row_part[g] = jnp.maximum(row_part[g], part) if g in row_part else part
+                    if wants_column:
+                        value = value * lanes_of(lane_scale, g)
+                else:
+                    value = jnp.where(keep, value * lanes_of(lane_scale, g), LOWEST)
                 if wants_column:
                     best = value if best is None else jnp.maximum(best, value)
             if wants_column:
@@ -216,7 +229,8 @@
                 preferred_element_type=jnp.float32,
             )
             for r in given:
-                passed(r, c)
+                if c * chunk < given[r].shape[1]:
+                    passed(r, c)
         if c > 0:
             passed(1, c - 1)
 
@@ -226,8 +240,8 @@
     for r in range(1, tiles):
         if two_sided[r - 1]:
             column_outs.pop(0)[...] = column_of(r)
+    own_best = column_of(0)
     own_bits = bits_of(facts[0][1])
-    own_best = jnp.full((1, rows), LOWEST, jnp.float32)
     named = facts[0][1].astype(jnp.int32)
     for k in range(2 * partners + 1):
         met = jnp.int32(0)
@@ -401,14 +415,14 @@
         mine = pieces[0] if len(pieces) == 1 else jnp.concatenate(pieces, axis=0)
         pieces.append(permuted(mine, across(bit)))
         bit *= 2
-    raw, whole = gathered_plane(blocks)
+    raw, turned, whole = gathered_plane(blocks)
     told, packed = joined(pieces, rows, raw)
     distant = [permuted(packed, along(t)) for t in range(1, planes)]
     device = device_table(shards, plane, planes, order, place_of, here)
     distances = range(1, half + 1)
     two_sided = [2 * distance != planes for distance in distances]
-    own_classes = classes(told, raw, partners)
-    given = [products(arrived[distance], whole, own_classes) for distance in distances[1:]]
+    own_classes = classes(told, turned, partners)
+    given = [raw] + [products(arrived[distance], whole, own_classes) for distance in distances[1:]]
     found = maxima(device, told, own_classes, distant, partners, arrived[1], whole, given, two_sided)
     gathered, columns = found[:plane], list(found[plane:])
 

time: 64.5 us -> 63.7 us (0.988)
  Pallas kernels: 16.9 us -> 13.7 us
  waiting for transfers between devices: 21.6 us -> 23 us
  starting transfers between devices: 16.7 us -> 17.7 us
    pallas_call x1, Pallas kernels: 6.77 us -> 3.35 us  [classes(): pl.pallas_call(functools.partial(classes_kernel, partners), out_shape=jax...]
    ppermute x16, waiting for transfers between devices: 21.6 us -> 23 us  [permuted(): return lax.ppermute(value, 'shard', [(s, target(s)) for s in range(shards)])]
    ppermute x16, starting transfers between devices: 16.7 us -> 17.7 us  [permuted(): return lax.ppermute(value, 'shard', [(s, target(s)) for s in range(shards)])]
  transfers between devices with their start and end apart: 16 -> 16, of which waited for: 6 -> 7; matrix products, arithmetic and copies ran while one was open for 11% -> 11% of each run, Pallas kernels for 20% -> 15%
where the time goes in v7:
time: 63.7 us; the launch traced here: 63.4 us
  waiting for transfers between devices  23 us (36%)
  starting transfers between devices  17.7 us (28%)
  Pallas kernels  13.7 us (22%)
  other arithmetic  5.33 us (8%)
  local copies, waits for them, and re-layouts  3.58 us (6%)
    ppermute x16, waiting for transfers between devices, permuted(): return lax.ppermute(value, 'shard', [(s, target(s)) for s in range(shards)])  23 us
    ppermute x16, starting transfers between devices, permuted(): return lax.ppermute(value, 'shard', [(s, target(s)) for s in range(shards)])  17.7 us
    pallas_call x1, Pallas kernels, gathered_plane(): pl.pallas_call(functools.partial(gather_kernel, len(blocks)), out_shape=[...  4.01 us
    pallas_call x1, Pallas kernels, maxima(): pl.pallas_call(functools.partial(maxima_kernel, partners, count, len(dist...  3.94 us
    pallas_call x1, Pallas kernels, classes(): pl.pallas_call(functools.partial(classes_kernel, partners), out_shape=jax...  3.35 us
    pallas_call x1, Pallas kernels, products(): pl.pallas_call(product_kernel, out_shape=jax.ShapeDtypeStruct((rows, othe...  2.38 us
    slice x1, local copies, waits for them, and re-layouts, per_device(): held = {(0, p): embeddings[p * size:(p + 1) * size] for p in range(parts)}  2.26 us
    reduce_sum x1, other arithmetic, device_table(): jnp.sum(jnp.where(jnp.arange(planes) == here // plane, jnp.asarray(place_...  1.3 us
  transfers between devices with their start and end apart: 16, of which 7 were waited for; matrix products, arithmetic and copies ran while one was open for 11% of the time, Pallas kernels for 15%

profile of v7, /device:TPU:0, one launch (start us, length us, event | category | flops | bytes accessed | tf_op | source)
XLA Modules:
  0.0 63.4 jit_solution(737835401587673148)
XLA Ops:
  0.5 2.6 %collective-permute-start.11 = (bf16[512,1024]{1,0:T(8,128)(2,1)}, bf16[512,1024]{1,0:T(8,128)(2,1)S(1)}, u32[]{:S(2)}, u32[]{:S(2)}) collective-permute-start(bf16[512,1024]{1,0:T(8,128)(2,1)} %refs_0_.1), channel_id=1, source_target_pairs={{0,4},{1,5},{2,6},{3,7},{4,0},{5,1},{6,2},{7,3},{8,12},{9,13},{10,... | collective-permute-start | bytes 3145736 | tf_op jit(solution)/shard_map/ppermute | solution.py:379
  3.0 2.6 %collective-permute-start.7 = (bf16[512,1024]{1,0:T(8,128)(2,1)}, bf16[512,1024]{1,0:T(8,128)(2,1)S(1)}, u32[]{:S(2)}, u32[]{:S(2)}) collective-permute-start(bf16[512,1024]{1,0:T(8,128)(2,1)} %refs_0_.1), channel_id=1, source_target_pairs={{0,8},{1,9},{2,10},{3,11},{4,12},{5,13},{6,14},{7,15},{8,4},{9,5},... | collective-permute-start | bytes 3145736 | tf_op jit(solution)/shard_map/ppermute | solution.py:379
  5.6 2.3 %fusion.8 = (bf16[256,1024]{1,0:T(8,128)(2,1)}, bf16[256,1024]{1,0:T(8,128)(2,1)}) fusion(bf16[512,1024]{1,0:T(8,128)(2,1)} %refs_0_.1), kind=kLoop, calls=%fused_computation.26 | loop fusion | bytes 2097152 | tf_op jit(solution)/shard_map/slice | solution.py:396
  7.9 1.5 %collective-permute-start = (bf16[256,1024]{1,0:T(8,128)(2,1)}, bf16[256,1024]{1,0:T(8,128)(2,1)S(1)}, u32[]{:S(2)}, u32[]{:S(2)}) collective-permute-start(bf16[256,1024]{1,0:T(8,128)(2,1)} %get-tuple-element.26), channel_id=1, source_target_pairs={{0,2},{1,3},{2,0},{3,1},{4,6},{5,7},{6,4},{7,5},{8,10},{9,11},{10,... | collective-permute-start | bytes 1572872 | tf_op jit(solution)/shard_map/ppermute | solution.py:379
  10.6 0.7 %convert_element_type.18 = f32[512,1]{0,1:T(1,128)S(1)} convert(s32[512,1]{0,1:T(1,128)} %param.8) | non-fusion elementwise | flops 512 | bytes 4096 | tf_op jit(solution)/shard_map/convert_element_type | solution.py:411
  11.2 0.7 %convert_element_type.17 = f32[512]{0:T(512)S(1)} convert(bf16[512]{0:T(512)(128)(2,1)} %param.7) | non-fusion elementwise | flops 512 | bytes 3072 | tf_op jit(solution)/shard_map/convert_element_type | solution.py:411
  12.0 1.3 %fusion.6 = s32[]{:T(128)} fusion(s32[4]{0:T(128)} %constant.61.clone, s32[]{:T(128)S(6)} %select_n.49), kind=kLoop, calls=%fused_computation.22 | loop fusion | flops 11 | bytes 24 | tf_op jit(solution)/shard_map/reduce_sum | solution.py:358
  13.9 9.0 %collective-permute-done.after.refs_2_ = bf16[256,1024]{1,0:T(8,128)(2,1)S(1)} collective-permute-done((bf16[256,1024]{1,0:T(8,128)(2,1)}, bf16[256,1024]{1,0:T(8,128)(2,1)S(1)}, u32[]{:S(2)}, u32[]{:S(2)}) %collective-permute-start) | collective-permute-done | bytes 524320 | tf_op jit(solution)/shard_map/ppermute | solution.py:379
  22.9 0.7 %select_reduce_fusion = s32[16]{0:T(128)S(1)} fusion(s32[4]{0:T(128)} %constant.61.clone, s32[16]{0:T(128)S(1)} %and_select_fusion), kind=kLoop, calls=%fused_computation.13 | loop fusion | flops 176 | bytes 144 | tf_op jit(solution)/shard_map/reduce_sum | solution.py:360
  23.6 9.5 %collective-permute-done.4.refs_3_ = bf16[256,1024]{1,0:T(8,128)(2,1)S(1)} collective-permute-done((bf16[256,1024]{1,0:T(8,128)(2,1)}, bf16[256,1024]{1,0:T(8,128)(2,1)S(1)}, u32[]{:S(2)}, u32[]{:S(2)}) %collective-permute-start.4) | collective-permute-done | bytes 524320 | tf_op jit(solution)/shard_map/ppermute | solution.py:379
  33.7 1.4 %collective-permute-done.5.refs_4_ = bf16[256,1024]{1,0:T(8,128)(2,1)} collective-permute-done((bf16[256,1024]{1,0:T(8,128)(2,1)S(1)}, bf16[256,1024]{1,0:T(8,128)(2,1)}, u32[]{:S(2)}, u32[]{:S(2)}) %collective-permute-start.5) | collective-permute-done | bytes 524320 | tf_op jit(solution)/shard_map/ppermute | solution.py:379
  35.1 1.5 %collective-permute-start.2 = (f32[2,1152]{1,0:T(2,128)S(1)}, f32[2,1152]{1,0:T(2,128)S(1)}, u32[]{:S(2)}, u32[]{:S(2)}) collective-permute-start(f32[2,1152]{1,0:T(2,128)S(1)} %pad_maximum_fusion), channel_id=1, source_target_pairs={{0,2},{1,3},{2,0},{3,1},{4,6},{5,7},{6,4},{7,5},{8,10},{9,11},{10,... | collective-permute-start | bytes 27656 | tf_op jit(solution)/shard_map/ppermute | solution.py:379
  36.7 1.2 %copy-done = bf16[512,1024]{1,0:T(8,128)(2,1)S(1)} copy-done((bf16[512,1024]{1,0:T(8,128)(2,1)S(1)}, bf16[512,1024]{1,0:T(8,128)(2,1)}, u32[]{:S(2)}) %copy-start) | copy-done | bytes 1048600
  37.9 4.0 %shard_map.65 = (f32[512,1024]{1,0:T(8,128)S(1)}, f32[1024,512]{1,0:T(8,128)S(1)}, bf16[2048,1024]{1,0:T(8,128)(2,1)S(1)}) custom-call(bf16[512,1024]{1,0:T(8,128)(2,1)S(1)} %copy-done, bf16[512,1024]{1,0:T(8,128)(2,1)} %collective-permute-done.3.refs_1_, bf16[256,1024]{1,0:T(8,128)(2,1)S(1)} %collective-permute-done.after.refs_2_, ...), custom_call_target="tpu_custom_call" | custom-call | flops 2147483648 | bytes 5242880 | tf_op jit(solution)/shard_map/pallas_call | solution.py:67
  41.9 1.3 %collective-permute-start.10 = (f32[4,384]{1,0:T(4,128)S(1)}, f32[4,384]{1,0:T(4,128)S(1)}, u32[]{:S(2)}, u32[]{:S(2)}) collective-permute-start(f32[4,384]{1,0:T(4,128)S(1)} %get-tuple-element.19), channel_id=1, source_target_pairs={{0,12},{1,13},{2,14},{3,15},{4,8},{5,9},{6,10},{7,11},{8,0},{9,1},... | collective-permute-start | bytes 18440 | tf_op jit(solution)/shard_map/ppermute | solution.py:379
  43.2 1.7 %collective-permute-start.8 = (f32[4,384]{1,0:T(4,128)S(1)}, f32[4,384]{1,0:T(4,128)S(1)}, u32[]{:S(2)}, u32[]{:S(2)}) collective-permute-start(f32[4,384]{1,0:T(4,128)S(1)} %get-tuple-element.19), channel_id=1, source_target_pairs={{0,8},{1,9},{2,10},{3,11},{4,12},{5,13},{6,14},{7,15},{8,4},{9,5},... | collective-permute-start | bytes 18440 | tf_op jit(solution)/shard_map/ppermute | solution.py:379
  45.4 3.3 %shard_map.67.after.own_classes = f32[11,512]{1,0:T(8,128)S(1)} custom-call(f32[4,1152]{1,0:T(4,128)S(1)} %get-tuple-element.16.told, f32[1024,512]{1,0:T(8,128)S(1)} %get-tuple-element.17.raw), custom_call_target="tpu_custom_call" | custom-call | tf_op jit(solution)/shard_map/pallas_call | solution.py:135
  48.7 2.4 %shard_map.68.refs_4_ = f32[512,2048]{1,0:T(8,128)S(1)} custom-call(bf16[512,1024]{1,0:T(8,128)(2,1)S(1)} %collective-permute-done.11.moving, bf16[2048,1024]{1,0:T(8,128)(2,1)S(1)} %get-tuple-element.18.plane, f32[11,512]{1,0:T(8,128)S(1)} %shard_map.67.after.own_classes), custom_call_target="tpu_custom_call" | custom-call | flops 2147483648 | bytes 5242880 | tf_op jit(solution)/shard_map/pallas_call | solution.py:86
  51.1 0.9 %collective-permute-done.7.moving = bf16[512,1024]{1,0:T(8,128)(2,1)S(1)} collective-permute-done((bf16[512,1024]{1,0:T(8,128)(2,1)}, bf16[512,1024]{1,0:T(8,128)(2,1)S(1)}, u32[]{:S(2)}, u32[]{:S(2)}) %collective-permute-start.7) | collective-permute-done | bytes 1048608 | tf_op jit(solution)/shard_map/ppermute | solution.py:379
  52.3 3.9 %shard_map.69 = (f32[1,512]{1,0:T(1,128)S(1)}, f32[1,512]{1,0:T(1,128)S(1)}, f32[1,512]{1,0:T(1,128)S(1)}, f32[1,512]{1,0:T(1,128)S(1)}, f32[1,512]{1,0:T(1,128)S(1)}) custom-call(s32[16,1]{1,0:T(8,128)S(1)} %fusion.1.device, f32[4,1152]{1,0:T(4,128)S(1)} %get-tuple-element.16.told, f32[11,512]{1,0:T(8,128)S(1)} %shard_map.67.after.own_classes, ...), custom_call_target="tpu_custom_call" | custom-call | flops 2147483648 | bytes 5242880 | tf_op jit(solution)/shard_map/pallas_call | solution.py:269
  56.2 2.7 %collective-permute-start.12 = (f32[1,512]{1,0:T(1,128)S(1)}, f32[1,512]{1,0:T(1,128)S(1)}, u32[]{:S(2)}, u32[]{:S(2)}) collective-permute-start(f32[1,512]{1,0:T(1,128)S(1)} %get-tuple-element.21), channel_id=1, source_target_pairs={{0,12},{1,13},{2,14},{3,15},{4,8},{5,9},{6,10},{7,11},{8,0},{9,1},... | collective-permute-start | bytes 6152 | tf_op jit(solution)/shard_map/ppermute | solution.py:379
  59.2 1.3 %collective-permute-start.14 = (f32[1,512]{1,0:T(1,128)S(1)}, f32[1,512]{1,0:T(1,128)S(1)}, u32[]{:S(2)}, u32[]{:S(2)}) collective-permute-start(f32[1,512]{1,0:T(1,128)S(1)} %get-tuple-element.23), channel_id=1, source_target_pairs={{0,2},{1,3},{2,0},{3,1},{4,6},{5,7},{6,4},{7,5},{8,10},{9,11},{10,... | collective-permute-start | bytes 6152 | tf_op jit(solution)/shard_map/ppermute | solution.py:379
  60.8 1.1 %collective-permute-done.13 = f32[1,512]{1,0:T(1,128)S(1)} collective-permute-done((f32[1,512]{1,0:T(1,128)S(1)}, f32[1,512]{1,0:T(1,128)S(1)}, u32[]{:S(2)}, u32[]{:S(2)}) %collective-permute-start.13) | collective-permute-done | bytes 2080 | tf_op jit(solution)/shard_map/ppermute | solution.py:379
  62.0 0.8 %collective-permute-done.14 = f32[1,512]{1,0:T(1,128)S(1)} collective-permute-done((f32[1,512]{1,0:T(1,128)S(1)}, f32[1,512]{1,0:T(1,128)S(1)}, u32[]{:S(2)}, u32[]{:S(2)}) %collective-permute-start.14) | collective-permute-done | bytes 2080 | tf_op jit(solution)/shard_map/ppermute | solution.py:379
  (30 shorter events, 4.8 us)
Async XLA Ops:
  0.0 36.7 %collective-permute-start.3 = (bf16[512,1024]{1,0:T(8,128)(2,1)}, bf16[512,1024]{1,0:T(8,128)(2,1)}, u32[]{:S(2)}, u32[]{:S(2)}) collective-permute-start(bf16[512,1024]{1,0:T(8,128)(2,1)} %refs_0_.1), channel_id=1, source_target_pairs={{0,1},{1,0},{2,3},{3,2},{4,5},{5,4},{6,7},{7,6},{8,9},{9,8},{10,11... | collective-permute-start | bytes 3145736 | tf_op jit(solution)/shard_map/ppermute | solution.py:379
  0.5 48.3 %collective-permute-start.11 = (bf16[512,1024]{1,0:T(8,128)(2,1)}, bf16[512,1024]{1,0:T(8,128)(2,1)S(1)}, u32[]{:S(2)}, u32[]{:S(2)}) collective-permute-start(bf16[512,1024]{1,0:T(8,128)(2,1)} %refs_0_.1), channel_id=1, source_target_pairs={{0,4},{1,5},{2,6},{3,7},{4,0},{5,1},{6,2},{7,3},{8,12},{9,13},{10,... | collective-permute-start | bytes 3145736 | tf_op jit(solution)/shard_map/ppermute | solution.py:379
  3.0 49.0 %collective-permute-start.7 = (bf16[512,1024]{1,0:T(8,128)(2,1)}, bf16[512,1024]{1,0:T(8,128)(2,1)S(1)}, u32[]{:S(2)}, u32[]{:S(2)}) collective-permute-start(bf16[512,1024]{1,0:T(8,128)(2,1)} %refs_0_.1), channel_id=1, source_target_pairs={{0,8},{1,9},{2,10},{3,11},{4,12},{5,13},{6,14},{7,15},{8,4},{9,5},... | collective-permute-start | bytes 3145736 | tf_op jit(solution)/shard_map/ppermute | solution.py:379
  7.9 15.0 %collective-permute-start = (bf16[256,1024]{1,0:T(8,128)(2,1)}, bf16[256,1024]{1,0:T(8,128)(2,1)S(1)}, u32[]{:S(2)}, u32[]{:S(2)}) collective-permute-start(bf16[256,1024]{1,0:T(8,128)(2,1)} %get-tuple-element.26), channel_id=1, source_target_pairs={{0,2},{1,3},{2,0},{3,1},{4,6},{5,7},{6,4},{7,5},{8,10},{9,11},{10,... | collective-permute-start | bytes 1572872 | tf_op jit(solution)/shard_map/ppermute | solution.py:379
  9.4 23.7 %collective-permute-start.4 = (bf16[256,1024]{1,0:T(8,128)(2,1)}, bf16[256,1024]{1,0:T(8,128)(2,1)S(1)}, u32[]{:S(2)}, u32[]{:S(2)}) collective-permute-start(bf16[256,1024]{1,0:T(8,128)(2,1)} %get-tuple-element.25), channel_id=1, source_target_pairs={{0,2},{1,3},{2,0},{3,1},{4,6},{5,7},{6,4},{7,5},{8,10},{9,11},{10,... | collective-permute-start | bytes 1572872 | tf_op jit(solution)/shard_map/ppermute | solution.py:379
  22.9 10.2 %collective-permute-start.1 = (f32[1,1152]{1,0:T(1,128)S(1)}, f32[1,1152]{1,0:T(1,128)S(1)}, u32[]{:S(2)}, u32[]{:S(2)}) collective-permute-start(f32[1,1152]{1,0:T(1,128)S(1)} %shard_map.64.refs_0_), channel_id=1, source_target_pairs={{0,1},{1,0},{2,3},{3,2},{4,5},{5,4},{6,7},{7,6},{8,9},{9,8},{10,11... | collective-permute-start | bytes 13832 | tf_op jit(solution)/shard_map/ppermute | solution.py:379
  33.1 2.0 %collective-permute-start.5 = (bf16[256,1024]{1,0:T(8,128)(2,1)S(1)}, bf16[256,1024]{1,0:T(8,128)(2,1)}, u32[]{:S(2)}, u32[]{:S(2)}) collective-permute-start(bf16[256,1024]{1,0:T(8,128)(2,1)S(1)} %collective-permute-done.after.refs_2_), channel_id=1, source_target_pairs={{0,1},{1,0},{2,3},{3,2},{4,5},{5,4},{6,7},{7,6},{8,9},{9,8},{10,11... | collective-permute-start | bytes 1572872 | tf_op jit(solution)/shard_map/ppermute | solution.py:379
  33.1 3.6 %collective-permute-start.6 = (bf16[256,1024]{1,0:T(8,128)(2,1)S(1)}, bf16[256,1024]{1,0:T(8,128)(2,1)}, u32[]{:S(2)}, u32[]{:S(2)}) collective-permute-start(bf16[256,1024]{1,0:T(8,128)(2,1)S(1)} %collective-permute-done.4.refs_3_), channel_id=1, source_target_pairs={{0,1},{1,0},{2,3},{3,2},{4,5},{5,4},{6,7},{7,6},{8,9},{9,8},{10,11... | collective-permute-start | bytes 1572872 | tf_op jit(solution)/shard_map/ppermute | solution.py:379
  35.1 6.8 %collective-permute-start.2 = (f32[2,1152]{1,0:T(2,128)S(1)}, f32[2,1152]{1,0:T(2,128)S(1)}, u32[]{:S(2)}, u32[]{:S(2)}) collective-permute-start(f32[2,1152]{1,0:T(2,128)S(1)} %pad_maximum_fusion), channel_id=1, source_target_pairs={{0,2},{1,3},{2,0},{3,1},{4,6},{5,7},{6,4},{7,5},{8,10},{9,11},{10,... | collective-permute-start | bytes 27656 | tf_op jit(solution)/shard_map/ppermute | solution.py:379
  36.7 1.2 %copy-start = (bf16[512,1024]{1,0:T(8,128)(2,1)S(1)}, bf16[512,1024]{1,0:T(8,128)(2,1)}, u32[]{:S(2)}) copy-start(bf16[512,1024]{1,0:T(8,128)(2,1)} %refs_0_.1) | copy-start | bytes 3145732
  41.9 10.3 %collective-permute-start.10 = (f32[4,384]{1,0:T(4,128)S(1)}, f32[4,384]{1,0:T(4,128)S(1)}, u32[]{:S(2)}, u32[]{:S(2)}) collective-permute-start(f32[4,384]{1,0:T(4,128)S(1)} %get-tuple-element.19), channel_id=1, source_target_pairs={{0,12},{1,13},{2,14},{3,15},{4,8},{5,9},{6,10},{7,11},{8,0},{9,1},... | collective-permute-start | bytes 18440 | tf_op jit(solution)/shard_map/ppermute | solution.py:379
  43.2 9.0 %collective-permute-start.8 = (f32[4,384]{1,0:T(4,128)S(1)}, f32[4,384]{1,0:T(4,128)S(1)}, u32[]{:S(2)}, u32[]{:S(2)}) collective-permute-start(f32[4,384]{1,0:T(4,128)S(1)} %get-tuple-element.19), channel_id=1, source_target_pairs={{0,8},{1,9},{2,10},{3,11},{4,12},{5,13},{6,14},{7,15},{8,4},{9,5},... | collective-permute-start | bytes 18440 | tf_op jit(solution)/shard_map/ppermute | solution.py:379
  44.9 7.3 %collective-permute-start.9 = (f32[4,384]{1,0:T(4,128)S(1)}, f32[4,384]{1,0:T(4,128)S(1)}, u32[]{:S(2)}, u32[]{:S(2)}) collective-permute-start(f32[4,384]{1,0:T(4,128)S(1)} %get-tuple-element.19), channel_id=1, source_target_pairs={{0,4},{1,5},{2,6},{3,7},{4,0},{5,1},{6,2},{7,3},{8,12},{9,13},{10,... | collective-permute-start | bytes 18440 | tf_op jit(solution)/shard_map/ppermute | solution.py:379
  56.2 4.6 %collective-permute-start.12 = (f32[1,512]{1,0:T(1,128)S(1)}, f32[1,512]{1,0:T(1,128)S(1)}, u32[]{:S(2)}, u32[]{:S(2)}) collective-permute-start(f32[1,512]{1,0:T(1,128)S(1)} %get-tuple-element.21), channel_id=1, source_target_pairs={{0,12},{1,13},{2,14},{3,15},{4,8},{5,9},{6,10},{7,11},{8,0},{9,1},... | collective-permute-start | bytes 6152 | tf_op jit(solution)/shard_map/ppermute | solution.py:379
  59.0 3.0 %collective-permute-start.13 = (f32[1,512]{1,0:T(1,128)S(1)}, f32[1,512]{1,0:T(1,128)S(1)}, u32[]{:S(2)}, u32[]{:S(2)}) collective-permute-start(f32[1,512]{1,0:T(1,128)S(1)} %get-tuple-element.22), channel_id=1, source_target_pairs={{0,3},{1,2},{2,1},{3,0},{4,7},{5,6},{6,5},{7,4},{8,11},{9,10},{10,... | collective-permute-start | bytes 6152 | tf_op jit(solution)/shard_map/ppermute | solution.py:379
  59.2 3.6 %collective-permute-start.14 = (f32[1,512]{1,0:T(1,128)S(1)}, f32[1,512]{1,0:T(1,128)S(1)}, u32[]{:S(2)}, u32[]{:S(2)}) collective-permute-start(f32[1,512]{1,0:T(1,128)S(1)} %get-tuple-element.23), channel_id=1, source_target_pairs={{0,2},{1,3},{2,0},{3,1},{4,6},{5,7},{6,4},{7,5},{8,10},{9,11},{10,... | collective-permute-start | bytes 6152 | tf_op jit(solution)/shard_map/ppermute | solution.py:379
  60.5 2.3 %collective-permute-start.15 = (f32[1,512]{1,0:T(1,128)S(1)}, f32[1,512]{1,0:T(1,128)S(1)}, u32[]{:S(2)}, u32[]{:S(2)}) collective-permute-start(f32[1,512]{1,0:T(1,128)S(1)} %get-tuple-element.24), channel_id=1, source_target_pairs={{0,1},{1,0},{2,3},{3,2},{4,5},{5,4},{6,7},{7,6},{8,9},{9,8},{10,11... | collective-permute-start | bytes 6152 | tf_op jit(solution)/shard_map/ppermute | solution.py:379

commit v8 on v7

--- a/solution.py
+++ b/solution.py
@@ -25,10 +25,15 @@
         at += block.shape[0]
     for copy in copies:
         copy.start()
-    for copy in copies:
-        copy.wait()
     first_part = out.shape[1]
+    starts = [sum(block.shape[0] for block in blocks[:j]) for j in range(count)]
+    for copy, start in zip(copies, starts):
+        if start < first_part:
+            copy.wait()
     times_plane(plane.at[:rows, :], plane.at[:first_part, :], out)
+    for copy, start in zip(copies, starts):
+        if start >= first_part:
+            copy.wait()
     chunk = min(256, rows)
     for first in range(first_part, plane.shape[0], chunk):
         turned[first - first_part : first - first_part + chunk, :] = lax.dot_general(

time: 63.7 us -> 63.7 us (level)
  no operation moved by 1% of the time
where the time goes in v8:
time: 63.7 us; the launch traced here: 63.4 us
  waiting for transfers between devices  23.1 us (36%)
  starting transfers between devices  17.7 us (28%)
  Pallas kernels  13.6 us (21%)
  other arithmetic  5.33 us (8%)
  local copies, waits for them, and re-layouts  3.58 us (6%)
    ppermute x16, waiting for transfers between devices, permuted(): return lax.ppermute(value, 'shard', [(s, target(s)) for s in range(shards)])  23.1 us
    ppermute x16, starting transfers between devices, permuted(): return lax.ppermute(value, 'shard', [(s, target(s)) for s in range(shards)])  17.7 us
    pallas_call x1, Pallas kernels, maxima(): pl.pallas_call(functools.partial(maxima_kernel, partners, count, len(dist...  3.94 us
    pallas_call x1, Pallas kernels, gathered_plane(): pl.pallas_call(functools.partial(gather_kernel, len(blocks)), out_shape=[...  3.92 us
    pallas_call x1, Pallas kernels, classes(): pl.pallas_call(functools.partial(classes_kernel, partners), out_shape=jax...  3.35 us
    pallas_call x1, Pallas kernels, products(): pl.pallas_call(product_kernel, out_shape=jax.ShapeDtypeStruct((rows, othe...  2.38 us
    slice x1, local copies, waits for them, and re-layouts, per_device(): held = {(0, p): embeddings[p * size:(p + 1) * size] for p in range(parts)}  2.26 us
    reduce_sum x1, other arithmetic, device_table(): jnp.sum(jnp.where(jnp.arange(planes) == here // plane, jnp.asarray(place_...  1.3 us
  transfers between devices with their start and end apart: 16, of which 7 were waited for; matrix products, arithmetic and copies ran while one was open for 11% of the time, Pallas kernels for 15%

profile of v8, /device:TPU:0, one launch (start us, length us, event | category | flops | bytes accessed | tf_op | source)
XLA Modules:
  0.0 63.4 jit_solution(8629029690177305264)
XLA Ops:
  0.5 2.6 %collective-permute-start.11 = (bf16[512,1024]{1,0:T(8,128)(2,1)}, bf16[512,1024]{1,0:T(8,128)(2,1)S(1)}, u32[]{:S(2)}, u32[]{:S(2)}) collective-permute-start(bf16[512,1024]{1,0:T(8,128)(2,1)} %refs_0_.1), channel_id=1, source_target_pairs={{0,4},{1,5},{2,6},{3,7},{4,0},{5,1},{6,2},{7,3},{8,12},{9,13},{10,... | collective-permute-start | bytes 3145736 | tf_op jit(solution)/shard_map/ppermute | solution.py:384
  3.0 2.6 %collective-permute-start.7 = (bf16[512,1024]{1,0:T(8,128)(2,1)}, bf16[512,1024]{1,0:T(8,128)(2,1)S(1)}, u32[]{:S(2)}, u32[]{:S(2)}) collective-permute-start(bf16[512,1024]{1,0:T(8,128)(2,1)} %refs_0_.1), channel_id=1, source_target_pairs={{0,8},{1,9},{2,10},{3,11},{4,12},{5,13},{6,14},{7,15},{8,4},{9,5},... | collective-permute-start | bytes 3145736 | tf_op jit(solution)/shard_map/ppermute | solution.py:384
  5.6 2.3 %fusion.8 = (bf16[256,1024]{1,0:T(8,128)(2,1)}, bf16[256,1024]{1,0:T(8,128)(2,1)}) fusion(bf16[512,1024]{1,0:T(8,128)(2,1)} %refs_0_.1), kind=kLoop, calls=%fused_computation.26 | loop fusion | bytes 2097152 | tf_op jit(solution)/shard_map/slice | solution.py:401
  7.9 1.5 %collective-permute-start = (bf16[256,1024]{1,0:T(8,128)(2,1)}, bf16[256,1024]{1,0:T(8,128)(2,1)S(1)}, u32[]{:S(2)}, u32[]{:S(2)}) collective-permute-start(bf16[256,1024]{1,0:T(8,128)(2,1)} %get-tuple-element.26), channel_id=1, source_target_pairs={{0,2},{1,3},{2,0},{3,1},{4,6},{5,7},{6,4},{7,5},{8,10},{9,11},{10,... | collective-permute-start | bytes 1572872 | tf_op jit(solution)/shard_map/ppermute | solution.py:384
  10.6 0.7 %convert_element_type.18 = f32[512,1]{0,1:T(1,128)S(1)} convert(s32[512,1]{0,1:T(1,128)} %param.8) | non-fusion elementwise | flops 512 | bytes 4096 | tf_op jit(solution)/shard_map/convert_element_type | solution.py:416
  11.2 0.7 %convert_element_type.17 = f32[512]{0:T(512)S(1)} convert(bf16[512]{0:T(512)(128)(2,1)} %param.7) | non-fusion elementwise | flops 512 | bytes 3072 | tf_op jit(solution)/shard_map/convert_element_type | solution.py:416
  12.0 1.3 %fusion.6 = s32[]{:T(128)} fusion(s32[4]{0:T(128)} %constant.61.clone, s32[]{:T(128)S(6)} %select_n.49), kind=kLoop, calls=%fused_computation.22 | loop fusion | flops 11 | bytes 24 | tf_op jit(solution)/shard_map/reduce_sum | solution.py:363
  13.9 9.0 %collective-permute-done.after.refs_2_ = bf16[256,1024]{1,0:T(8,128)(2,1)S(1)} collective-permute-done((bf16[256,1024]{1,0:T(8,128)(2,1)}, bf16[256,1024]{1,0:T(8,128)(2,1)S(1)}, u32[]{:S(2)}, u32[]{:S(2)}) %collective-permute-start) | collective-permute-done | bytes 524320 | tf_op jit(solution)/shard_map/ppermute | solution.py:384
  22.9 0.7 %select_reduce_fusion = s32[16]{0:T(128)S(1)} fusion(s32[4]{0:T(128)} %constant.61.clone, s32[16]{0:T(128)S(1)} %and_select_fusion), kind=kLoop, calls=%fused_computation.13 | loop fusion | flops 176 | bytes 144 | tf_op jit(solution)/shard_map/reduce_sum | solution.py:365
  23.6 9.5 %collective-permute-done.4.refs_3_ = bf16[256,1024]{1,0:T(8,128)(2,1)S(1)} collective-permute-done((bf16[256,1024]{1,0:T(8,128)(2,1)}, bf16[256,1024]{1,0:T(8,128)(2,1)S(1)}, u32[]{:S(2)}, u32[]{:S(2)}) %collective-permute-start.4) | collective-permute-done | bytes 524320 | tf_op jit(solution)/shard_map/ppermute | solution.py:384
  33.7 1.4 %collective-permute-done.5.refs_4_ = bf16[256,1024]{1,0:T(8,128)(2,1)} collective-permute-done((bf16[256,1024]{1,0:T(8,128)(2,1)S(1)}, bf16[256,1024]{1,0:T(8,128)(2,1)}, u32[]{:S(2)}, u32[]{:S(2)}) %collective-permute-start.5) | collective-permute-done | bytes 524320 | tf_op jit(solution)/shard_map/ppermute | solution.py:384
  35.1 1.5 %collective-permute-start.2 = (f32[2,1152]{1,0:T(2,128)S(1)}, f32[2,1152]{1,0:T(2,128)S(1)}, u32[]{:S(2)}, u32[]{:S(2)}) collective-permute-start(f32[2,1152]{1,0:T(2,128)S(1)} %pad_maximum_fusion), channel_id=1, source_target_pairs={{0,2},{1,3},{2,0},{3,1},{4,6},{5,7},{6,4},{7,5},{8,10},{9,11},{10,... | collective-permute-start | bytes 27656 | tf_op jit(solution)/shard_map/ppermute | solution.py:384
  36.7 1.2 %copy-done = bf16[512,1024]{1,0:T(8,128)(2,1)S(1)} copy-done((bf16[512,1024]{1,0:T(8,128)(2,1)S(1)}, bf16[512,1024]{1,0:T(8,128)(2,1)}, u32[]{:S(2)}) %copy-start) | copy-done | bytes 1048600
  37.9 3.9 %shard_map.65 = (f32[512,1024]{1,0:T(8,128)S(1)}, f32[1024,512]{1,0:T(8,128)S(1)}, bf16[2048,1024]{1,0:T(8,128)(2,1)S(1)}) custom-call(bf16[512,1024]{1,0:T(8,128)(2,1)S(1)} %copy-done, bf16[512,1024]{1,0:T(8,128)(2,1)} %collective-permute-done.3.refs_1_, bf16[256,1024]{1,0:T(8,128)(2,1)S(1)} %collective-permute-done.after.refs_2_, ...), custom_call_target="tpu_custom_call" | custom-call | flops 2147483648 | bytes 5242880 | tf_op jit(solution)/shard_map/pallas_call | solution.py:72
  41.9 1.3 %collective-permute-start.10 = (f32[4,384]{1,0:T(4,128)S(1)}, f32[4,384]{1,0:T(4,128)S(1)}, u32[]{:S(2)}, u32[]{:S(2)}) collective-permute-start(f32[4,384]{1,0:T(4,128)S(1)} %get-tuple-element.19), channel_id=1, source_target_pairs={{0,12},{1,13},{2,14},{3,15},{4,8},{5,9},{6,10},{7,11},{8,0},{9,1},... | collective-permute-start | bytes 18440 | tf_op jit(solution)/shard_map/ppermute | solution.py:384
  43.1 1.7 %collective-permute-start.8 = (f32[4,384]{1,0:T(4,128)S(1)}, f32[4,384]{1,0:T(4,128)S(1)}, u32[]{:S(2)}, u32[]{:S(2)}) collective-permute-start(f32[4,384]{1,0:T(4,128)S(1)} %get-tuple-element.19), channel_id=1, source_target_pairs={{0,8},{1,9},{2,10},{3,11},{4,12},{5,13},{6,14},{7,15},{8,4},{9,5},... | collective-permute-start | bytes 18440 | tf_op jit(solution)/shard_map/ppermute | solution.py:384
  45.3 3.3 %shard_map.67.after.own_classes = f32[11,512]{1,0:T(8,128)S(1)} custom-call(f32[4,1152]{1,0:T(4,128)S(1)} %get-tuple-element.16.told, f32[1024,512]{1,0:T(8,128)S(1)} %get-tuple-element.17.raw), custom_call_target="tpu_custom_call" | custom-call | tf_op jit(solution)/shard_map/pallas_call | solution.py:140
  48.6 2.4 %shard_map.68.refs_4_ = f32[512,2048]{1,0:T(8,128)S(1)} custom-call(bf16[512,1024]{1,0:T(8,128)(2,1)S(1)} %collective-permute-done.11.moving, bf16[2048,1024]{1,0:T(8,128)(2,1)S(1)} %get-tuple-element.18.plane, f32[11,512]{1,0:T(8,128)S(1)} %shard_map.67.after.own_classes), custom_call_target="tpu_custom_call" | custom-call | flops 2147483648 | bytes 5242880 | tf_op jit(solution)/shard_map/pallas_call | solution.py:91
  51.0 1.0 %collective-permute-done.7.moving = bf16[512,1024]{1,0:T(8,128)(2,1)S(1)} collective-permute-done((bf16[512,1024]{1,0:T(8,128)(2,1)}, bf16[512,1024]{1,0:T(8,128)(2,1)S(1)}, u32[]{:S(2)}, u32[]{:S(2)}) %collective-permute-start.7) | collective-permute-done | bytes 1048608 | tf_op jit(solution)/shard_map/ppermute | solution.py:384
  52.3 3.9 %shard_map.69 = (f32[1,512]{1,0:T(1,128)S(1)}, f32[1,512]{1,0:T(1,128)S(1)}, f32[1,512]{1,0:T(1,128)S(1)}, f32[1,512]{1,0:T(1,128)S(1)}, f32[1,512]{1,0:T(1,128)S(1)}) custom-call(s32[16,1]{1,0:T(8,128)S(1)} %fusion.1.device, f32[4,1152]{1,0:T(4,128)S(1)} %get-tuple-element.16.told, f32[11,512]{1,0:T(8,128)S(1)} %shard_map.67.after.own_classes, ...), custom_call_target="tpu_custom_call" | custom-call | flops 2147483648 | bytes 5242880 | tf_op jit(solution)/shard_map/pallas_call | solution.py:274
  56.2 2.7 %collective-permute-start.12 = (f32[1,512]{1,0:T(1,128)S(1)}, f32[1,512]{1,0:T(1,128)S(1)}, u32[]{:S(2)}, u32[]{:S(2)}) collective-permute-start(f32[1,512]{1,0:T(1,128)S(1)} %get-tuple-element.21), channel_id=1, source_target_pairs={{0,12},{1,13},{2,14},{3,15},{4,8},{5,9},{6,10},{7,11},{8,0},{9,1},... | collective-permute-start | bytes 6152 | tf_op jit(solution)/shard_map/ppermute | solution.py:384
  59.2 1.3 %collective-permute-start.14 = (f32[1,512]{1,0:T(1,128)S(1)}, f32[1,512]{1,0:T(1,128)S(1)}, u32[]{:S(2)}, u32[]{:S(2)}) collective-permute-start(f32[1,512]{1,0:T(1,128)S(1)} %get-tuple-element.23), channel_id=1, source_target_pairs={{0,2},{1,3},{2,0},{3,1},{4,6},{5,7},{6,4},{7,5},{8,10},{9,11},{10,... | collective-permute-start | bytes 6152 | tf_op jit(solution)/shard_map/ppermute | solution.py:384
  60.8 1.1 %collective-permute-done.13 = f32[1,512]{1,0:T(1,128)S(1)} collective-permute-done((f32[1,512]{1,0:T(1,128)S(1)}, f32[1,512]{1,0:T(1,128)S(1)}, u32[]{:S(2)}, u32[]{:S(2)}) %collective-permute-start.13) | collective-permute-done | bytes 2080 | tf_op jit(solution)/shard_map/ppermute | solution.py:384
  62.0 0.8 %collective-permute-done.14 = f32[1,512]{1,0:T(1,128)S(1)} collective-permute-done((f32[1,512]{1,0:T(1,128)S(1)}, f32[1,512]{1,0:T(1,128)S(1)}, u32[]{:S(2)}, u32[]{:S(2)}) %collective-permute-start.14) | collective-permute-done | bytes 2080 | tf_op jit(solution)/shard_map/ppermute | solution.py:384
  (30 shorter events, 4.8 us)
Async XLA Ops:
  0.0 36.7 %collective-permute-start.3 = (bf16[512,1024]{1,0:T(8,128)(2,1)}, bf16[512,1024]{1,0:T(8,128)(2,1)}, u32[]{:S(2)}, u32[]{:S(2)}) collective-permute-start(bf16[512,1024]{1,0:T(8,128)(2,1)} %refs_0_.1), channel_id=1, source_target_pairs={{0,1},{1,0},{2,3},{3,2},{4,5},{5,4},{6,7},{7,6},{8,9},{9,8},{10,11... | collective-permute-start | bytes 3145736 | tf_op jit(solution)/shard_map/ppermute | solution.py:384
  0.5 48.2 %collective-permute-start.11 = (bf16[512,1024]{1,0:T(8,128)(2,1)}, bf16[512,1024]{1,0:T(8,128)(2,1)S(1)}, u32[]{:S(2)}, u32[]{:S(2)}) collective-permute-start(bf16[512,1024]{1,0:T(8,128)(2,1)} %refs_0_.1), channel_id=1, source_target_pairs={{0,4},{1,5},{2,6},{3,7},{4,0},{5,1},{6,2},{7,3},{8,12},{9,13},{10,... | collective-permute-start | bytes 3145736 | tf_op jit(solution)/shard_map/ppermute | solution.py:384
  3.0 49.0 %collective-permute-start.7 = (bf16[512,1024]{1,0:T(8,128)(2,1)}, bf16[512,1024]{1,0:T(8,128)(2,1)S(1)}, u32[]{:S(2)}, u32[]{:S(2)}) collective-permute-start(bf16[512,1024]{1,0:T(8,128)(2,1)} %refs_0_.1), channel_id=1, source_target_pairs={{0,8},{1,9},{2,10},{3,11},{4,12},{5,13},{6,14},{7,15},{8,4},{9,5},... | collective-permute-start | bytes 3145736 | tf_op jit(solution)/shard_map/ppermute | solution.py:384
  7.9 15.0 %collective-permute-start = (bf16[256,1024]{1,0:T(8,128)(2,1)}, bf16[256,1024]{1,0:T(8,128)(2,1)S(1)}, u32[]{:S(2)}, u32[]{:S(2)}) collective-permute-start(bf16[256,1024]{1,0:T(8,128)(2,1)} %get-tuple-element.26), channel_id=1, source_target_pairs={{0,2},{1,3},{2,0},{3,1},{4,6},{5,7},{6,4},{7,5},{8,10},{9,11},{10,... | collective-permute-start | bytes 1572872 | tf_op jit(solution)/shard_map/ppermute | solution.py:384
  9.4 23.7 %collective-permute-start.4 = (bf16[256,1024]{1,0:T(8,128)(2,1)}, bf16[256,1024]{1,0:T(8,128)(2,1)S(1)}, u32[]{:S(2)}, u32[]{:S(2)}) collective-permute-start(bf16[256,1024]{1,0:T(8,128)(2,1)} %get-tuple-element.25), channel_id=1, source_target_pairs={{0,2},{1,3},{2,0},{3,1},{4,6},{5,7},{6,4},{7,5},{8,10},{9,11},{10,... | collective-permute-start | bytes 1572872 | tf_op jit(solution)/shard_map/ppermute | solution.py:384
  22.9 10.2 %collective-permute-start.1 = (f32[1,1152]{1,0:T(1,128)S(1)}, f32[1,1152]{1,0:T(1,128)S(1)}, u32[]{:S(2)}, u32[]{:S(2)}) collective-permute-start(f32[1,1152]{1,0:T(1,128)S(1)} %shard_map.64.refs_0_), channel_id=1, source_target_pairs={{0,1},{1,0},{2,3},{3,2},{4,5},{5,4},{6,7},{7,6},{8,9},{9,8},{10,11... | collective-permute-start | bytes 13832 | tf_op jit(solution)/shard_map/ppermute | solution.py:384
  33.1 2.0 %collective-permute-start.5 = (bf16[256,1024]{1,0:T(8,128)(2,1)S(1)}, bf16[256,1024]{1,0:T(8,128)(2,1)}, u32[]{:S(2)}, u32[]{:S(2)}) collective-permute-start(bf16[256,1024]{1,0:T(8,128)(2,1)S(1)} %collective-permute-done.after.refs_2_), channel_id=1, source_target_pairs={{0,1},{1,0},{2,3},{3,2},{4,5},{5,4},{6,7},{7,6},{8,9},{9,8},{10,11... | collective-permute-start | bytes 1572872 | tf_op jit(solution)/shard_map/ppermute | solution.py:384
  33.1 3.6 %collective-permute-start.6 = (bf16[256,1024]{1,0:T(8,128)(2,1)S(1)}, bf16[256,1024]{1,0:T(8,128)(2,1)}, u32[]{:S(2)}, u32[]{:S(2)}) collective-permute-start(bf16[256,1024]{1,0:T(8,128)(2,1)S(1)} %collective-permute-done.4.refs_3_), channel_id=1, source_target_pairs={{0,1},{1,0},{2,3},{3,2},{4,5},{5,4},{6,7},{7,6},{8,9},{9,8},{10,11... | collective-permute-start | bytes 1572872 | tf_op jit(solution)/shard_map/ppermute | solution.py:384
  35.1 6.7 %collective-permute-start.2 = (f32[2,1152]{1,0:T(2,128)S(1)}, f32[2,1152]{1,0:T(2,128)S(1)}, u32[]{:S(2)}, u32[]{:S(2)}) collective-permute-start(f32[2,1152]{1,0:T(2,128)S(1)} %pad_maximum_fusion), channel_id=1, source_target_pairs={{0,2},{1,3},{2,0},{3,1},{4,6},{5,7},{6,4},{7,5},{8,10},{9,11},{10,... | collective-permute-start | bytes 27656 | tf_op jit(solution)/shard_map/ppermute | solution.py:384
  36.7 1.2 %copy-start = (bf16[512,1024]{1,0:T(8,128)(2,1)S(1)}, bf16[512,1024]{1,0:T(8,128)(2,1)}, u32[]{:S(2)}) copy-start(bf16[512,1024]{1,0:T(8,128)(2,1)} %refs_0_.1) | copy-start | bytes 3145732
  41.9 10.4 %collective-permute-start.10 = (f32[4,384]{1,0:T(4,128)S(1)}, f32[4,384]{1,0:T(4,128)S(1)}, u32[]{:S(2)}, u32[]{:S(2)}) collective-permute-start(f32[4,384]{1,0:T(4,128)S(1)} %get-tuple-element.19), channel_id=1, source_target_pairs={{0,12},{1,13},{2,14},{3,15},{4,8},{5,9},{6,10},{7,11},{8,0},{9,1},... | collective-permute-start | bytes 18440 | tf_op jit(solution)/shard_map/ppermute | solution.py:384
  43.1 9.1 %collective-permute-start.8 = (f32[4,384]{1,0:T(4,128)S(1)}, f32[4,384]{1,0:T(4,128)S(1)}, u32[]{:S(2)}, u32[]{:S(2)}) collective-permute-start(f32[4,384]{1,0:T(4,128)S(1)} %get-tuple-element.19), channel_id=1, source_target_pairs={{0,8},{1,9},{2,10},{3,11},{4,12},{5,13},{6,14},{7,15},{8,4},{9,5},... | collective-permute-start | bytes 18440 | tf_op jit(solution)/shard_map/ppermute | solution.py:384
  44.8 7.4 %collective-permute-start.9 = (f32[4,384]{1,0:T(4,128)S(1)}, f32[4,384]{1,0:T(4,128)S(1)}, u32[]{:S(2)}, u32[]{:S(2)}) collective-permute-start(f32[4,384]{1,0:T(4,128)S(1)} %get-tuple-element.19), channel_id=1, source_target_pairs={{0,4},{1,5},{2,6},{3,7},{4,0},{5,1},{6,2},{7,3},{8,12},{9,13},{10,... | collective-permute-start | bytes 18440 | tf_op jit(solution)/shard_map/ppermute | solution.py:384
  56.2 4.6 %collective-permute-start.12 = (f32[1,512]{1,0:T(1,128)S(1)}, f32[1,512]{1,0:T(1,128)S(1)}, u32[]{:S(2)}, u32[]{:S(2)}) collective-permute-start(f32[1,512]{1,0:T(1,128)S(1)} %get-tuple-element.21), channel_id=1, source_target_pairs={{0,12},{1,13},{2,14},{3,15},{4,8},{5,9},{6,10},{7,11},{8,0},{9,1},... | collective-permute-start | bytes 6152 | tf_op jit(solution)/shard_map/ppermute | solution.py:384
  59.0 3.0 %collective-permute-start.13 = (f32[1,512]{1,0:T(1,128)S(1)}, f32[1,512]{1,0:T(1,128)S(1)}, u32[]{:S(2)}, u32[]{:S(2)}) collective-permute-start(f32[1,512]{1,0:T(1,128)S(1)} %get-tuple-element.22), channel_id=1, source_target_pairs={{0,3},{1,2},{2,1},{3,0},{4,7},{5,6},{6,5},{7,4},{8,11},{9,10},{10,... | collective-permute-start | bytes 6152 | tf_op jit(solution)/shard_map/ppermute | solution.py:384
  59.2 3.6 %collective-permute-start.14 = (f32[1,512]{1,0:T(1,128)S(1)}, f32[1,512]{1,0:T(1,128)S(1)}, u32[]{:S(2)}, u32[]{:S(2)}) collective-permute-start(f32[1,512]{1,0:T(1,128)S(1)} %get-tuple-element.23), channel_id=1, source_target_pairs={{0,2},{1,3},{2,0},{3,1},{4,6},{5,7},{6,4},{7,5},{8,10},{9,11},{10,... | collective-permute-start | bytes 6152 | tf_op jit(solution)/shard_map/ppermute | solution.py:384
  60.5 2.3 %collective-permute-start.15 = (f32[1,512]{1,0:T(1,128)S(1)}, f32[1,512]{1,0:T(1,128)S(1)}, u32[]{:S(2)}, u32[]{:S(2)}) collective-permute-start(f32[1,512]{1,0:T(1,128)S(1)} %get-tuple-element.24), channel_id=1, source_target_pairs={{0,1},{1,0},{2,3},{3,2},{4,5},{5,4},{6,7},{7,6},{8,9},{9,8},{10,11... | collective-permute-start | bytes 6152 | tf_op jit(solution)/shard_map/ppermute | solution.py:384
